TPU v7x, 256 devices: a whole 4x4x8 slice. The times are simulated.
256 devices in a mesh: shot: 32 (over z_hi, y, x), slab: 8 (over z_lo, core).
Axes of the slice: x: 4, y: 4, z: 8 (z_hi: 2, z_lo: 4; z = z_hi * 4 + z_lo), core: 2. Of those that a mesh axis runs over, the one named last changes fastest.
Arguments:
- waves: float32 [32, 2, 5, 64, 4096], P('shot', None, None, 'slab'), may hold values from -6 to 6
- traces: float32 [32, 16, 1024], P('shot', None, 'slab'), may hold values from -6 to 6
- rec_tile: int32 [32, 1024, 1], P('shot', 'slab'), may hold values from 0 to 7; in each aligned block of 128 rows (0 to 127, 128 to 255, ..., all dimensions but the last counted through in order) at most 48 rows name the same one
- rec_col: int32 [32, 1024], P('shot', 'slab'), may hold values from 0 to 7
- offsets: int32 [32], replicated, may hold values from 0 to 7
- directory: int32 [8], replicated, may hold values from 0 to 7, each once
- model_store: bfloat16 [7, 8, 64, 4096], P(None, None, 'slab', 'shot'), as said below
Outputs:
- waves_out: float32 [32, 2, 5, 64, 4096], P('shot', None, None, 'slab')
- image_stack: float32 [8, 64, 4096], P(None, 'slab', 'shot')
Inputs may be any that keep to these rules, and one draw needn't show every extreme that they name: `rec_tile`: within the receivers of one shot held by one slab index (aligned blocks of 128), at most 48 lie in the same slab. directory is a permutation. `model_store`: in every cell the first six entries form a positive-definite stiffness of a tilted transversely isotropic medium and the seventh, the buoyancy, is positive.
All inputs are finite; a program needn't handle non-finite values.
Results may differ from a plain program's by a relative error of at most 0.00045.
Values may be sent and summed in bfloat16 or wider, within the bound.
No kernel may reach another device: no remote copies, remote signals or barrier semaphores. Data moves between devices by JAX's collectives and lax.ppermute only.
A program may use at most 128 MiB of HBM per device.

v0:
```python
import jax
import jax.numpy as jnp
from jax import lax
from jax.sharding import PartitionSpec as P

STEPS = 16
PML = 16
REC_DEPTH = 24


damping_peak = 0.2


def from_behind(block, axis, distance):
    devices = range(lax.axis_size(axis))
    route = [(i - distance, i) for i in devices if i - distance in devices]
    return lax.ppermute(block, axis, route)


def z_below(array):
    return jnp.concatenate([jnp.zeros_like(array[..., :1]), array[..., :-1]], axis=-1)


def z_above(array):
    return jnp.concatenate([array[..., 1:], jnp.zeros_like(array[..., :1])], axis=-1)


def damping(x_index, total_x, depth_count):
    z_index = jnp.arange(depth_count, dtype=jnp.int32)
    wide_x = (
        jnp.maximum(jnp.maximum(PML - x_index, x_index - (total_x - 1 - PML)), 0).astype(
            jnp.float32
        )
        / PML
    )
    wide_z = (
        jnp.maximum(jnp.maximum(PML - z_index, z_index - (depth_count - 1 - PML)), 0).astype(
            jnp.float32
        )
        / PML
    )
    return 1.0 - damping_peak * (
        wide_x[:, None] * wide_x[:, None] + wide_z[None, :] * wide_z[None, :]
    )


def velocity_update(waves, coefs, signs, stress_left, inject_row):
    stress = waves[:, 2:5]
    extended = jnp.concatenate([stress_left, stress], axis=2)
    here = extended[:, :, 1:]
    left = extended[:, :, :-1]
    here_z = z_below(here)
    left_z = z_below(left)
    grad_x = 0.5 * (here + here_z - (left + left_z))
    grad_z = 0.5 * (here + left - (here_z + left_z))
    buoyant = signs * coefs[6]
    vel_x = waves[:, 0] + buoyant * (grad_x[:, 0] + grad_z[:, 2])
    vel_z = waves[:, 1] + buoyant * (grad_x[:, 2] + grad_z[:, 1])
    vel_z = vel_z.at[1, :, REC_DEPTH].add(inject_row)
    return jnp.concatenate([jnp.stack([vel_x, vel_z], axis=1), stress], axis=1)


def stress_update(waves, coefs, signs, vel_right, profile):
    velocity = waves[:, 0:2]
    extended = jnp.concatenate([velocity, vel_right], axis=2)
    here = extended[:, :, :-1]
    right = extended[:, :, 1:]
    here_z = z_above(here)
    right_z = z_above(right)
    grad_x = 0.5 * (right + right_z - (here + here_z))
    grad_z = 0.5 * (here_z + right_z - (here + right))
    strain_xx = grad_x[:, 0]
    strain_zz = grad_z[:, 1]
    strain_xz = grad_z[:, 0] + grad_x[:, 1]
    stress_xx = waves[:, 2] + signs * (
        coefs[0] * strain_xx + coefs[1] * strain_zz + coefs[2] * strain_xz
    )
    stress_zz = waves[:, 3] + signs * (
        coefs[1] * strain_xx + coefs[3] * strain_zz + coefs[4] * strain_xz
    )
    stress_xz = waves[:, 4] + signs * (
        coefs[2] * strain_xx + coefs[4] * strain_zz + coefs[5] * strain_xz
    )
    updated = (
        jnp.stack([velocity[:, 0], velocity[:, 1], stress_xx, stress_zz, stress_xz], axis=1)
        * profile
    )
    pressure = updated[:, 2] + updated[:, 3]
    return (updated, pressure[0] * pressure[1] * (1.0 / STEPS))


def local(waves, traces, rec_tile, rec_col, offsets, directory, model_store):
    slab_count = lax.axis_size("slab")
    my_shot = lax.axis_index("shot")
    my_slab = lax.axis_index("slab")
    fields = waves[0]
    width = fields.shape[2]
    depth_count = fields.shape[3]
    block_count = model_store.shape[1]
    slot = directory[offsets[my_shot]]
    whole = lax.all_gather(model_store, "shot", axis=3, tiled=True)
    coefs_low = lax.dynamic_index_in_dim(whole, slot, 1, keepdims=False)
    rec_count = traces.shape[2]
    capacity = min(rec_count, 3 * rec_count // slab_count)
    target = rec_tile[0, :, 0]
    onehot_target = (target[:, None] == jnp.arange(slab_count, dtype=jnp.int32)[None, :]).astype(
        jnp.int32
    )
    rank = jnp.sum((jnp.cumsum(onehot_target, axis=0) - 1) * onehot_target, axis=1)
    slot_index = target * capacity + rank
    placed = slot_index[:, None] == jnp.arange(slab_count * capacity, dtype=jnp.int32)[None, :]
    values = jnp.dot(traces[0], placed.astype(jnp.float32), precision=lax.Precision.HIGHEST)
    columns = (jnp.sum(jnp.where(placed, (rec_col[0] + 1)[:, None], 0), axis=0) - 1)[None, :]
    values_in, columns_in = (
        lax.all_to_all(values, "slab", split_axis=1, concat_axis=1, tiled=True),
        lax.all_to_all(columns, "slab", split_axis=1, concat_axis=1, tiled=True),
    )
    landing = (columns_in[0][:, None] == jnp.arange(width, dtype=jnp.int32)[None, :]).astype(
        jnp.float32
    )
    inject = jnp.dot(values_in, landing, precision=lax.Precision.HIGHEST)
    total_x = width * slab_count
    signs = jnp.array([-1.0, 1.0], dtype=jnp.float32).reshape(2, 1, 1)
    start = (fields, jnp.zeros((width, depth_count), jnp.float32))
    coefs = coefs_low.astype(jnp.float32)
    x_index = my_slab * width + jnp.arange(width, dtype=jnp.int32)
    profile = damping(x_index, total_x, depth_count)

    def turn(step, carry):
        state, image = carry
        row = lax.dynamic_index_in_dim(inject, step, 0, keepdims=False)
        stress_left = from_behind(state[:, 2:5, -1:, :], "slab", 1)
        state = velocity_update(state, coefs, signs, stress_left, row)
        vel_right = from_behind(state[:, 0:2, :1, :], "slab", -1)
        state, term = stress_update(state, coefs, signs, vel_right, profile)
        return (state, image + term)

    fields, image = lax.fori_loop(0, STEPS, turn, start)
    marker = (jnp.arange(block_count, dtype=jnp.int32) == offsets[my_shot]).astype(jnp.float32)
    spread = marker[:, None, None] * image[None]
    stacked = lax.psum_scatter(spread, "shot", scatter_dimension=2, tiled=True)
    return (fields[None], stacked)


def solution(mesh):
    placed = (
        P("shot", None, None, "slab", None),
        P("shot", None, "slab"),
        P("shot", "slab", None),
        P("shot", "slab"),
        P(),
        P(),
        P(None, None, "slab", "shot"),
    )
    return jax.shard_map(
        local,
        mesh=mesh,
        in_specs=placed,
        out_specs=(P("shot", None, None, "slab", None), P(None, "slab", "shot")),
        check_vma=False,
    )
```

profile of v0, /device:TPU:32, one launch (start us, length us, event | category | flops | bytes accessed | tf_op | source)
XLA Modules:
  0.0 748.6 jit_solution(11531669338068694933)
XLA Ops:
  10.1 6.0 all-to-all-start.1
  17.8 2.4 all-to-all-done.1
  20.2 4.7 all-to-all-start
  33.8 104.9 %all-gather.2.cloned.1.call-done = bf16[7,8,8,4096]{3,2,0,1:T(8,128)(2,1)} async-done(((bf16[7,8,8,128]{3,2,0,1:T(8,128)(2,1)}), bf16[7,8,8,4096]{3,2,0,1:T(8,128)(2,1)}) %all-gather.2.cloned.1.call-update) | async-done | bytes 3670032 | tf_op jit(solution)/shard_map/all_gather | solution.py:101
  140.8 375.6 %while.21 = (s32[]{:T(128)}, f32[2,5,8,4096]{3,2,1,0:T(8,128)S(1)}, f32[8,4096]{1,0:T(8,128)}, f32[7,8,4096]{2,1,0:T(8,128)}, f32[16,8]{1,0:T(8,128)S(1)}, /*ind...) while((s32[]{:T(128)}, f32[2,5,8,4096]{3,2,1,0:T(8,128)S(1)}, ...), condition=%wide.region_4.5_spmd.clone.clone.clone, body=%wide.region_3.4_spmd.clone.clone.clone.sunk | while | flops 7028738 | bytes 40554692 | solution.py:138
  153.7 3.2 collective-permute-start.1
  165.3 2.0 collective-permute-start
  177.2 3.2 collective-permute-start.1
  188.7 2.0 collective-permute-start
  200.7 3.2 collective-permute-start.1
  212.2 2.0 collective-permute-start
  224.1 3.2 collective-permute-start.1
  235.7 2.0 collective-permute-start
  247.6 3.2 collective-permute-start.1
  259.2 2.0 collective-permute-start
  271.1 3.2 collective-permute-start.1
  294.6 3.2 collective-permute-start.1
  306.1 2.0 collective-permute-start
  318.1 3.2 collective-permute-start.1
  341.5 3.2 collective-permute-start.1
  353.1 2.0 collective-permute-start
  365.0 3.2 collective-permute-start.1
  388.5 3.2 collective-permute-start.1
  412.0 3.2 collective-permute-start.1
  423.5 2.0 collective-permute-start
  435.5 3.2 collective-permute-start.1
  458.9 3.2 collective-permute-start.1
  482.4 3.2 collective-permute-start.1
  494.0 2.0 collective-permute-start
  505.9 3.2 collective-permute-start.1
  516.4 2.2 broadcast_multiply_fusion.1
  518.6 223.2 %reduce-scatter.2.cloned.1.call-done = f32[8,8,128]{2,1,0:T(8,128)} async-done(((f32[8,8,4096]{2,1,0:T(8,128)}), f32[8,8,128]{2,1,0:T(8,128)}) %reduce-scatter.2.cloned.1.call-update) | async-done | bytes 32784 | tf_op jit(solution)/shard_map/reduce_scatter | solution.py:141
  (1051 shorter events, 313.7 us)
Async XLA Ops:
  7.2 131.5 %all-gather.2.cloned.1.call-start = ((), (), s32[]{:S(2)}) async-start(), calls=%async_computation.3 | async-start | bytes 3784704 | tf_op jit(solution)/shard_map/all_gather | solution.py:101
  10.1 10.1 %all-to-all-start.1 = ((s32[1,8,48]{2,0,1:T(1,128)}), s32[1,8,48]{2,0,1:T(1,128)S(1)}, u32[]{:S(2)}, u32[]{:S(2)}) async-start(s32[1,8,48]{2,0,1:T(1,128)} %sub.82), calls=%async_computation.1 | async-start | bytes 8192 | tf_op jit(solution)/shard_map/all_to_all | solution.py:116
  20.2 11.9 %all-to-all-start = ((f32[8,1,768]{2,1,0:T(1,128)}), f32[8,1,768]{2,1,0:T(1,128)S(1)}, u32[]{:S(2)}, u32[]{:S(2)}) async-start(f32[8,1,768]{2,1,0:T(1,128)} %reshape.175), calls=%async_computation | async-start | bytes 49152 | tf_op jit(solution)/shard_map/all_to_all | solution.py:115
  24.9 716.9 %reduce-scatter.2.cloned.1.call-start = ((), (), s32[]{:S(2)}) async-start(), calls=%async_computation.4 | async-start | bytes 1081344 | tf_op jit(solution)/shard_map/reduce_scatter | solution.py:141
  141.8 6.0 collective-permute-start
  153.7 5.0 collective-permute-start.1
  165.3 6.1 collective-permute-start
  177.2 5.0 collective-permute-start.1
  188.7 6.1 collective-permute-start
  200.7 5.0 collective-permute-start.1
  212.2 6.1 collective-permute-start
  224.1 5.0 collective-permute-start.1
  235.7 6.1 collective-permute-start
  247.6 5.0 collective-permute-start.1
  259.2 6.1 collective-permute-start
  271.1 5.0 collective-permute-start.1
  282.7 6.1 collective-permute-start
  294.6 5.0 collective-permute-start.1
  306.1 6.1 collective-permute-start
  318.1 5.0 collective-permute-start.1
  329.6 6.1 collective-permute-start
  341.5 5.0 collective-permute-start.1
  353.1 6.1 collective-permute-start
  365.0 5.0 collective-permute-start.1
  376.6 6.1 collective-permute-start
  400.1 6.1 collective-permute-start
  412.0 5.0 collective-permute-start.1
  423.5 6.1 collective-permute-start
  435.5 5.0 collective-permute-start.1
  447.0 6.1 collective-permute-start
  470.5 6.1 collective-permute-start
  494.0 6.1 collective-permute-start
  (253 other events, 1116.0 us)
Sparse Core Ops, SparseCore 0:
  11.8 126.8 all-gather.1
  518.7 222.9 reduce-scatter.1
where the time goes:
time: 754 us; the launch traced here: 749 us
  waiting for transfers between devices  367 us (49%)
  local copies, waits for them, and re-layouts  137 us (18%)
  other arithmetic  128 us (17%)
  starting transfers between devices  93.8 us (12%)
  between operations  18.2 us (2%)
    reduce_scatter x1, waiting for transfers between devices, local(): stacked = lax.psum_scatter(spread, 'shot', scatter_dimension=2, tiled=True)  223 us
    all_gather x1, waiting for transfers between devices, local(): whole = lax.all_gather(model_store, 'shot', axis=3, tiled=True)  105 us
    ppermute x32, starting transfers between devices, from_behind(): return lax.ppermute(block, axis, route)  83.1 us
    while x512, local copies, waits for them, and re-layouts  60.1 us
    while x48, other arithmetic  42.4 us
    ppermute x32, waiting for transfers between devices, from_behind(): return lax.ppermute(block, axis, route)  36.5 us
    another operation x48, other arithmetic, velocity_update(): return jnp.concatenate([jnp.stack([vel_x, vel_z], axis=1), stress], axis=1)  35.5 us
    ppermute x32, local copies, waits for them, and re-layouts, from_behind(): return lax.ppermute(block, axis, route)  17 us
  transfers between devices with their start and end apart: 36, of which 35 were waited for; matrix products, arithmetic and copies ran while one was open for 8% of the time, Pallas kernels for 0%

commit v1 on v0

v1 whole, which is shorter than its diff:
```python
import functools

import jax
import jax.numpy as jnp
from jax import lax
from jax.experimental import pallas as pl
from jax.experimental.pallas import tpu as pltpu
from jax.sharding import PartitionSpec as P

STEPS = 16
PML = 16
REC_DEPTH = 24
damping_peak = 0.2

COLS = 8
TILES = 32
WIDE = 3 * COLS
PHASE = 8
ROWS = 32
VMEM_LIMIT = 56 * 1024 * 1024


def pick_kernel(offsets_ref, directory_ref, store_ref, out_ref):
    shots = out_ref.shape[0]

    def one(shot, _):
        slot = directory_ref[offsets_ref[shot]]
        for entry in range(7):
            out_ref[shot, entry] = store_ref[entry, slot]
        return 0

    lax.fori_loop(0, shots, one, 0)


def row_of(tile):
    return (tile % 4) * 8 + tile // 4


def iota8(axis):
    return lax.broadcasted_iota(jnp.int32, (8, 128), axis)


def lane_index():
    return lax.broadcasted_iota(jnp.int32, (ROWS, 128), 1)


def from_below(v, lane, sub):
    r = pltpu.roll(v, 1, 1)
    wrap = jnp.where(sub == 0, 0.0, pltpu.roll(r[24:32], 1, 0))
    return jnp.where(lane == 0, jnp.concatenate([wrap, r[0:24]], axis=0), r)


def from_above(v, lane, sub):
    r = pltpu.roll(v, 127, 1)
    wrap = jnp.where(sub == 7, 0.0, pltpu.roll(r[0:8], 7, 0))
    return jnp.where(lane == 127, jnp.concatenate([r[8:32], wrap], axis=0), r)


def advance(state, coef, image, inject_ref, first_step):
    lane = lane_index()
    sub = iota8(0)
    spot = jnp.where((iota8(0) == 0) & (iota8(1) == REC_DEPTH), 1.0, 0.0)

    def at(column):
        return pl.ds(pl.multiple_of(column * ROWS, ROWS), ROWS)

    def stress_at(w, i):
        return tuple(state[5 * w + q, at(i), :] for q in (2, 3, 4))

    def velocity(w, i, old, step):
        sxx, szz, sxz = here = stress_at(w, i)
        sxx_l, szz_l, sxz_l = old
        half_b = coef[6, at(i), :]
        d, s = sxx - sxx_l, sxz + sxz_l
        gx = half_b * (d + s + from_below(d - s, lane, sub))
        d, s = sxz - sxz_l, szz + szz_l
        gz = half_b * (d + s + from_below(d - s, lane, sub))
        vx = state[5 * w, at(i), :]
        vz = state[5 * w + 1, at(i), :]
        if w == 0:
            vx, vz = vx - gx, vz - gz
        else:
            vx, vz = vx + gx, vz + gz
            add = inject_ref[first_step + step - 1, i]
            vz = jnp.concatenate([vz[0:8] + add * spot, vz[8:32]], axis=0)
        damp = coef[7, at(i), :]
        state[5 * w, at(i), :] = vx * damp
        state[5 * w + 1, at(i), :] = vz * damp
        vx_z = from_above(vx, lane, sub)
        vz_z = from_above(vz, lane, sub)
        px, mx = vx + vx_z, vx_z - vx
        pz, mz = vz + vz_z, vz_z - vz
        return here, (px, mz, mx - pz), mx + pz

    def stress(w, i, old, left, here, g2):
        exx = here[0] - left[0]
        ezz = here[1] + left[1]
        gxz = left[2] + g2
        c = [coef[q, at(i), :] for q in range(6)]
        damp = coef[7, at(i), :]
        txx = c[0] * exx + c[1] * ezz + c[2] * gxz
        tzz = c[1] * exx + c[3] * ezz + c[4] * gxz
        txz = c[2] * exx + c[4] * ezz + c[5] * gxz
        sxx, szz, sxz = old
        if w == 0:
            new = (sxx - txx, szz - tzz, sxz - txz)
        else:
            new = (sxx + txx, szz + tzz, sxz + txz)
        new = tuple(v * damp for v in new)
        for q in range(3):
            state[5 * w + 2 + q, at(i), :] = new[q]
        return new[0] + new[1]

    def one_step(step, _):
        carry = []
        for w in range(2):
            here, left, _ = velocity(w, step, stress_at(w, step - 1), step)
            carry.append((here, left))

        def column(i, carry):
            after, pressure = [], []
            for w in range(2):
                old, left = carry[w]
                here, now, g2 = velocity(w, i, old, step)
                pressure.append(stress(w, i - 1, old, left, now, g2))
                after.append((here, now))
            image[at(i - 1), :] += pressure[0] * pressure[1]
            return tuple(after)

        lax.fori_loop(step + 1, WIDE - step + 1, column, tuple(carry))
        return 0

    lax.fori_loop(1, PHASE + 1, one_step, 0)


def first_kernel(
    slab_ref,
    inject_ref,
    left_ref,
    own_ref,
    right_ref,
    coef_left_ref,
    coef_own_ref,
    coef_right_ref,
    state_out,
    coef,
    image_out,
    state,
    image,
):
    for part, (waves, store) in enumerate(
        ((left_ref, coef_left_ref), (own_ref, coef_own_ref), (right_ref, coef_right_ref))
    ):
        base = part * COLS * ROWS
        for tile in range(TILES):
            rows = pl.ds(base + row_of(tile), COLS, stride=ROWS)
            lanes = pl.ds(tile * 128, 128)
            for q in range(10):
                state[q, rows, :] = waves[q, :, lanes]
            for q in range(7):
                coef[q, rows, :] = 0.5 * store[tile, q].astype(jnp.float32)

    row = lax.broadcasted_iota(jnp.int32, (ROWS, 128), 0)
    z = (row % 8) * 512 + (row // 8) * 128 + lane_index()
    depth = ROWS * 128
    wide_z = jnp.maximum(jnp.maximum(PML - z, z - (depth - 1 - PML)), 0).astype(jnp.float32) / PML
    square_z = wide_z * wide_z

    def profile(i, _):
        x = (slab_ref[0] - 1) * COLS + i
        total = slab_ref[1] * COLS
        wide_x = jnp.maximum(jnp.maximum(PML - x, x - (total - 1 - PML)), 0).astype(jnp.float32) * (1.0 / PML)
        coef[7, pl.ds(pl.multiple_of(i * ROWS, ROWS), ROWS), :] = 1.0 - damping_peak * (wide_x * wide_x + square_z)
        return 0

    lax.fori_loop(0, WIDE, profile, 0)
    image[...] = jnp.zeros_like(image)
    advance(state, coef, image, inject_ref, 0)
    mid = pl.ds(COLS * ROWS, COLS * ROWS)
    for q in range(10):
        state_out[q] = state[q, mid, :]
    image_out[...] = image[mid, :]


def second_kernel(
    inject_ref, left_ref, own_ref, right_ref, coef, image_in, waves_out, image_out, state, image
):
    size = COLS * ROWS
    for part, waves in enumerate((left_ref, own_ref, right_ref)):
        for q in range(10):
            state[q, pl.ds(part * size, size), :] = waves[q]
    image[...] = jnp.zeros_like(image)
    image[pl.ds(size, size), :] = image_in[...]
    advance(state, coef, image, inject_ref, PHASE)
    for tile in range(TILES):
        rows = pl.ds(size + row_of(tile), COLS, stride=ROWS)
        for q in range(10):
            waves_out[q, :, pl.ds(tile * 128, 128)] = state[q, rows, :]
        image_out[tile] = image[rows, :] * (1.0 / STEPS)


def stack_kernel(offsets_ref, pieces_ref, out_ref):
    out_ref[...] = jnp.zeros_like(out_ref)

    def one(shot, _):
        out_ref[offsets_ref[shot]] += pieces_ref[shot]
        return 0

    lax.fori_loop(0, pieces_ref.shape[0], one, 0)


VMEM = pl.BlockSpec(memory_space=pltpu.VMEM)
SMEM = pl.BlockSpec(memory_space=pltpu.SMEM)
PARAMS = pltpu.CompilerParams(vmem_limit_bytes=VMEM_LIMIT)


def shape(*dims, dtype=jnp.float32):
    return jax.ShapeDtypeStruct(dims, dtype)


def neighbours(block, axis):
    count = lax.axis_size(axis)
    up = [(i, i + 1) for i in range(count - 1)]
    down = [(i + 1, i) for i in range(count - 1)]
    return lax.ppermute(block, axis, up), lax.ppermute(block, axis, down)


def injection(traces, rec_tile, rec_col, slabs):
    cell = rec_tile[0, :, 0] * COLS + rec_col[0]
    window = jnp.arange(slabs, dtype=jnp.int32)[:, None] * COLS - COLS + jnp.arange(WIDE, dtype=jnp.int32)[None, :]
    place = (cell[:, None] == window.reshape(1, -1)).astype(jnp.float32)
    part = jnp.dot(traces[0], place, precision=lax.Precision.HIGHEST)
    part = part.reshape(STEPS, slabs, WIDE).transpose(1, 0, 2).reshape(slabs, STEPS * WIDE // 128, 128)
    part = lax.all_to_all(part, "slab", split_axis=0, concat_axis=0, tiled=True)
    return part.sum(axis=0).reshape(STEPS, WIDE)


def local(waves, traces, rec_tile, rec_col, offsets, directory, model_store):
    slabs = lax.axis_size("slab")
    shots = lax.axis_size("shot")
    depth = waves.shape[4]
    own = waves.reshape(10, COLS, depth)
    left, right = neighbours(own, "slab")

    picked = pl.pallas_call(
        pick_kernel,
        out_shape=shape(shots, 7, COLS, 128, dtype=jnp.bfloat16),
        in_specs=[SMEM, SMEM, VMEM],
        out_specs=VMEM,
        compiler_params=PARAMS,
    )(offsets, directory, model_store)
    coef_own = lax.all_to_all(picked, "shot", split_axis=0, concat_axis=0, tiled=True)
    coef_left, coef_right = neighbours(coef_own, "slab")
    inject = injection(traces, rec_tile, rec_col, slabs)

    place = jnp.stack([lax.axis_index("slab"), jnp.int32(slabs)]).astype(jnp.int32)
    own_rows = COLS * ROWS
    all_rows = WIDE * ROWS
    state, coef, image = pl.pallas_call(
        first_kernel,
        out_shape=(shape(10, own_rows, 128), shape(8, all_rows, 128), shape(own_rows, 128)),
        in_specs=[SMEM, SMEM] + [VMEM] * 6,
        out_specs=(VMEM,) * 3,
        scratch_shapes=[pltpu.VMEM((10, all_rows, 128), jnp.float32), pltpu.VMEM((all_rows, 128), jnp.float32)],
        compiler_params=PARAMS,
    )(place, inject, left, own, right, coef_left, coef_own, coef_right)
    state_left, state_right = neighbours(state, "slab")
    waves_out, pieces = pl.pallas_call(
        second_kernel,
        out_shape=(shape(10, COLS, depth), shape(TILES, COLS, 128)),
        in_specs=[SMEM] + [VMEM] * 5,
        out_specs=(VMEM,) * 2,
        scratch_shapes=[pltpu.VMEM((10, all_rows, 128), jnp.float32), pltpu.VMEM((all_rows, 128), jnp.float32)],
        compiler_params=PARAMS,
    )(inject, state_left, state, state_right, coef, image)
    pieces = lax.all_to_all(pieces, "shot", split_axis=0, concat_axis=0, tiled=True)
    stacked = pl.pallas_call(
        stack_kernel,
        out_shape=shape(model_store.shape[1], COLS, 128),
        in_specs=[SMEM, VMEM],
        out_specs=VMEM,
        compiler_params=PARAMS,
    )(offsets, pieces)
    return waves_out.reshape(waves.shape), stacked


def solution(mesh):
    placed = (
        P("shot", None, None, "slab", None),
        P("shot", None, "slab"),
        P("shot", "slab", None),
        P("shot", "slab"),
        P(),
        P(),
        P(None, None, "slab", "shot"),
    )
    return jax.shard_map(
        local,
        mesh=mesh,
        in_specs=placed,
        out_specs=(P("shot", None, None, "slab", None), P(None, "slab", "shot")),
        check_vma=False,
    )
```

time: 754 us -> 204 us (0.27)
  waiting for transfers between devices: 367 us -> 36.3 us
  local copies, waits for them, and re-layouts: 137 us -> 7.47 us
  other arithmetic: 128 us -> 2.13 us
  Pallas kernels: 0 us -> 108 us
  starting transfers between devices: 93.8 us -> 30.4 us
  blocking collectives: 0 us -> 17.7 us
  between operations: 18.2 us -> 0.78 us
    reduce_scatter x1 -> x0, waiting for transfers between devices: 223 us -> none  [local(): stacked = lax.psum_scatter(spread, 'shot', scatter_dimension=2, tiled=True)]
    pallas_call x0 -> x4, Pallas kernels: none -> 108 us  [the longest x1 54.8 us: local(): pl.pallas_call(first_kernel, out_shape=(shape(10, own_rows, 128), shape(8...]
    all_gather x1 -> x0, waiting for transfers between devices: 105 us -> none  [local(): whole = lax.all_gather(model_store, 'shot', axis=3, tiled=True)]
    ppermute x32 -> x6, starting transfers between devices: 83.1 us -> 13.3 us  [neighbours(): return (lax.ppermute(block, axis, up), lax.ppermute(block, axis, down))]
    while x512 -> x0, local copies, waits for them, and re-layouts: 60.1 us -> none
    another operation x65 -> x1, other arithmetic: 48.2 us -> 0.66 us  [local(): jnp.stack([lax.axis_index('slab'), jnp.int32(slabs)]).astype(jnp.int32)]
    while x48 -> x0, other arithmetic: 42.4 us -> none
    ppermute x32 -> x6, waiting for transfers between devices: 36.5 us -> 17.2 us  [neighbours(): return (lax.ppermute(block, axis, up), lax.ppermute(block, axis, down))]
  transfers between devices with their start and end apart: 36 -> 8, of which waited for: 35 -> 4; matrix products, arithmetic and copies ran while one was open for 8% -> 4% of each run, Pallas kernels for 0% -> 0%
where the time goes in v1:
time: 204 us; the launch traced here: 203 us
  Pallas kernels  108 us (53%)
  waiting for transfers between devices  36.3 us (18%)
  starting transfers between devices  30.4 us (15%)
  blocking collectives  17.7 us (9%)
  local copies, waits for them, and re-layouts  7.47 us (4%)
  other arithmetic  2.13 us (1%)
    pallas_call x1, Pallas kernels, local(): pl.pallas_call(first_kernel, out_shape=(shape(10, own_rows, 128), shape(8...  54.8 us
    pallas_call x1, Pallas kernels, local(): pl.pallas_call(second_kernel, out_shape=(shape(10, COLS, depth), shape(TI...  49 us
    all_to_all x1, blocking collectives, local(): lax.all_to_all(pieces, 'shot', split_axis=0, concat_axis=0, tiled=True)  17.7 us
    ppermute x6, waiting for transfers between devices, neighbours(): return (lax.ppermute(block, axis, up), lax.ppermute(block, axis, down))  17.2 us
    all_to_all x1, waiting for transfers between devices, local(): lax.all_to_all(picked, 'shot', split_axis=0, concat_axis=0, tiled=True)  15.4 us
    ppermute x6, starting transfers between devices, neighbours(): return (lax.ppermute(block, axis, up), lax.ppermute(block, axis, down))  13.3 us
    all_to_all x1, starting transfers between devices, local(): lax.all_to_all(picked, 'shot', split_axis=0, concat_axis=0, tiled=True)  13 us
    reshape x3, local copies, waits for them, and re-layouts, injection(): part.reshape(STEPS, slabs, WIDE).transpose(1, 0, 2)  4.44 us
  transfers between devices with their start and end apart: 8, of which 4 were waited for; matrix products, arithmetic and copies ran while one was open for 4% of the time, Pallas kernels for 0%

profile of v1, /device:TPU:32, one launch (start us, length us, event | category | flops | bytes accessed | tf_op | source)
XLA Modules:
  0.0 203.2 jit_solution(15541749526425093870)
XLA Ops:
  0.6 0.0 copy-start
  0.6 0.0 copy-start.2
  0.7 2.1 %shard_map.86 = bf16[32,7,8,128]{3,2,1,0:T(8,128)(2,1)} custom-call(s32[32]{0:T(128)} %offsets_ref.3, s32[8]{0:T(128)} %directory_ref.1, bf16[7,8,8,128]{3,2,1,0:T(8,128)(2,1)} %store_ref.1), custom_call_target="tpu_custom_call" | custom-call | tf_op jit(solution)/shard_map/pallas_call | solution.py:245
  2.8 13.0 %all-to-all-start.1 = ((bf16[32,7,8,128]{3,2,1,0:T(8,128)(2,1)}), bf16[32,7,8,128]{3,2,1,0:T(8,128)(2,1)S(1)}, u32[]{:S(2)}, u32[]{:S(2)}) async-start(bf16[32,7,8,128]{3,2,1,0:T(8,128)(2,1)} %shard_map.86), calls=%async_computation.1 | async-start | bytes 917504 | tf_op jit(solution)/shard_map/all_to_all | solution.py:252
  15.9 2.1 %collective-permute-start.1 = (f32[10,8,4096]{2,1,0:T(8,128)S(1)}, f32[10,8,4096]{2,1,0:T(8,128)S(1)}, u32[]{:S(2)}, u32[]{:S(2)}) collective-permute-start(f32[10,8,4096]{2,1,0:T(8,128)S(1)} %bitcast.16), channel_id=1, source_target_pairs={{1,0},{2,1},{3,2},{4,3},{5,4},{6,5},{7,6},{9,8},{10,9},{11,10},{12... | collective-permute-start | bytes 3932168 | tf_op jit(solution)/shard_map/ppermute | solution.py:225
  18.0 2.3 %collective-permute-start = (f32[10,8,4096]{2,1,0:T(8,128)S(1)}, f32[10,8,4096]{2,1,0:T(8,128)}, u32[]{:S(2)}, u32[]{:S(2)}) collective-permute-start(f32[10,8,4096]{2,1,0:T(8,128)S(1)} %bitcast.17), channel_id=1, source_target_pairs={{0,1},{1,2},{2,3},{3,4},{4,5},{5,6},{6,7},{8,9},{9,10},{10,11},{11... | collective-permute-start | bytes 3932168 | tf_op jit(solution)/shard_map/ppermute | solution.py:225
  20.2 0.1 iota_add_fusion
  20.3 0.1 add.37
  20.4 15.4 %all-to-all-done.1.coef_own_ref = bf16[32,7,8,128]{3,2,1,0:T(8,128)(2,1)S(1)} async-done(((bf16[32,7,8,128]{3,2,1,0:T(8,128)(2,1)}), bf16[32,7,8,128]{3,2,1,0:T(8,128)(2,1)S(1)}, u32[]{:S(2)}, u32[]{:S(2)}) %all-to-all-start.1) | async-done | bytes 458784 | tf_op jit(solution)/shard_map/all_to_all | solution.py:252
  35.8 1.9 collective-permute-start.3
  37.7 2.4 %collective-permute-start.2 = (bf16[32,7,8,128]{3,2,1,0:T(8,128)(2,1)S(1)}, bf16[32,7,8,128]{3,2,1,0:T(8,128)(2,1)}, u32[]{:S(2)}, u32[]{:S(2)}) collective-permute-start(bf16[32,7,8,128]{3,2,1,0:T(8,128)(2,1)S(1)} %all-to-all-done.1.coef_own_ref), channel_id=1, source_target_pairs={{0,1},{1,2},{2,3},{3,4},{4,5},{5,6},{6,7},{8,9},{9,10},{10,11},{11... | collective-permute-start | bytes 1376264 | tf_op jit(solution)/shard_map/ppermute | solution.py:225
  40.1 0.7 bitcast_add_fusion
  40.8 0.8 convolution_bitcast_fusion
  41.6 1.4 reshape.53
  43.0 1.5 copy.11
  44.5 1.5 reshape.54
  46.0 4.1 %all-to-all-start = ((f32[8,3,128]{2,1,0:T(4,128)}), f32[8,3,128]{2,1,0:T(4,128)}, u32[]{:S(2)}, u32[]{:S(2)}) async-start(f32[8,3,128]{2,1,0:T(4,128)} %reshape.54), calls=%async_computation | async-start | bytes 32768 | tf_op jit(solution)/shard_map/all_to_all | solution.py:234
  50.1 0.7 pad_add_fusion.slab_ref
  50.8 3.7 %all-to-all-done = f32[8,3,128]{2,1,0:T(4,128)} async-done(((f32[8,3,128]{2,1,0:T(4,128)}), f32[8,3,128]{2,1,0:T(4,128)}, u32[]{:S(2)}, u32[]{:S(2)}) %all-to-all-start) | async-done | bytes 12320 | tf_op jit(solution)/shard_map/all_to_all | solution.py:234
  54.4 0.7 reduce_sum.9
  55.2 0.7 reshape.55.inject_ref
  55.9 1.0 copy-done.3
  56.9 0.2 copy-done.6
  57.1 54.8 %shard_map.87 = (f32[10,256,128]{2,1,0:T(8,128)}, f32[8,768,128]{2,1,0:T(8,128)}, f32[256,128]{1,0:T(8,128)}) custom-call(s32[2]{0:T(128)} %pad_add_fusion.slab_ref, f32[16,24]{1,0:T(8,128)} %reshape.55.inject_ref, f32[10,8,4096]{2,1,0:T(8,128)} %collective-permute-done.left_ref, f32[10,8,4096]{2,1,0:T(8,128)} %bitcast.15, f32[10,8,4096]{2,1,0:T(8,128)} %copy-done.3, ...), custom_call_target="tpu_custom_call" | custom-call | tf_op jit(solution)/shard_map/pallas_call | solution.py:259
  111.9 2.7 %collective-permute-start.5 = (f32[10,256,128]{2,1,0:T(8,128)}, f32[10,256,128]{2,1,0:T(8,128)S(1)}, u32[]{:S(2)}, u32[]{:S(2)}) collective-permute-start(f32[10,256,128]{2,1,0:T(8,128)} %get-tuple-element.7.own_ref), channel_id=1, source_target_pairs={{1,0},{2,1},{3,2},{4,3},{5,4},{6,5},{7,6},{9,8},{10,9},{11,10},{12... | collective-permute-start | bytes 3932168 | tf_op jit(solution)/shard_map/ppermute | solution.py:225
  114.6 1.9 collective-permute-start.4
  116.6 13.5 %collective-permute-done.5.right_ref = f32[10,256,128]{2,1,0:T(8,128)S(1)} collective-permute-done((f32[10,256,128]{2,1,0:T(8,128)}, f32[10,256,128]{2,1,0:T(8,128)S(1)}, u32[]{:S(2)}, u32[]{:S(2)}) %collective-permute-start.5) | collective-permute-done | bytes 1310752 | tf_op jit(solution)/shard_map/ppermute | solution.py:225
  130.0 3.7 %collective-permute-done.4.left_ref = f32[10,256,128]{2,1,0:T(8,128)S(1)} collective-permute-done((f32[10,256,128]{2,1,0:T(8,128)}, f32[10,256,128]{2,1,0:T(8,128)S(1)}, u32[]{:S(2)}, u32[]{:S(2)}) %collective-permute-start.4) | collective-permute-done | bytes 1310752 | tf_op jit(solution)/shard_map/ppermute | solution.py:225
  133.8 1.1 copy-done.5
  134.8 49.0 %shard_map.88 = (f32[10,8,4096]{2,1,0:T(8,128)}, f32[32,8,128]{2,1,0:T(8,128)}) custom-call(f32[16,24]{1,0:T(8,128)} %reshape.55.inject_ref, f32[10,256,128]{2,1,0:T(8,128)} %copy-done.5, f32[10,256,128]{2,1,0:T(8,128)} %get-tuple-element.7.own_ref, f32[10,256,128]{2,1,0:T(8,128)} %copy-done.4, f32[8,768,128]{2,1,0:T(8,128)} %get-tuple-element.8.coef, ...), custom_call_target="tpu_custom_call" | custom-call | tf_op jit(solution)/shard_map/pallas_call | solution.py:268
  183.8 17.7 %all_to_all.15.pieces_ref = f32[32,8,128]{2,1,0:T(8,128)} all-to-all(f32[32,8,128]{2,1,0:T(8,128)} %get-tuple-element.11), channel_id=1, replica_groups=mesh['shot'=32,'slab'=8] {'shot'}, dimensions={0} | all-to-all | bytes 262144 | tf_op jit(solution)/shard_map/all_to_all | solution.py:276
  201.5 1.7 shard_map.89
  (16 shorter events, 0.0 us)
Async XLA Ops:
  0.6 40.1 %copy-start = (f32[1,16,128]{2,1,0:T(8,128)S(1)}, f32[1,16,128]{2,1,0:T(8,128)}, u32[]{:S(2)}) copy-start(f32[1,16,128]{2,1,0:T(8,128)} %param.8) | copy-start | bytes 24580
  0.6 15.2 %copy-start.2 = (f32[1,2,5,8,4096]{4,3,2,1,0:T(8,128)S(1)}, f32[1,2,5,8,4096]{4,3,2,1,0:T(8,128)}, u32[]{:S(2)}) copy-start(f32[1,2,5,8,4096]{4,3,2,1,0:T(8,128)} %param.7) | copy-start | bytes 3932164
  0.7 39.4 %copy-start.7 = (s32[1,128]{1,0:T(1,128)S(1)}, s32[1,128]{1,0:T(1,128)}, u32[]{:S(2)}) copy-start(s32[1,128]{1,0:T(1,128)} %param.10) | copy-start | bytes 1540
  2.8 32.9 %all-to-all-start.1 = ((bf16[32,7,8,128]{3,2,1,0:T(8,128)(2,1)}), bf16[32,7,8,128]{3,2,1,0:T(8,128)(2,1)S(1)}, u32[]{:S(2)}, u32[]{:S(2)}) async-start(bf16[32,7,8,128]{3,2,1,0:T(8,128)(2,1)} %shard_map.86), calls=%async_computation.1 | async-start | bytes 917504 | tf_op jit(solution)/shard_map/all_to_all | solution.py:252
  15.9 40.0 %collective-permute-start.1 = (f32[10,8,4096]{2,1,0:T(8,128)S(1)}, f32[10,8,4096]{2,1,0:T(8,128)S(1)}, u32[]{:S(2)}, u32[]{:S(2)}) collective-permute-start(f32[10,8,4096]{2,1,0:T(8,128)S(1)} %bitcast.16), channel_id=1, source_target_pairs={{1,0},{2,1},{3,2},{4,3},{5,4},{6,5},{7,6},{9,8},{10,9},{11,10},{12... | collective-permute-start | bytes 3932168 | tf_op jit(solution)/shard_map/ppermute | solution.py:225
  18.0 37.9 %collective-permute-start = (f32[10,8,4096]{2,1,0:T(8,128)S(1)}, f32[10,8,4096]{2,1,0:T(8,128)}, u32[]{:S(2)}, u32[]{:S(2)}) collective-permute-start(f32[10,8,4096]{2,1,0:T(8,128)S(1)} %bitcast.17), channel_id=1, source_target_pairs={{0,1},{1,2},{2,3},{3,4},{4,5},{5,6},{6,7},{8,9},{9,10},{10,11},{11... | collective-permute-start | bytes 3932168 | tf_op jit(solution)/shard_map/ppermute | solution.py:225
  35.8 20.2 %copy-start.1 = (bf16[32,7,8,128]{3,2,1,0:T(8,128)(2,1)}, bf16[32,7,8,128]{3,2,1,0:T(8,128)(2,1)S(1)}, u32[]{:S(2)}) copy-start(bf16[32,7,8,128]{3,2,1,0:T(8,128)(2,1)S(1)} %all-to-all-done.1.coef_own_ref) | copy-start | bytes 1376260
  35.8 20.1 %collective-permute-start.3 = (bf16[32,7,8,128]{3,2,1,0:T(8,128)(2,1)S(1)}, bf16[32,7,8,128]{3,2,1,0:T(8,128)(2,1)S(1)}, u32[]{:S(2)}, u32[]{:S(2)}) collective-permute-start(bf16[32,7,8,128]{3,2,1,0:T(8,128)(2,1)S(1)} %all-to-all-done.1.coef_own_ref), channel_id=1, source_target_pairs={{1,0},{2,1},{3,2},{4,3},{5,4},{6,5},{7,6},{9,8},{10,9},{11,10},{12... | collective-permute-start | bytes 1376264 | tf_op jit(solution)/shard_map/ppermute | solution.py:225
  37.7 18.2 %collective-permute-start.2 = (bf16[32,7,8,128]{3,2,1,0:T(8,128)(2,1)S(1)}, bf16[32,7,8,128]{3,2,1,0:T(8,128)(2,1)}, u32[]{:S(2)}, u32[]{:S(2)}) collective-permute-start(bf16[32,7,8,128]{3,2,1,0:T(8,128)(2,1)S(1)} %all-to-all-done.1.coef_own_ref), channel_id=1, source_target_pairs={{0,1},{1,2},{2,3},{3,4},{4,5},{5,6},{6,7},{8,9},{9,10},{10,11},{11... | collective-permute-start | bytes 1376264 | tf_op jit(solution)/shard_map/ppermute | solution.py:225
  46.0 8.4 %all-to-all-start = ((f32[8,3,128]{2,1,0:T(4,128)}), f32[8,3,128]{2,1,0:T(4,128)}, u32[]{:S(2)}, u32[]{:S(2)}) async-start(f32[8,3,128]{2,1,0:T(4,128)} %reshape.54), calls=%async_computation | async-start | bytes 32768 | tf_op jit(solution)/shard_map/all_to_all | solution.py:234
  55.9 1.1 copy-start.3
  55.9 1.2 copy-start.6
  111.9 18.1 %collective-permute-start.5 = (f32[10,256,128]{2,1,0:T(8,128)}, f32[10,256,128]{2,1,0:T(8,128)S(1)}, u32[]{:S(2)}, u32[]{:S(2)}) collective-permute-start(f32[10,256,128]{2,1,0:T(8,128)} %get-tuple-element.7.own_ref), channel_id=1, source_target_pairs={{1,0},{2,1},{3,2},{4,3},{5,4},{6,5},{7,6},{9,8},{10,9},{11,10},{12... | collective-permute-start | bytes 3932168 | tf_op jit(solution)/shard_map/ppermute | solution.py:225
  114.6 19.1 %collective-permute-start.4 = (f32[10,256,128]{2,1,0:T(8,128)}, f32[10,256,128]{2,1,0:T(8,128)S(1)}, u32[]{:S(2)}, u32[]{:S(2)}) collective-permute-start(f32[10,256,128]{2,1,0:T(8,128)} %get-tuple-element.7.own_ref), channel_id=1, source_target_pairs={{0,1},{1,2},{2,3},{3,4},{4,5},{5,6},{6,7},{8,9},{9,10},{10,11},{11... | collective-permute-start | bytes 3932168 | tf_op jit(solution)/shard_map/ppermute | solution.py:225
  130.0 3.7 %copy-start.4 = (f32[10,256,128]{2,1,0:T(8,128)}, f32[10,256,128]{2,1,0:T(8,128)S(1)}, u32[]{:S(2)}) copy-start(f32[10,256,128]{2,1,0:T(8,128)S(1)} %collective-permute-done.5.right_ref) | copy-start | bytes 3932164
  133.8 1.1 copy-start.5

commit v2 on v1

v2 whole, which is shorter than its diff:
```python
import functools

import jax
import jax.numpy as jnp
from jax import lax
from jax.experimental import pallas as pl
from jax.experimental.pallas import tpu as pltpu
from jax.sharding import PartitionSpec as P

STEPS = 16
PML = 16
REC_DEPTH = 24
damping_peak = 0.2

COLS = 8
TILES = 32
WIDE = 3 * COLS
PHASE = 8
PAD = 4
HELD = 36
GRADS, PARTS, PLANES = 10, 14, 22
ROWS = 32
VMEM_LIMIT = 40 * 1024 * 1024


def pick_kernel(offsets_ref, directory_ref, store_ref, out_ref):
    shots = out_ref.shape[0]

    def one(shot, _):
        slot = directory_ref[offsets_ref[shot]]
        for entry in range(7):
            out_ref[shot, entry] = store_ref[entry, slot]
        return 0

    lax.fori_loop(0, shots, one, 0)


def row_of(tile):
    return (tile % 4) * 8 + tile // 4


def iota8(axis):
    return lax.broadcasted_iota(jnp.int32, (8, 128), axis)


def lane_index():
    return lax.broadcasted_iota(jnp.int32, (ROWS, 128), 1)


def from_below(v, lane, sub):
    r = pltpu.roll(v, 1, 1)
    wrap = jnp.where(sub == 0, 0.0, pltpu.roll(r[24:32], 1, 0))
    return jnp.where(lane == 0, jnp.concatenate([wrap, r[0:24]], axis=0), r)


def from_above(v, lane, sub):
    r = pltpu.roll(v, 127, 1)
    wrap = jnp.where(sub == 7, 0.0, pltpu.roll(r[0:8], 7, 0))
    return jnp.where(lane == 127, jnp.concatenate([r[8:32], wrap], axis=0), r)


def advance(state, coef, image, inject_ref, first_step):
    lane = lane_index()
    sub = iota8(0)
    spot = jnp.where((iota8(0) == 0) & (iota8(1) == REC_DEPTH), 1.0, 0.0)

    def at(base, k):
        return pl.ds(pl.multiple_of(base + k * ROWS, ROWS), ROWS)

    def stress_at(w, base, k):
        return tuple(state[5 * w + q, at(base, k), :] for q in (2, 3, 4))

    def gradients(base, ks):
        for w in range(2):
            left = stress_at(w, base, ks[0] - 1)
            for k in ks:
                here = stress_at(w, base, k)
                d, s = here[0] - left[0], here[2] + left[2]
                state[GRADS + 2 * w, at(base, k), :] = d + s + from_below(d - s, lane, sub)
                d, s = here[2] - left[2], here[1] + left[1]
                state[GRADS + 2 * w + 1, at(base, k), :] = d + s + from_below(d - s, lane, sub)
                left = here

    def velocities(a, base, ks, step):
        for k in ks:
            half_b = coef[6, at(base, k), :]
            damp = coef[7, at(base, k), :]
            for w in range(2):
                gx = half_b * state[GRADS + 2 * w, at(base, k), :]
                gz = half_b * state[GRADS + 2 * w + 1, at(base, k), :]
                vx = state[5 * w, at(base, k), :]
                vz = state[5 * w + 1, at(base, k), :]
                if w == 0:
                    vx, vz = vx - gx, vz - gz
                else:
                    vx, vz = vx + gx, vz + gz
                    add = inject_ref[first_step + step - 1, a + k]
                    vz = jnp.concatenate([vz[0:8] + add * spot, vz[8:32]], axis=0)
                state[5 * w, at(base, k), :] = vx * damp
                state[5 * w + 1, at(base, k), :] = vz * damp
                vx_z = from_above(vx, lane, sub)
                vz_z = from_above(vz, lane, sub)
                mx, pz = vx_z - vx, vz + vz_z
                state[PARTS + 4 * w, at(base, k), :] = vx + vx_z
                state[PARTS + 4 * w + 1, at(base, k), :] = vz_z - vz
                state[PARTS + 4 * w + 2, at(base, k), :] = mx - pz
                state[PARTS + 4 * w + 3, at(base, k), :] = mx + pz

    def stresses(base, ks):
        for k in ks:
            c = [coef[q, at(base, k), :] for q in range(6)]
            damp = coef[7, at(base, k), :]
            pressure = []
            for w in range(2):
                exx = state[PARTS + 4 * w, at(base, k + 1), :] - state[PARTS + 4 * w, at(base, k), :]
                ezz = state[PARTS + 4 * w + 1, at(base, k + 1), :] + state[PARTS + 4 * w + 1, at(base, k), :]
                gxz = state[PARTS + 4 * w + 3, at(base, k + 1), :] + state[PARTS + 4 * w + 2, at(base, k), :]
                txx = c[0] * exx + c[1] * ezz + c[2] * gxz
                tzz = c[1] * exx + c[3] * ezz + c[4] * gxz
                txz = c[2] * exx + c[4] * ezz + c[5] * gxz
                sxx, szz, sxz = stress_at(w, base, k)
                if w == 0:
                    new = (sxx - txx, szz - tzz, sxz - txz)
                else:
                    new = (sxx + txx, szz + tzz, sxz + txz)
                new = tuple(v * damp for v in new)
                for q in range(3):
                    state[5 * w + 2 + q, at(base, k), :] = new[q]
                pressure.append(new[0] + new[1])
            image[at(base, k), :] += pressure[0] * pressure[1]

    def one_step(step, _):
        start = pl.multiple_of((step + PAD) * ROWS, ROWS)
        gradients(start, (0, 1))

        def turn(j, _):
            a = step + 2 * j
            base = pl.multiple_of((a + PAD) * ROWS, ROWS)
            velocities(a, base, (0, 1), step)
            gradients(base, (2, 3))
            stresses(base, (-3, -2))
            return 0

        lax.fori_loop(0, PHASE + 6 - step, turn, 0)
        return 0

    lax.fori_loop(1, PHASE + 1, one_step, 0)


def window(part):
    return pl.ds((PAD + part * COLS) * ROWS, COLS * ROWS)


def waves_kernel(left_ref, own_ref, right_ref, out_ref):
    for part, waves in enumerate((left_ref, own_ref, right_ref)):
        for tile in range(TILES):
            rows = pl.ds(part * COLS * ROWS + row_of(tile), COLS, stride=ROWS)
            for q in range(10):
                out_ref[q, rows, :] = waves[q, :, pl.ds(tile * 128, 128)]


def inject_kernel(traces_ref, tile_ref, col_ref, out_ref):
    cell = tile_ref[...] * COLS + col_ref[...]
    column = lax.broadcasted_iota(jnp.int32, (128, 128), 0)
    for slab in range(out_ref.shape[0]):
        hit = (cell == column + (slab - 1) * COLS) & (column < WIDE)
        out_ref[slab] = lax.dot_general(
            traces_ref[...],
            jnp.where(hit, 1.0, 0.0),
            (((1,), (1,)), ((), ())),
            precision=lax.Precision.HIGHEST,
            preferred_element_type=jnp.float32,
        )


def first_kernel(
    slabs,
    slab_ref,
    inject_ref,
    waves_ref,
    coef_left_ref,
    coef_own_ref,
    coef_right_ref,
    state_out,
    coef_out,
    image_out,
    state,
    coef,
    image,
    sem,
):
    all_rows = pl.ds(PAD * ROWS, WIDE * ROWS)
    copy = pltpu.make_async_copy(waves_ref, state.at[pl.ds(0, 10), all_rows, :], sem)
    copy.start()
    for part, store in enumerate((coef_left_ref, coef_own_ref, coef_right_ref)):
        base = (PAD + part * COLS) * ROWS
        for tile in range(TILES):
            rows = pl.ds(base + row_of(tile), COLS, stride=ROWS)
            for q in range(7):
                coef[q, rows, :] = 0.5 * store[tile, q].astype(jnp.float32)

    row = lax.broadcasted_iota(jnp.int32, (ROWS, 128), 0)
    z = (row % 8) * 512 + (row // 8) * 128 + lane_index()
    depth = ROWS * 128
    wide_z = jnp.maximum(jnp.maximum(PML - z, z - (depth - 1 - PML)), 0).astype(jnp.float32) / PML
    square_z = wide_z * wide_z
    first = (slab_ref[0] - 1) * COLS

    def profile(i, _):
        x = first + i
        last = slabs * COLS - 1 - PML
        wide_x = jnp.maximum(jnp.maximum(PML - x, x - last), 0).astype(jnp.float32) * (1.0 / PML)
        rows = pl.ds(pl.multiple_of((i + PAD) * ROWS, ROWS), ROWS)
        coef[7, rows, :] = 1.0 - damping_peak * (wide_x * wide_x + square_z)
        return 0

    lax.fori_loop(0, WIDE, profile, 0)
    image[...] = jnp.zeros_like(image)
    copy.wait()
    advance(state, coef, image, inject_ref, 0)
    for q in range(10):
        state_out[q] = state[q, window(1), :]
    for q in range(8):
        coef_out[q] = coef[q, all_rows, :]
    image_out[...] = image[window(1), :]


def second_kernel(
    inject_ref,
    left_ref,
    own_ref,
    right_ref,
    coef_ref,
    image_in,
    waves_out,
    image_out,
    state,
    coef,
    image,
    sems,
):
    copies = [
        pltpu.make_async_copy(ref, state.at[pl.ds(0, 10), window(part), :], sems.at[part])
        for part, ref in enumerate((left_ref, own_ref, right_ref))
    ]
    copies.append(pltpu.make_async_copy(coef_ref, coef.at[:, pl.ds(PAD * ROWS, WIDE * ROWS), :], sems.at[3]))
    for copy in copies:
        copy.start()
    image[...] = jnp.zeros_like(image)
    image[window(1), :] = image_in[...]
    for copy in copies:
        copy.wait()
    advance(state, coef, image, inject_ref, PHASE)
    for tile in range(TILES):
        rows = pl.ds((PAD + COLS) * ROWS + row_of(tile), COLS, stride=ROWS)
        for q in range(10):
            waves_out[q, :, pl.ds(tile * 128, 128)] = state[q, rows, :]
        image_out[tile] = image[rows, :] * (1.0 / STEPS)


def stack_kernel(offsets_ref, pieces_ref, out_ref):
    out_ref[...] = jnp.zeros_like(out_ref)

    def one(shot, _):
        out_ref[offsets_ref[shot]] += pieces_ref[shot]
        return 0

    lax.fori_loop(0, pieces_ref.shape[0], one, 0)


VMEM = pl.BlockSpec(memory_space=pltpu.VMEM)
ANY = pl.BlockSpec(memory_space=pl.ANY)
SMEM = pl.BlockSpec(memory_space=pltpu.SMEM)
PARAMS = pltpu.CompilerParams(vmem_limit_bytes=VMEM_LIMIT)


def shape(*dims, dtype=jnp.float32):
    return jax.ShapeDtypeStruct(dims, dtype)


def neighbours(block, axis):
    count = lax.axis_size(axis)
    up = [(i, i + 1) for i in range(count - 1)]
    down = [(i + 1, i) for i in range(count - 1)]
    return lax.ppermute(block, axis, up), lax.ppermute(block, axis, down)


def scratch(copies):
    held = HELD * ROWS
    return [
        pltpu.VMEM((PLANES, held, 128), jnp.float32),
        pltpu.VMEM((8, held, 128), jnp.float32),
        pltpu.VMEM((held, 128), jnp.float32),
        pltpu.SemaphoreType.DMA((copies,)) if copies > 1 else pltpu.SemaphoreType.DMA,
    ]


def local(waves, traces, rec_tile, rec_col, offsets, directory, model_store):
    slabs = lax.axis_size("slab")
    shots = lax.axis_size("shot")
    depth = waves.shape[4]
    own = waves.reshape(10, COLS, depth)
    own_rows = COLS * ROWS
    all_rows = WIDE * ROWS

    picked = pl.pallas_call(
        pick_kernel,
        out_shape=shape(shots, 7, COLS, 128, dtype=jnp.bfloat16),
        in_specs=[SMEM, SMEM, VMEM],
        out_specs=VMEM,
        compiler_params=PARAMS,
    )(offsets, directory, model_store)
    coef_own = lax.all_to_all(picked, "shot", split_axis=0, concat_axis=0, tiled=True)

    left, right = neighbours(own, "slab")
    adds = pl.pallas_call(
        inject_kernel,
        out_shape=shape(slabs, STEPS, 128),
        in_specs=[VMEM] * 3,
        out_specs=VMEM,
        compiler_params=PARAMS,
    )(traces[0], rec_tile.reshape(1, -1), rec_col)
    inject = lax.all_to_all(adds, "slab", split_axis=0, concat_axis=0, tiled=True).sum(axis=0)
    waves_in = pl.pallas_call(
        waves_kernel,
        out_shape=shape(10, all_rows, 128),
        in_specs=[VMEM] * 3,
        out_specs=VMEM,
        compiler_params=PARAMS,
        cost_estimate=pl.CostEstimate(flops=0, bytes_accessed=8 << 20, transcendentals=0),
    )(left, own, right)

    coef_own, inject = lax.optimization_barrier((coef_own, inject))
    coef_left, coef_right = neighbours(coef_own, "slab")
    state, coef, image = pl.pallas_call(
        functools.partial(first_kernel, slabs),
        out_shape=(shape(10, own_rows, 128), shape(8, all_rows, 128), shape(own_rows, 128)),
        in_specs=[SMEM, SMEM, ANY] + [VMEM] * 3,
        out_specs=(VMEM,) * 3,
        scratch_shapes=scratch(1),
        compiler_params=PARAMS,
    )(lax.axis_index("slab").astype(jnp.int32).reshape(1), inject, waves_in, coef_left, coef_own, coef_right)
    state_left, state_right = neighbours(state, "slab")
    waves_out, pieces = pl.pallas_call(
        second_kernel,
        out_shape=(shape(10, COLS, depth), shape(TILES, COLS, 128)),
        in_specs=[SMEM] + [ANY] * 4 + [VMEM],
        out_specs=(VMEM,) * 2,
        scratch_shapes=scratch(4),
        compiler_params=PARAMS,
    )(inject, state_left, state, state_right, coef, image)
    pieces = lax.all_to_all(pieces, "shot", split_axis=0, concat_axis=0, tiled=True)
    stacked = pl.pallas_call(
        stack_kernel,
        out_shape=shape(model_store.shape[1], COLS, 128),
        in_specs=[SMEM, VMEM],
        out_specs=VMEM,
        compiler_params=PARAMS,
    )(offsets, pieces)
    return waves_out.reshape(waves.shape), stacked


def solution(mesh):
    placed = (
        P("shot", None, None, "slab", None),
        P("shot", None, "slab"),
        P("shot", "slab", None),
        P("shot", "slab"),
        P(),
        P(),
        P(None, None, "slab", "shot"),
    )
    return jax.shard_map(
        local,
        mesh=mesh,
        in_specs=placed,
        out_specs=(P("shot", None, None, "slab", None), P(None, "slab", "shot")),
        check_vma=False,
    )
```

time: 204 us -> 143 us (0.70)
  Pallas kernels: 108 us -> 49 us
  blocking collectives: 17.7 us -> 23.6 us
  local copies, waits for them, and re-layouts: 7.47 us -> 4.32 us
  other arithmetic: 2.13 us -> 0.01 us
    pallas_call x1, Pallas kernels: 49 us -> 19.1 us  [local(): pl.pallas_call(second_kernel, out_shape=(shape(10, COLS, depth), shape(TI...]
    pallas_call x1 -> x3, Pallas kernels: 54.8 us -> 26.8 us  [the longest x1 20.7 us: local(): pl.pallas_call(functools.partial(first_kernel, slabs), out_shape=(shape(1...]
    all_to_all x1, blocking collectives: 17.7 us -> 23.6 us  [local(): lax.all_to_all(pieces, 'shot', split_axis=0, concat_axis=0, tiled=True)]
    reshape x4 -> x0, local copies, waits for them, and re-layouts: 5.13 us -> none  [the longest x3 4.44 us: injection(): part.reshape(STEPS, slabs, WIDE).transpose(1, 0, 2)]
    all_to_all x1, waiting for transfers between devices: 3.68 us -> 0.74 us  [local(): lax.all_to_all(adds, 'slab', split_axis=0, concat_axis=0, tiled=True)]
    unnamed x16, local copies, waits for them, and re-layouts: 2.26 us -> 4.32 us
  transfers between devices with their start and end apart: 8 -> 8, of which waited for: 4 -> 6; matrix products, arithmetic and copies ran while one was open for 4% -> 0% of each run, Pallas kernels for 0% -> 5%
where the time goes in v2:
time: 143 us
  Pallas kernels  49 us (34%)
  waiting for transfers between devices  34.9 us (24%)
  starting transfers between devices  30.3 us (21%)
  blocking collectives  23.6 us (17%)
  local copies, waits for them, and re-layouts  4.32 us (3%)
    all_to_all x1, blocking collectives, local(): lax.all_to_all(pieces, 'shot', split_axis=0, concat_axis=0, tiled=True)  23.6 us
    pallas_call x1, Pallas kernels, local(): pl.pallas_call(functools.partial(first_kernel, slabs), out_shape=(shape(1...  20.7 us
    pallas_call x1, Pallas kernels, local(): pl.pallas_call(second_kernel, out_shape=(shape(10, COLS, depth), shape(TI...  19.1 us
    ppermute x6, waiting for transfers between devices, neighbours(): return (lax.ppermute(block, axis, up), lax.ppermute(block, axis, down))  18.8 us
    all_to_all x1, waiting for transfers between devices, local(): lax.all_to_all(picked, 'shot', split_axis=0, concat_axis=0, tiled=True)  15.4 us
    ppermute x6, starting transfers between devices, neighbours(): return (lax.ppermute(block, axis, up), lax.ppermute(block, axis, down))  13 us
    all_to_all x1, starting transfers between devices, local(): lax.all_to_all(picked, 'shot', split_axis=0, concat_axis=0, tiled=True)  11.3 us
    all_to_all x1, starting transfers between devices, local(): lax.all_to_all(adds, 'slab', split_axis=0, concat_axis=0, tiled=True)  6.01 us
  transfers between devices with their start and end apart: 8, of which 6 were waited for; matrix products, arithmetic and copies ran while one was open for 0% of the time, Pallas kernels for 5%

profile of v2, /device:TPU:32, one launch (start us, length us, event | category | flops | bytes accessed | tf_op | source)
XLA Modules:
  0.0 142.9 jit_solution(7578096151368797813)
XLA Ops:
  0.6 0.0 copy-start
  0.6 0.0 copy-start.2
  0.7 0.8 copy-done.2
  1.4 0.7 copy-done.5
  2.1 0.7 copy-done.6
  2.8 0.9 shard_map.87
  3.7 6.0 %all-to-all-start.1 = ((f32[8,16,128]{2,1,0:T(8,128)}), f32[8,16,128]{2,1,0:T(8,128)S(1)}, u32[]{:S(2)}, u32[]{:S(2)}) async-start(f32[8,16,128]{2,1,0:T(8,128)} %shard_map.87), calls=%async_computation.1 | async-start | bytes 131072 | tf_op jit(solution)/shard_map/all_to_all | solution.py:323
  9.7 0.9 copy-done.1
  10.6 0.7 copy-done.3
  11.2 0.7 copy-done.7
  11.9 1.7 %shard_map.86 = bf16[32,7,8,128]{3,2,1,0:T(8,128)(2,1)} custom-call(s32[32]{0:T(128)S(1)} %copy-done.3, s32[8]{0:T(128)S(1)} %copy-done.7, bf16[7,8,8,128]{3,2,1,0:T(8,128)(2,1)S(1)} %copy-done.1), custom_call_target="tpu_custom_call" | custom-call | tf_op jit(solution)/shard_map/pallas_call | solution.py:306
  13.6 0.7 all-to-all-done.1
  14.3 11.3 %all-to-all-start = ((bf16[32,7,8,128]{3,2,1,0:T(8,128)(2,1)}), bf16[32,7,8,128]{3,2,1,0:T(8,128)(2,1)S(1)}, u32[]{:S(2)}, u32[]{:S(2)}) async-start(bf16[32,7,8,128]{3,2,1,0:T(8,128)(2,1)} %shard_map.86), calls=%async_computation | async-start | bytes 917504 | tf_op jit(solution)/shard_map/all_to_all | solution.py:313
  25.6 0.0 copy-done
  25.7 2.2 %collective-permute-start.1 = (f32[10,8,4096]{2,1,0:T(8,128)S(1)}, f32[10,8,4096]{2,1,0:T(8,128)S(1)}, u32[]{:S(2)}, u32[]{:S(2)}) collective-permute-start(f32[10,8,4096]{2,1,0:T(8,128)S(1)} %bitcast.5), channel_id=1, source_target_pairs={{1,0},{2,1},{3,2},{4,3},{5,4},{6,5},{7,6},{9,8},{10,9},{11,10},{12... | collective-permute-start | bytes 3932168 | tf_op jit(solution)/shard_map/ppermute | solution.py:285
  27.8 2.1 %collective-permute-start = (f32[10,8,4096]{2,1,0:T(8,128)S(1)}, f32[10,8,4096]{2,1,0:T(8,128)}, u32[]{:S(2)}, u32[]{:S(2)}) collective-permute-start(f32[10,8,4096]{2,1,0:T(8,128)S(1)} %bitcast.6), channel_id=1, source_target_pairs={{0,1},{1,2},{2,3},{3,4},{4,5},{5,6},{6,7},{8,9},{9,10},{10,11},{11... | collective-permute-start | bytes 3932168 | tf_op jit(solution)/shard_map/ppermute | solution.py:285
  30.0 15.4 %all-to-all-done.coef_own_ref = bf16[32,7,8,128]{3,2,1,0:T(8,128)(2,1)S(1)} async-done(((bf16[32,7,8,128]{3,2,1,0:T(8,128)(2,1)}), bf16[32,7,8,128]{3,2,1,0:T(8,128)(2,1)S(1)}, u32[]{:S(2)}, u32[]{:S(2)}) %all-to-all-start) | async-done | bytes 458784 | tf_op jit(solution)/shard_map/all_to_all | solution.py:313
  45.4 1.9 %collective-permute-start.3 = (bf16[32,7,8,128]{3,2,1,0:T(8,128)(2,1)S(1)}, bf16[32,7,8,128]{3,2,1,0:T(8,128)(2,1)S(1)}, u32[]{:S(2)}, u32[]{:S(2)}) collective-permute-start(bf16[32,7,8,128]{3,2,1,0:T(8,128)(2,1)S(1)} %all-to-all-done.coef_own_ref), channel_id=1, source_target_pairs={{1,0},{2,1},{3,2},{4,3},{5,4},{6,5},{7,6},{9,8},{10,9},{11,10},{12... | collective-permute-start | bytes 1376264 | tf_op jit(solution)/shard_map/ppermute | solution.py:285
  47.3 2.4 %collective-permute-start.2 = (bf16[32,7,8,128]{3,2,1,0:T(8,128)(2,1)S(1)}, bf16[32,7,8,128]{3,2,1,0:T(8,128)(2,1)}, u32[]{:S(2)}, u32[]{:S(2)}) collective-permute-start(bf16[32,7,8,128]{3,2,1,0:T(8,128)(2,1)S(1)} %all-to-all-done.coef_own_ref), channel_id=1, source_target_pairs={{0,1},{1,2},{2,3},{3,4},{4,5},{5,6},{6,7},{8,9},{9,10},{10,11},{11... | collective-permute-start | bytes 1376264 | tf_op jit(solution)/shard_map/ppermute | solution.py:285
  49.7 0.0 collective-permute-done.1.right_ref
  49.7 1.4 collective-permute-done.left_ref
  51.1 5.2 %shard_map.88.waves_ref = f32[10,768,128]{2,1,0:T(8,128)S(1)} custom-call(f32[10,8,4096]{2,1,0:T(8,128)} %collective-permute-done.left_ref, f32[10,8,4096]{2,1,0:T(8,128)S(1)} %bitcast.7, f32[10,8,4096]{2,1,0:T(8,128)S(1)} %collective-permute-done.1.right_ref), custom_call_target="tpu_custom_call" | custom-call | bytes 8388608 | tf_op jit(solution)/shard_map/pallas_call | solution.py:324
  56.3 0.0 collective-permute-done.3.coef_right_ref
  56.3 0.9 collective-permute-done.2.coef_left_ref
  57.2 20.7 %shard_map.89 = (f32[10,256,128]{2,1,0:T(8,128)S(1)}, f32[8,768,128]{2,1,0:T(8,128)S(1)}, f32[256,128]{1,0:T(8,128)S(1)}) custom-call(s32[1]{0:T(128)} %bitcast.2.slab_ref, f32[16,128]{1,0:T(8,128)S(1)} %reduce_sum.9.inject_ref, f32[10,768,128]{2,1,0:T(8,128)S(1)} %shard_map.88.waves_ref, bf16[32,7,8,128]{3,2,1,0:T(8,128)(2,1)} %collective-permute-done.2.coef_left_ref, ...), custom_call_target="tpu_custom_call" | custom-call | tf_op jit(solution)/shard_map/pallas_call | solution.py:335
  77.9 1.9 %collective-permute-start.5 = (f32[10,256,128]{2,1,0:T(8,128)S(1)}, f32[10,256,128]{2,1,0:T(8,128)S(1)}, u32[]{:S(2)}, u32[]{:S(2)}) collective-permute-start(f32[10,256,128]{2,1,0:T(8,128)S(1)} %get-tuple-element.11.own_ref), channel_id=1, source_target_pairs={{1,0},{2,1},{3,2},{4,3},{5,4},{6,5},{7,6},{9,8},{10,9},{11,10},{12... | collective-permute-start | bytes 3932168 | tf_op jit(solution)/shard_map/ppermute | solution.py:285
  79.9 2.4 %collective-permute-start.4 = (f32[10,256,128]{2,1,0:T(8,128)S(1)}, f32[10,256,128]{2,1,0:T(8,128)S(1)}, u32[]{:S(2)}, u32[]{:S(2)}) collective-permute-start(f32[10,256,128]{2,1,0:T(8,128)S(1)} %get-tuple-element.11.own_ref), channel_id=1, source_target_pairs={{0,1},{1,2},{2,3},{3,4},{4,5},{5,6},{6,7},{8,9},{9,10},{10,11},{11... | collective-permute-start | bytes 3932168 | tf_op jit(solution)/shard_map/ppermute | solution.py:285
  82.3 12.7 %collective-permute-done.5.right_ref = f32[10,256,128]{2,1,0:T(8,128)S(1)} collective-permute-done((f32[10,256,128]{2,1,0:T(8,128)S(1)}, f32[10,256,128]{2,1,0:T(8,128)S(1)}, u32[]{:S(2)}, u32[]{:S(2)}) %collective-permute-start.5) | collective-permute-done | bytes 1310752 | tf_op jit(solution)/shard_map/ppermute | solution.py:285
  95.0 3.8 %collective-permute-done.4.left_ref = f32[10,256,128]{2,1,0:T(8,128)S(1)} collective-permute-done((f32[10,256,128]{2,1,0:T(8,128)S(1)}, f32[10,256,128]{2,1,0:T(8,128)S(1)}, u32[]{:S(2)}, u32[]{:S(2)}) %collective-permute-start.4) | collective-permute-done | bytes 1310752 | tf_op jit(solution)/shard_map/ppermute | solution.py:285
  98.8 19.1 %shard_map.90 = (f32[10,8,4096]{2,1,0:T(8,128)}, f32[32,8,128]{2,1,0:T(8,128)S(1)}) custom-call(f32[16,128]{1,0:T(8,128)S(1)} %reduce_sum.9.inject_ref, f32[10,256,128]{2,1,0:T(8,128)S(1)} %collective-permute-done.4.left_ref, f32[10,256,128]{2,1,0:T(8,128)S(1)} %get-tuple-element.11.own_ref, f32[10,256,128]{2,1,0:T(8,128)S(1)} %collective-permute-done.5.right_ref, ...), custom_call_target="tpu_custom_call" | custom-call | tf_op jit(solution)/shard_map/pallas_call | solution.py:344
  117.9 23.6 %all_to_all.15.pieces_ref = f32[32,8,128]{2,1,0:T(8,128)S(1)} all-to-all(f32[32,8,128]{2,1,0:T(8,128)S(1)} %get-tuple-element.15), channel_id=1, replica_groups=mesh['shot'=32,'slab'=8] {'shot'}, dimensions={0} | all-to-all | bytes 262144 | tf_op jit(solution)/shard_map/all_to_all | solution.py:352
  141.5 1.4 shard_map.91
  (8 shorter events, 0.0 us)
Async XLA Ops:
  0.6 25.0 %copy-start = (f32[1,2,5,8,4096]{4,3,2,1,0:T(8,128)S(1)}, f32[1,2,5,8,4096]{4,3,2,1,0:T(8,128)}, u32[]{:S(2)}) copy-start(f32[1,2,5,8,4096]{4,3,2,1,0:T(8,128)} %param.7) | copy-start | bytes 3932164
  0.6 0.8 copy-start.2
  1.4 0.7 copy-start.5
  2.1 0.7 copy-start.6
  3.7 10.6 %all-to-all-start.1 = ((f32[8,16,128]{2,1,0:T(8,128)}), f32[8,16,128]{2,1,0:T(8,128)S(1)}, u32[]{:S(2)}, u32[]{:S(2)}) async-start(f32[8,16,128]{2,1,0:T(8,128)} %shard_map.87), calls=%async_computation.1 | async-start | bytes 131072 | tf_op jit(solution)/shard_map/all_to_all | solution.py:323
  9.7 0.9 copy-start.1
  10.6 0.7 copy-start.3
  11.2 0.7 copy-start.7
  14.3 31.1 %all-to-all-start = ((bf16[32,7,8,128]{3,2,1,0:T(8,128)(2,1)}), bf16[32,7,8,128]{3,2,1,0:T(8,128)(2,1)S(1)}, u32[]{:S(2)}, u32[]{:S(2)}) async-start(bf16[32,7,8,128]{3,2,1,0:T(8,128)(2,1)} %shard_map.86), calls=%async_computation | async-start | bytes 917504 | tf_op jit(solution)/shard_map/all_to_all | solution.py:313
  25.7 24.1 %collective-permute-start.1 = (f32[10,8,4096]{2,1,0:T(8,128)S(1)}, f32[10,8,4096]{2,1,0:T(8,128)S(1)}, u32[]{:S(2)}, u32[]{:S(2)}) collective-permute-start(f32[10,8,4096]{2,1,0:T(8,128)S(1)} %bitcast.5), channel_id=1, source_target_pairs={{1,0},{2,1},{3,2},{4,3},{5,4},{6,5},{7,6},{9,8},{10,9},{11,10},{12... | collective-permute-start | bytes 3932168 | tf_op jit(solution)/shard_map/ppermute | solution.py:285
  27.8 23.3 %collective-permute-start = (f32[10,8,4096]{2,1,0:T(8,128)S(1)}, f32[10,8,4096]{2,1,0:T(8,128)}, u32[]{:S(2)}, u32[]{:S(2)}) collective-permute-start(f32[10,8,4096]{2,1,0:T(8,128)S(1)} %bitcast.6), channel_id=1, source_target_pairs={{0,1},{1,2},{2,3},{3,4},{4,5},{5,6},{6,7},{8,9},{9,10},{10,11},{11... | collective-permute-start | bytes 3932168 | tf_op jit(solution)/shard_map/ppermute | solution.py:285
  45.4 10.9 %collective-permute-start.3 = (bf16[32,7,8,128]{3,2,1,0:T(8,128)(2,1)S(1)}, bf16[32,7,8,128]{3,2,1,0:T(8,128)(2,1)S(1)}, u32[]{:S(2)}, u32[]{:S(2)}) collective-permute-start(bf16[32,7,8,128]{3,2,1,0:T(8,128)(2,1)S(1)} %all-to-all-done.coef_own_ref), channel_id=1, source_target_pairs={{1,0},{2,1},{3,2},{4,3},{5,4},{6,5},{7,6},{9,8},{10,9},{11,10},{12... | collective-permute-start | bytes 1376264 | tf_op jit(solution)/shard_map/ppermute | solution.py:285
  47.3 9.9 %collective-permute-start.2 = (bf16[32,7,8,128]{3,2,1,0:T(8,128)(2,1)S(1)}, bf16[32,7,8,128]{3,2,1,0:T(8,128)(2,1)}, u32[]{:S(2)}, u32[]{:S(2)}) collective-permute-start(bf16[32,7,8,128]{3,2,1,0:T(8,128)(2,1)S(1)} %all-to-all-done.coef_own_ref), channel_id=1, source_target_pairs={{0,1},{1,2},{2,3},{3,4},{4,5},{5,6},{6,7},{8,9},{9,10},{10,11},{11... | collective-permute-start | bytes 1376264 | tf_op jit(solution)/shard_map/ppermute | solution.py:285
  77.9 17.0 %collective-permute-start.5 = (f32[10,256,128]{2,1,0:T(8,128)S(1)}, f32[10,256,128]{2,1,0:T(8,128)S(1)}, u32[]{:S(2)}, u32[]{:S(2)}) collective-permute-start(f32[10,256,128]{2,1,0:T(8,128)S(1)} %get-tuple-element.11.own_ref), channel_id=1, source_target_pairs={{1,0},{2,1},{3,2},{4,3},{5,4},{6,5},{7,6},{9,8},{10,9},{11,10},{12... | collective-permute-start | bytes 3932168 | tf_op jit(solution)/shard_map/ppermute | solution.py:285
  79.9 18.9 %collective-permute-start.4 = (f32[10,256,128]{2,1,0:T(8,128)S(1)}, f32[10,256,128]{2,1,0:T(8,128)S(1)}, u32[]{:S(2)}, u32[]{:S(2)}) collective-permute-start(f32[10,256,128]{2,1,0:T(8,128)S(1)} %get-tuple-element.11.own_ref), channel_id=1, source_target_pairs={{0,1},{1,2},{2,3},{3,4},{4,5},{5,6},{6,7},{8,9},{9,10},{10,11},{11... | collective-permute-start | bytes 3932168 | tf_op jit(solution)/shard_map/ppermute | solution.py:285
  98.8 42.7 %copy-start.4 = (s32[32]{0:T(128)S(1)}, s32[32]{0:T(128)}, u32[]{:S(2)}) copy-start(s32[32]{0:T(128)} %offsets_ref.3) | copy-start | bytes 388

commit v3 on v2

--- a/solution.py
+++ b/solution.py
@@ -20,7 +20,7 @@
 HELD = 36
 GRADS, PARTS, PLANES = 10, 14, 22
 ROWS = 32
-VMEM_LIMIT = 40 * 1024 * 1024
+VMEM_LIMIT = 32 * 1024 * 1024
 
 
 def pick_kernel(offsets_ref, directory_ref, store_ref, out_ref):
@@ -59,7 +59,7 @@
     return jnp.where(lane == 127, jnp.concatenate([r[8:32], wrap], axis=0), r)
 
 
-def advance(state, coef, image, inject_ref, first_step):
+def advance(state, coef, image, slab, inject_ref, first_step):
     lane = lane_index()
     sub = iota8(0)
     spot = jnp.where((iota8(0) == 0) & (iota8(1) == REC_DEPTH), 1.0, 0.0)
@@ -94,7 +94,7 @@
                     vx, vz = vx - gx, vz - gz
                 else:
                     vx, vz = vx + gx, vz + gz
-                    add = inject_ref[first_step + step - 1, a + k]
+                    add = inject_ref[first_step + step - 1, (slab + 1) * COLS + a + k]
                     vz = jnp.concatenate([vz[0:8] + add * spot, vz[8:32]], axis=0)
                 state[5 * w, at(base, k), :] = vx * damp
                 state[5 * w + 1, at(base, k), :] = vz * damp
@@ -161,16 +161,14 @@
 
 def inject_kernel(traces_ref, tile_ref, col_ref, out_ref):
     cell = tile_ref[...] * COLS + col_ref[...]
-    column = lax.broadcasted_iota(jnp.int32, (128, 128), 0)
-    for slab in range(out_ref.shape[0]):
-        hit = (cell == column + (slab - 1) * COLS) & (column < WIDE)
-        out_ref[slab] = lax.dot_general(
-            traces_ref[...],
-            jnp.where(hit, 1.0, 0.0),
-            (((1,), (1,)), ((), ())),
-            precision=lax.Precision.HIGHEST,
-            preferred_element_type=jnp.float32,
-        )
+    lane = lax.broadcasted_iota(jnp.int32, (128, 128), 0)
+    out_ref[...] = lax.dot_general(
+        traces_ref[...],
+        jnp.where(cell + 2 * COLS == lane, 1.0, 0.0),
+        (((1,), (1,)), ((), ())),
+        precision=lax.Precision.HIGHEST,
+        preferred_element_type=jnp.float32,
+    )
 
 
 def first_kernel(
@@ -182,10 +180,9 @@
     coef_own_ref,
     coef_right_ref,
     state_out,
-    coef_out,
+    coef,
     image_out,
     state,
-    coef,
     image,
     sem,
 ):
@@ -204,7 +201,8 @@
     depth = ROWS * 128
     wide_z = jnp.maximum(jnp.maximum(PML - z, z - (depth - 1 - PML)), 0).astype(jnp.float32) / PML
     square_z = wide_z * wide_z
-    first = (slab_ref[0] - 1) * COLS
+    slab = slab_ref[0]
+    first = (slab - 1) * COLS
 
     def profile(i, _):
         x = first + i
@@ -217,25 +215,23 @@
     lax.fori_loop(0, WIDE, profile, 0)
     image[...] = jnp.zeros_like(image)
     copy.wait()
-    advance(state, coef, image, inject_ref, 0)
+    advance(state, coef, image, slab, inject_ref, 0)
     for q in range(10):
         state_out[q] = state[q, window(1), :]
-    for q in range(8):
-        coef_out[q] = coef[q, all_rows, :]
     image_out[...] = image[window(1), :]
 
 
 def second_kernel(
+    slab_ref,
     inject_ref,
     left_ref,
     own_ref,
     right_ref,
-    coef_ref,
+    coef,
     image_in,
     waves_out,
     image_out,
     state,
-    coef,
     image,
     sems,
 ):
@@ -243,14 +239,13 @@
         pltpu.make_async_copy(ref, state.at[pl.ds(0, 10), window(part), :], sems.at[part])
         for part, ref in enumerate((left_ref, own_ref, right_ref))
     ]
-    copies.append(pltpu.make_async_copy(coef_ref, coef.at[:, pl.ds(PAD * ROWS, WIDE * ROWS), :], sems.at[3]))
     for copy in copies:
         copy.start()
     image[...] = jnp.zeros_like(image)
     image[window(1), :] = image_in[...]
     for copy in copies:
         copy.wait()
-    advance(state, coef, image, inject_ref, PHASE)
+    advance(state, coef, image, slab_ref[0], inject_ref, PHASE)
     for tile in range(TILES):
         rows = pl.ds((PAD + COLS) * ROWS + row_of(tile), COLS, stride=ROWS)
         for q in range(10):
@@ -272,6 +267,7 @@
 ANY = pl.BlockSpec(memory_space=pl.ANY)
 SMEM = pl.BlockSpec(memory_space=pltpu.SMEM)
 PARAMS = pltpu.CompilerParams(vmem_limit_bytes=VMEM_LIMIT)
+LARGE = pltpu.CompilerParams(vmem_limit_bytes=56 * 1024 * 1024)
 
 
 def shape(*dims, dtype=jnp.float32):
@@ -289,7 +285,6 @@
     held = HELD * ROWS
     return [
         pltpu.VMEM((PLANES, held, 128), jnp.float32),
-        pltpu.VMEM((8, held, 128), jnp.float32),
         pltpu.VMEM((held, 128), jnp.float32),
         pltpu.SemaphoreType.DMA((copies,)) if copies > 1 else pltpu.SemaphoreType.DMA,
     ]
@@ -303,24 +298,29 @@
     own_rows = COLS * ROWS
     all_rows = WIDE * ROWS
 
+    def added(rows, bit):
+        partner = [(i, i ^ bit) for i in range(slabs)]
+        return rows + lax.ppermute(rows, "slab", partner)
+
+    inject = pl.pallas_call(
+        inject_kernel,
+        out_shape=shape(STEPS, 128),
+        in_specs=[VMEM] * 3,
+        out_specs=VMEM,
+        compiler_params=LARGE,
+    )(traces[0], rec_tile.reshape(1, -1), rec_col)
+    inject, store = lax.optimization_barrier((inject, model_store))
     picked = pl.pallas_call(
         pick_kernel,
         out_shape=shape(shots, 7, COLS, 128, dtype=jnp.bfloat16),
         in_specs=[SMEM, SMEM, VMEM],
         out_specs=VMEM,
-        compiler_params=PARAMS,
-    )(offsets, directory, model_store)
+        compiler_params=LARGE,
+    )(offsets, directory, store)
+    inject, picked = lax.optimization_barrier((added(added(inject, 1), 2), picked))
     coef_own = lax.all_to_all(picked, "shot", split_axis=0, concat_axis=0, tiled=True)
-
+    inject, own = lax.optimization_barrier((added(inject, 4), own))
     left, right = neighbours(own, "slab")
-    adds = pl.pallas_call(
-        inject_kernel,
-        out_shape=shape(slabs, STEPS, 128),
-        in_specs=[VMEM] * 3,
-        out_specs=VMEM,
-        compiler_params=PARAMS,
-    )(traces[0], rec_tile.reshape(1, -1), rec_col)
-    inject = lax.all_to_all(adds, "slab", split_axis=0, concat_axis=0, tiled=True).sum(axis=0)
     waves_in = pl.pallas_call(
         waves_kernel,
         out_shape=shape(10, all_rows, 128),
@@ -330,25 +330,25 @@
         cost_estimate=pl.CostEstimate(flops=0, bytes_accessed=8 << 20, transcendentals=0),
     )(left, own, right)
 
-    coef_own, inject = lax.optimization_barrier((coef_own, inject))
+    slab = lax.axis_index("slab").astype(jnp.int32).reshape(1)
     coef_left, coef_right = neighbours(coef_own, "slab")
     state, coef, image = pl.pallas_call(
         functools.partial(first_kernel, slabs),
-        out_shape=(shape(10, own_rows, 128), shape(8, all_rows, 128), shape(own_rows, 128)),
+        out_shape=(shape(10, own_rows, 128), shape(8, HELD * ROWS, 128), shape(own_rows, 128)),
         in_specs=[SMEM, SMEM, ANY] + [VMEM] * 3,
         out_specs=(VMEM,) * 3,
         scratch_shapes=scratch(1),
         compiler_params=PARAMS,
-    )(lax.axis_index("slab").astype(jnp.int32).reshape(1), inject, waves_in, coef_left, coef_own, coef_right)
+    )(slab, inject, waves_in, coef_left, coef_own, coef_right)
     state_left, state_right = neighbours(state, "slab")
     waves_out, pieces = pl.pallas_call(
         second_kernel,
         out_shape=(shape(10, COLS, depth), shape(TILES, COLS, 128)),
-        in_specs=[SMEM] + [ANY] * 4 + [VMEM],
+        in_specs=[SMEM, SMEM] + [ANY] * 3 + [VMEM] * 2,
         out_specs=(VMEM,) * 2,
-        scratch_shapes=scratch(4),
+        scratch_shapes=scratch(3),
         compiler_params=PARAMS,
-    )(inject, state_left, state, state_right, coef, image)
+    )(slab, inject, state_left, state, state_right, coef, image)
     pieces = lax.all_to_all(pieces, "shot", split_axis=0, concat_axis=0, tiled=True)
     stacked = pl.pallas_call(
         stack_kernel,

time: 143 us -> 145 us (1.014)
  local copies, waits for them, and re-layouts: 4.32 us -> 0.01 us
  blocking collectives: 23.6 us -> 26.7 us
  waiting for transfers between devices: 34.9 us -> 36.7 us
    all_to_all x1, waiting for transfers between devices: 15.4 us -> 7.55 us  [local(): lax.all_to_all(picked, 'shot', split_axis=0, concat_axis=0, tiled=True)]
    ppermute x0 -> x3, waiting for transfers between devices: none -> 7.37 us  [added(): return rows + lax.ppermute(rows, 'slab', partner)]
    all_to_all x1 -> x0, starting transfers between devices: 6.01 us -> none  [local(): lax.all_to_all(adds, 'slab', split_axis=0, concat_axis=0, tiled=True)]
    unnamed x16 -> x4, local copies, waits for them, and re-layouts: 4.32 us -> 0.01 us
    ppermute x0 -> x3, starting transfers between devices: none -> 3.41 us  [added(): return rows + lax.ppermute(rows, 'slab', partner)]
    all_to_all x1, blocking collectives: 23.6 us -> 26.7 us  [local(): lax.all_to_all(pieces, 'shot', split_axis=0, concat_axis=0, tiled=True)]
    ppermute x6, waiting for transfers between devices: 18.8 us -> 21.8 us  [neighbours(): return (lax.ppermute(block, axis, up), lax.ppermute(block, axis, down))]
    all_to_all x1, starting transfers between devices: 11.3 us -> 12.8 us  [local(): lax.all_to_all(picked, 'shot', split_axis=0, concat_axis=0, tiled=True)]
  transfers between devices with their start and end apart: 8 -> 10, of which waited for: 6 -> 7; matrix products, arithmetic and copies ran while one was open for 0% -> 0% of each run, Pallas kernels for 5% -> 5%
where the time goes in v3:
time: 145 us; the launch traced here: 144 us
  Pallas kernels  50.4 us (35%)
  waiting for transfers between devices  36.7 us (25%)
  starting transfers between devices  29.2 us (20%)
  blocking collectives  26.7 us (18%)
    all_to_all x1, blocking collectives, local(): lax.all_to_all(pieces, 'shot', split_axis=0, concat_axis=0, tiled=True)  26.7 us
    ppermute x6, waiting for transfers between devices, neighbours(): return (lax.ppermute(block, axis, up), lax.ppermute(block, axis, down))  21.8 us
    pallas_call x1, Pallas kernels, local(): pl.pallas_call(functools.partial(first_kernel, slabs), out_shape=(shape(1...  20.9 us
    pallas_call x1, Pallas kernels, local(): pl.pallas_call(second_kernel, out_shape=(shape(10, COLS, depth), shape(TI...  19.2 us
    ppermute x6, starting transfers between devices, neighbours(): return (lax.ppermute(block, axis, up), lax.ppermute(block, axis, down))  13 us
    all_to_all x1, starting transfers between devices, local(): lax.all_to_all(picked, 'shot', split_axis=0, concat_axis=0, tiled=True)  12.8 us
    all_to_all x1, waiting for transfers between devices, local(): lax.all_to_all(picked, 'shot', split_axis=0, concat_axis=0, tiled=True)  7.55 us
    ppermute x3, waiting for transfers between devices, added(): return rows + lax.ppermute(rows, 'slab', partner)  7.37 us
  transfers between devices with their start and end apart: 10, of which 7 were waited for; matrix products, arithmetic and copies ran while one was open for 0% of the time, Pallas kernels for 5%

profile of v3, /device:TPU:32, one launch (start us, length us, event | category | flops | bytes accessed | tf_op | source)
XLA Modules:
  0.0 144.5 jit_solution(4576268294633180769)
XLA Ops:
  0.6 0.0 copy-start
  0.6 1.6 %shard_map.86 = f32[16,128]{1,0:T(8,128)} custom-call(f32[16,128]{1,0:T(8,128)} %bitcast.8, s32[1,128]{1,0:T(1,128)} %bitcast.9, s32[1,128]{1,0:T(1,128)} %col_ref.1), custom_call_target="tpu_custom_call" | custom-call | tf_op jit(solution)/shard_map/pallas_call | solution.py:305
  2.3 0.0 collective-permute-start
  2.3 1.4 collective-permute-done
  3.7 0.7 add.9
  4.4 1.8 %collective-permute-start.1 = (f32[16,128]{1,0:T(8,128)S(1)}, f32[16,128]{1,0:T(8,128)S(1)}, u32[]{:S(2)}, u32[]{:S(2)}) collective-permute-start(f32[16,128]{1,0:T(8,128)S(1)} %add.9), channel_id=1, source_target_pairs={{0,2},{1,3},{2,0},{3,1},{4,6},{5,7},{6,4},{7,5},{8,10},{9,11},{10,... | collective-permute-start | bytes 24584 | tf_op jit(solution)/shard_map/ppermute | solution.py:303
  6.2 2.0 %shard_map.87 = bf16[32,7,8,128]{3,2,1,0:T(8,128)(2,1)} custom-call(s32[32]{0:T(128)} %offsets_ref.3, s32[8]{0:T(128)} %directory_ref.1, bf16[7,8,8,128]{3,2,1,0:T(8,128)(2,1)} %store_ref), custom_call_target="tpu_custom_call" | custom-call | tf_op jit(solution)/shard_map/pallas_call | solution.py:313
  8.3 0.0 collective-permute-done.1
  8.3 12.8 %all-to-all-start = ((bf16[32,7,8,128]{3,2,1,0:T(8,128)(2,1)}), bf16[32,7,8,128]{3,2,1,0:T(8,128)(2,1)S(1)}, u32[]{:S(2)}, u32[]{:S(2)}) async-start(bf16[32,7,8,128]{3,2,1,0:T(8,128)(2,1)} %shard_map.87), calls=%async_computation | async-start | bytes 917504 | tf_op jit(solution)/shard_map/all_to_all | solution.py:321
  21.1 1.6 %collective-permute-start.2 = (f32[16,128]{1,0:T(8,128)S(1)}, f32[16,128]{1,0:T(8,128)S(1)}, u32[]{:S(2)}, u32[]{:S(2)}) collective-permute-start(f32[16,128]{1,0:T(8,128)S(1)} %add.10), channel_id=1, source_target_pairs={{0,4},{1,5},{2,6},{3,7},{4,0},{5,1},{6,2},{7,3},{8,12},{9,13},{10,... | collective-permute-start | bytes 24584 | tf_op jit(solution)/shard_map/ppermute | solution.py:303
  22.6 6.0 %collective-permute-done.2 = f32[16,128]{1,0:T(8,128)S(1)} collective-permute-done((f32[16,128]{1,0:T(8,128)S(1)}, f32[16,128]{1,0:T(8,128)S(1)}, u32[]{:S(2)}, u32[]{:S(2)}) %collective-permute-start.2) | collective-permute-done | bytes 8224 | tf_op jit(solution)/shard_map/ppermute | solution.py:303
  28.6 0.0 copy-done
  28.6 1.9 %collective-permute-start.4 = (f32[10,8,4096]{2,1,0:T(8,128)S(1)}, f32[10,8,4096]{2,1,0:T(8,128)S(1)}, u32[]{:S(2)}, u32[]{:S(2)}) collective-permute-start(f32[10,8,4096]{2,1,0:T(8,128)S(1)} %bitcast.5), channel_id=1, source_target_pairs={{1,0},{2,1},{3,2},{4,3},{5,4},{6,5},{7,6},{9,8},{10,9},{11,10},{12... | collective-permute-start | bytes 3932168 | tf_op jit(solution)/shard_map/ppermute | solution.py:281
  30.5 2.4 %collective-permute-start.3 = (f32[10,8,4096]{2,1,0:T(8,128)S(1)}, f32[10,8,4096]{2,1,0:T(8,128)}, u32[]{:S(2)}, u32[]{:S(2)}) collective-permute-start(f32[10,8,4096]{2,1,0:T(8,128)S(1)} %bitcast.6), channel_id=1, source_target_pairs={{0,1},{1,2},{2,3},{3,4},{4,5},{5,6},{6,7},{8,9},{9,10},{10,11},{11... | collective-permute-start | bytes 3932168 | tf_op jit(solution)/shard_map/ppermute | solution.py:281
  33.0 7.6 %all-to-all-done.coef_own_ref = bf16[32,7,8,128]{3,2,1,0:T(8,128)(2,1)S(1)} async-done(((bf16[32,7,8,128]{3,2,1,0:T(8,128)(2,1)}), bf16[32,7,8,128]{3,2,1,0:T(8,128)(2,1)S(1)}, u32[]{:S(2)}, u32[]{:S(2)}) %all-to-all-start) | async-done | bytes 458784 | tf_op jit(solution)/shard_map/all_to_all | solution.py:321
  40.5 1.9 %collective-permute-start.6 = (bf16[32,7,8,128]{3,2,1,0:T(8,128)(2,1)S(1)}, bf16[32,7,8,128]{3,2,1,0:T(8,128)(2,1)S(1)}, u32[]{:S(2)}, u32[]{:S(2)}) collective-permute-start(bf16[32,7,8,128]{3,2,1,0:T(8,128)(2,1)S(1)} %all-to-all-done.coef_own_ref), channel_id=1, source_target_pairs={{1,0},{2,1},{3,2},{4,3},{5,4},{6,5},{7,6},{9,8},{10,9},{11,10},{12... | collective-permute-start | bytes 1376264 | tf_op jit(solution)/shard_map/ppermute | solution.py:281
  42.4 2.4 %collective-permute-start.5 = (bf16[32,7,8,128]{3,2,1,0:T(8,128)(2,1)S(1)}, bf16[32,7,8,128]{3,2,1,0:T(8,128)(2,1)}, u32[]{:S(2)}, u32[]{:S(2)}) collective-permute-start(bf16[32,7,8,128]{3,2,1,0:T(8,128)(2,1)S(1)} %all-to-all-done.coef_own_ref), channel_id=1, source_target_pairs={{0,1},{1,2},{2,3},{3,4},{4,5},{5,6},{6,7},{8,9},{9,10},{10,11},{11... | collective-permute-start | bytes 1376264 | tf_op jit(solution)/shard_map/ppermute | solution.py:281
  44.8 0.8 collective-permute-done.4.right_ref
  45.6 4.5 %collective-permute-done.3.left_ref = f32[10,8,4096]{2,1,0:T(8,128)} collective-permute-done((f32[10,8,4096]{2,1,0:T(8,128)S(1)}, f32[10,8,4096]{2,1,0:T(8,128)}, u32[]{:S(2)}, u32[]{:S(2)}) %collective-permute-start.3) | collective-permute-done | bytes 1310752 | tf_op jit(solution)/shard_map/ppermute | solution.py:281
  50.1 5.2 %shard_map.88.waves_ref = f32[10,768,128]{2,1,0:T(8,128)S(1)} custom-call(f32[10,8,4096]{2,1,0:T(8,128)} %collective-permute-done.3.left_ref, f32[10,8,4096]{2,1,0:T(8,128)S(1)} %bitcast.7, f32[10,8,4096]{2,1,0:T(8,128)S(1)} %collective-permute-done.4.right_ref), custom_call_target="tpu_custom_call" | custom-call | bytes 8388608 | tf_op jit(solution)/shard_map/pallas_call | solution.py:324
  55.3 0.0 collective-permute-done.6.coef_right_ref
  55.4 0.0 collective-permute-done.5.coef_left_ref
  55.4 20.9 %shard_map.89 = (f32[10,256,128]{2,1,0:T(8,128)S(1)}, f32[8,1152,128]{2,1,0:T(8,128)S(1)}, f32[256,128]{1,0:T(8,128)S(1)}) custom-call(s32[1]{0:T(128)} %bitcast.slab_ref, f32[16,128]{1,0:T(8,128)S(1)} %add.11.inject_ref, f32[10,768,128]{2,1,0:T(8,128)S(1)} %shard_map.88.waves_ref, bf16[32,7,8,128]{3,2,1,0:T(8,128)(2,1)} %collective-permute-done.5.coef_left_ref, ...), custom_call_target="tpu_custom_call" | custom-call | tf_op jit(solution)/shard_map/pallas_call | solution.py:335
  76.3 1.9 %collective-permute-start.8 = (f32[10,256,128]{2,1,0:T(8,128)S(1)}, f32[10,256,128]{2,1,0:T(8,128)S(1)}, u32[]{:S(2)}, u32[]{:S(2)}) collective-permute-start(f32[10,256,128]{2,1,0:T(8,128)S(1)} %get-tuple-element.19.own_ref), channel_id=1, source_target_pairs={{1,0},{2,1},{3,2},{4,3},{5,4},{6,5},{7,6},{9,8},{10,9},{11,10},{12... | collective-permute-start | bytes 3932168 | tf_op jit(solution)/shard_map/ppermute | solution.py:281
  78.2 2.4 %collective-permute-start.7 = (f32[10,256,128]{2,1,0:T(8,128)S(1)}, f32[10,256,128]{2,1,0:T(8,128)S(1)}, u32[]{:S(2)}, u32[]{:S(2)}) collective-permute-start(f32[10,256,128]{2,1,0:T(8,128)S(1)} %get-tuple-element.19.own_ref), channel_id=1, source_target_pairs={{0,1},{1,2},{2,3},{3,4},{4,5},{5,6},{6,7},{8,9},{9,10},{10,11},{11... | collective-permute-start | bytes 3932168 | tf_op jit(solution)/shard_map/ppermute | solution.py:281
  80.6 12.7 %collective-permute-done.8.right_ref = f32[10,256,128]{2,1,0:T(8,128)S(1)} collective-permute-done((f32[10,256,128]{2,1,0:T(8,128)S(1)}, f32[10,256,128]{2,1,0:T(8,128)S(1)}, u32[]{:S(2)}, u32[]{:S(2)}) %collective-permute-start.8) | collective-permute-done | bytes 1310752 | tf_op jit(solution)/shard_map/ppermute | solution.py:281
  93.3 3.8 %collective-permute-done.7.left_ref = f32[10,256,128]{2,1,0:T(8,128)S(1)} collective-permute-done((f32[10,256,128]{2,1,0:T(8,128)S(1)}, f32[10,256,128]{2,1,0:T(8,128)S(1)}, u32[]{:S(2)}, u32[]{:S(2)}) %collective-permute-start.7) | collective-permute-done | bytes 1310752 | tf_op jit(solution)/shard_map/ppermute | solution.py:281
  97.1 0.0 copy-start.1
  97.1 19.2 %shard_map.90 = (f32[10,8,4096]{2,1,0:T(8,128)}, f32[32,8,128]{2,1,0:T(8,128)S(1)}) custom-call(s32[1]{0:T(128)} %bitcast.slab_ref, f32[16,128]{1,0:T(8,128)S(1)} %add.11.inject_ref, f32[10,256,128]{2,1,0:T(8,128)S(1)} %collective-permute-done.7.left_ref, f32[10,256,128]{2,1,0:T(8,128)S(1)} %get-tuple-element.19.own_ref, ...), custom_call_target="tpu_custom_call" | custom-call | tf_op jit(solution)/shard_map/pallas_call | solution.py:344
  116.4 26.7 %all_to_all.10.pieces_ref = f32[32,8,128]{2,1,0:T(8,128)S(1)} all-to-all(f32[32,8,128]{2,1,0:T(8,128)S(1)} %get-tuple-element.23), channel_id=1, replica_groups=mesh['shot'=32,'slab'=8] {'shot'}, dimensions={0} | all-to-all | bytes 262144 | tf_op jit(solution)/shard_map/all_to_all | solution.py:352
  143.1 0.0 copy-done.1
  143.1 1.4 shard_map.91
  (2 shorter events, 0.0 us)
Async XLA Ops:
  0.6 28.0 %copy-start = (f32[1,2,5,8,4096]{4,3,2,1,0:T(8,128)S(1)}, f32[1,2,5,8,4096]{4,3,2,1,0:T(8,128)}, u32[]{:S(2)}) copy-start(f32[1,2,5,8,4096]{4,3,2,1,0:T(8,128)} %param.7) | copy-start | bytes 3932164
  2.3 1.4 collective-permute-start
  4.4 3.9 %collective-permute-start.1 = (f32[16,128]{1,0:T(8,128)S(1)}, f32[16,128]{1,0:T(8,128)S(1)}, u32[]{:S(2)}, u32[]{:S(2)}) collective-permute-start(f32[16,128]{1,0:T(8,128)S(1)} %add.9), channel_id=1, source_target_pairs={{0,2},{1,3},{2,0},{3,1},{4,6},{5,7},{6,4},{7,5},{8,10},{9,11},{10,... | collective-permute-start | bytes 24584 | tf_op jit(solution)/shard_map/ppermute | solution.py:303
  8.3 32.3 %all-to-all-start = ((bf16[32,7,8,128]{3,2,1,0:T(8,128)(2,1)}), bf16[32,7,8,128]{3,2,1,0:T(8,128)(2,1)S(1)}, u32[]{:S(2)}, u32[]{:S(2)}) async-start(bf16[32,7,8,128]{3,2,1,0:T(8,128)(2,1)} %shard_map.87), calls=%async_computation | async-start | bytes 917504 | tf_op jit(solution)/shard_map/all_to_all | solution.py:321
  21.1 7.5 %collective-permute-start.2 = (f32[16,128]{1,0:T(8,128)S(1)}, f32[16,128]{1,0:T(8,128)S(1)}, u32[]{:S(2)}, u32[]{:S(2)}) collective-permute-start(f32[16,128]{1,0:T(8,128)S(1)} %add.10), channel_id=1, source_target_pairs={{0,4},{1,5},{2,6},{3,7},{4,0},{5,1},{6,2},{7,3},{8,12},{9,13},{10,... | collective-permute-start | bytes 24584 | tf_op jit(solution)/shard_map/ppermute | solution.py:303
  28.6 17.0 %collective-permute-start.4 = (f32[10,8,4096]{2,1,0:T(8,128)S(1)}, f32[10,8,4096]{2,1,0:T(8,128)S(1)}, u32[]{:S(2)}, u32[]{:S(2)}) collective-permute-start(f32[10,8,4096]{2,1,0:T(8,128)S(1)} %bitcast.5), channel_id=1, source_target_pairs={{1,0},{2,1},{3,2},{4,3},{5,4},{6,5},{7,6},{9,8},{10,9},{11,10},{12... | collective-permute-start | bytes 3932168 | tf_op jit(solution)/shard_map/ppermute | solution.py:281
  30.5 19.6 %collective-permute-start.3 = (f32[10,8,4096]{2,1,0:T(8,128)S(1)}, f32[10,8,4096]{2,1,0:T(8,128)}, u32[]{:S(2)}, u32[]{:S(2)}) collective-permute-start(f32[10,8,4096]{2,1,0:T(8,128)S(1)} %bitcast.6), channel_id=1, source_target_pairs={{0,1},{1,2},{2,3},{3,4},{4,5},{5,6},{6,7},{8,9},{9,10},{10,11},{11... | collective-permute-start | bytes 3932168 | tf_op jit(solution)/shard_map/ppermute | solution.py:281
  40.5 14.8 %collective-permute-start.6 = (bf16[32,7,8,128]{3,2,1,0:T(8,128)(2,1)S(1)}, bf16[32,7,8,128]{3,2,1,0:T(8,128)(2,1)S(1)}, u32[]{:S(2)}, u32[]{:S(2)}) collective-permute-start(bf16[32,7,8,128]{3,2,1,0:T(8,128)(2,1)S(1)} %all-to-all-done.coef_own_ref), channel_id=1, source_target_pairs={{1,0},{2,1},{3,2},{4,3},{5,4},{6,5},{7,6},{9,8},{10,9},{11,10},{12... | collective-permute-start | bytes 1376264 | tf_op jit(solution)/shard_map/ppermute | solution.py:281
  42.4 12.9 %collective-permute-start.5 = (bf16[32,7,8,128]{3,2,1,0:T(8,128)(2,1)S(1)}, bf16[32,7,8,128]{3,2,1,0:T(8,128)(2,1)}, u32[]{:S(2)}, u32[]{:S(2)}) collective-permute-start(bf16[32,7,8,128]{3,2,1,0:T(8,128)(2,1)S(1)} %all-to-all-done.coef_own_ref), channel_id=1, source_target_pairs={{0,1},{1,2},{2,3},{3,4},{4,5},{5,6},{6,7},{8,9},{9,10},{10,11},{11... | collective-permute-start | bytes 1376264 | tf_op jit(solution)/shard_map/ppermute | solution.py:281
  76.3 17.0 %collective-permute-start.8 = (f32[10,256,128]{2,1,0:T(8,128)S(1)}, f32[10,256,128]{2,1,0:T(8,128)S(1)}, u32[]{:S(2)}, u32[]{:S(2)}) collective-permute-start(f32[10,256,128]{2,1,0:T(8,128)S(1)} %get-tuple-element.19.own_ref), channel_id=1, source_target_pairs={{1,0},{2,1},{3,2},{4,3},{5,4},{6,5},{7,6},{9,8},{10,9},{11,10},{12... | collective-permute-start | bytes 3932168 | tf_op jit(solution)/shard_map/ppermute | solution.py:281
  78.2 18.9 %collective-permute-start.7 = (f32[10,256,128]{2,1,0:T(8,128)S(1)}, f32[10,256,128]{2,1,0:T(8,128)S(1)}, u32[]{:S(2)}, u32[]{:S(2)}) collective-permute-start(f32[10,256,128]{2,1,0:T(8,128)S(1)} %get-tuple-element.19.own_ref), channel_id=1, source_target_pairs={{0,1},{1,2},{2,3},{3,4},{4,5},{5,6},{6,7},{8,9},{9,10},{10,11},{11... | collective-permute-start | bytes 3932168 | tf_op jit(solution)/shard_map/ppermute | solution.py:281
  97.1 46.0 %copy-start.1 = (s32[32]{0:T(128)S(1)}, s32[32]{0:T(128)}, u32[]{:S(2)}) copy-start(s32[32]{0:T(128)} %offsets_ref.3) | copy-start | bytes 388

commit v4 on v3

--- a/solution.py
+++ b/solution.py
@@ -151,12 +151,21 @@
     return pl.ds((PAD + part * COLS) * ROWS, COLS * ROWS)
 
 
-def waves_kernel(left_ref, own_ref, right_ref, out_ref):
-    for part, waves in enumerate((left_ref, own_ref, right_ref)):
-        for tile in range(TILES):
-            rows = pl.ds(part * COLS * ROWS + row_of(tile), COLS, stride=ROWS)
-            for q in range(10):
-                out_ref[q, rows, :] = waves[q, :, pl.ds(tile * 128, 128)]
+def waves_kernel(waves_ref, out_ref):
+    for tile in range(TILES):
+        rows = pl.ds(row_of(tile), COLS, stride=ROWS)
+        for q in range(10):
+            out_ref[q, rows, :] = waves_ref[q, :, pl.ds(tile * 128, 128)]
+
+
+def fetch(slabs, state, sems):
+    copies = [
+        pltpu.make_async_copy(ref, state.at[pl.ds(0, 10), window(part), :], sems.at[part])
+        for part, ref in enumerate(slabs)
+    ]
+    for copy in copies:
+        copy.start()
+    return copies
 
 
 def inject_kernel(traces_ref, tile_ref, col_ref, out_ref):
@@ -175,7 +184,9 @@
     slabs,
     slab_ref,
     inject_ref,
-    waves_ref,
+    left_ref,
+    own_ref,
+    right_ref,
     coef_left_ref,
     coef_own_ref,
     coef_right_ref,
@@ -184,11 +195,9 @@
     image_out,
     state,
     image,
-    sem,
+    sems,
 ):
-    all_rows = pl.ds(PAD * ROWS, WIDE * ROWS)
-    copy = pltpu.make_async_copy(waves_ref, state.at[pl.ds(0, 10), all_rows, :], sem)
-    copy.start()
+    copies = fetch((left_ref, own_ref, right_ref), state, sems)
     for part, store in enumerate((coef_left_ref, coef_own_ref, coef_right_ref)):
         base = (PAD + part * COLS) * ROWS
         for tile in range(TILES):
@@ -214,7 +223,8 @@
 
     lax.fori_loop(0, WIDE, profile, 0)
     image[...] = jnp.zeros_like(image)
-    copy.wait()
+    for copy in copies:
+        copy.wait()
     advance(state, coef, image, slab, inject_ref, 0)
     for q in range(10):
         state_out[q] = state[q, window(1), :]
@@ -235,12 +245,7 @@
     image,
     sems,
 ):
-    copies = [
-        pltpu.make_async_copy(ref, state.at[pl.ds(0, 10), window(part), :], sems.at[part])
-        for part, ref in enumerate((left_ref, own_ref, right_ref))
-    ]
-    for copy in copies:
-        copy.start()
+    copies = fetch((left_ref, own_ref, right_ref), state, sems)
     image[...] = jnp.zeros_like(image)
     image[window(1), :] = image_in[...]
     for copy in copies:
@@ -281,12 +286,12 @@
     return lax.ppermute(block, axis, up), lax.ppermute(block, axis, down)
 
 
-def scratch(copies):
+def scratch():
     held = HELD * ROWS
     return [
         pltpu.VMEM((PLANES, held, 128), jnp.float32),
         pltpu.VMEM((held, 128), jnp.float32),
-        pltpu.SemaphoreType.DMA((copies,)) if copies > 1 else pltpu.SemaphoreType.DMA,
+        pltpu.SemaphoreType.DMA((3,)),
     ]
 
 
@@ -296,12 +301,28 @@
     depth = waves.shape[4]
     own = waves.reshape(10, COLS, depth)
     own_rows = COLS * ROWS
-    all_rows = WIDE * ROWS
 
     def added(rows, bit):
         partner = [(i, i ^ bit) for i in range(slabs)]
         return rows + lax.ppermute(rows, "slab", partner)
 
+    picked = pl.pallas_call(
+        pick_kernel,
+        out_shape=shape(shots, 7, COLS, 128, dtype=jnp.bfloat16),
+        in_specs=[SMEM, SMEM, VMEM],
+        out_specs=VMEM,
+        compiler_params=LARGE,
+    )(offsets, directory, model_store)
+    picked, own, traces = lax.optimization_barrier((picked, own, traces))
+    coef_own = lax.all_to_all(picked, "shot", split_axis=0, concat_axis=0, tiled=True)
+    own = pl.pallas_call(
+        waves_kernel,
+        out_shape=shape(10, own_rows, 128),
+        in_specs=[VMEM],
+        out_specs=VMEM,
+        compiler_params=PARAMS,
+    )(own)
+    left, right = neighbours(own, "slab")
     inject = pl.pallas_call(
         inject_kernel,
         out_shape=shape(STEPS, 128),
@@ -309,44 +330,25 @@
         out_specs=VMEM,
         compiler_params=LARGE,
     )(traces[0], rec_tile.reshape(1, -1), rec_col)
-    inject, store = lax.optimization_barrier((inject, model_store))
-    picked = pl.pallas_call(
-        pick_kernel,
-        out_shape=shape(shots, 7, COLS, 128, dtype=jnp.bfloat16),
-        in_specs=[SMEM, SMEM, VMEM],
-        out_specs=VMEM,
-        compiler_params=LARGE,
-    )(offsets, directory, store)
-    inject, picked = lax.optimization_barrier((added(added(inject, 1), 2), picked))
-    coef_own = lax.all_to_all(picked, "shot", split_axis=0, concat_axis=0, tiled=True)
-    inject, own = lax.optimization_barrier((added(inject, 4), own))
-    left, right = neighbours(own, "slab")
-    waves_in = pl.pallas_call(
-        waves_kernel,
-        out_shape=shape(10, all_rows, 128),
-        in_specs=[VMEM] * 3,
-        out_specs=VMEM,
-        compiler_params=PARAMS,
-        cost_estimate=pl.CostEstimate(flops=0, bytes_accessed=8 << 20, transcendentals=0),
-    )(left, own, right)
-
+    coef_own, inject = lax.optimization_barrier((coef_own, added(inject, 1)))
+    inject = added(added(inject, 2), 4)
     slab = lax.axis_index("slab").astype(jnp.int32).reshape(1)
     coef_left, coef_right = neighbours(coef_own, "slab")
     state, coef, image = pl.pallas_call(
         functools.partial(first_kernel, slabs),
         out_shape=(shape(10, own_rows, 128), shape(8, HELD * ROWS, 128), shape(own_rows, 128)),
-        in_specs=[SMEM, SMEM, ANY] + [VMEM] * 3,
+        in_specs=[SMEM, SMEM] + [ANY] * 3 + [VMEM] * 3,
         out_specs=(VMEM,) * 3,
-        scratch_shapes=scratch(1),
+        scratch_shapes=scratch(),
         compiler_params=PARAMS,
-    )(slab, inject, waves_in, coef_left, coef_own, coef_right)
+    )(slab, inject, left, own, right, coef_left, coef_own, coef_right)
     state_left, state_right = neighbours(state, "slab")
     waves_out, pieces = pl.pallas_call(
         second_kernel,
         out_shape=(shape(10, COLS, depth), shape(TILES, COLS, 128)),
         in_specs=[SMEM, SMEM] + [ANY] * 3 + [VMEM] * 2,
         out_specs=(VMEM,) * 2,
-        scratch_shapes=scratch(3),
+        scratch_shapes=scratch(),
         compiler_params=PARAMS,
     )(slab, inject, state_left, state, state_right, coef, image)
     pieces = lax.all_to_all(pieces, "shot", split_axis=0, concat_axis=0, tiled=True)

time: 145 us -> 138 us (0.952)
  Pallas kernels: 50.4 us -> 46.7 us
  blocking collectives: 26.7 us -> 24.9 us
  waiting for transfers between devices: 36.7 us -> 35 us
    ppermute x6, waiting for transfers between devices: 21.8 us -> 16.1 us  [neighbours(): return (lax.ppermute(block, axis, up), lax.ppermute(block, axis, down))]
    pallas_call x1, Pallas kernels: 5.24 us -> 1.3 us  [local(): pl.pallas_call(waves_kernel, out_shape=shape(10, own_rows, 128), in_specs...]
    all_to_all x1, waiting for transfers between devices: 7.55 us -> 10.2 us  [local(): lax.all_to_all(picked, 'shot', split_axis=0, concat_axis=0, tiled=True)]
    all_to_all x1, blocking collectives: 26.7 us -> 24.9 us  [local(): lax.all_to_all(pieces, 'shot', split_axis=0, concat_axis=0, tiled=True)]
  transfers between devices with their start and end apart: 10 -> 10, of which waited for: 7 -> 6; matrix products, arithmetic and copies ran while one was open for 0% -> 1% of each run, Pallas kernels for 5% -> 2%
where the time goes in v4:
time: 138 us
  Pallas kernels  46.7 us (34%)
  waiting for transfers between devices  35 us (25%)
  starting transfers between devices  29.8 us (22%)
  blocking collectives  24.9 us (18%)
    all_to_all x1, blocking collectives, local(): lax.all_to_all(pieces, 'shot', split_axis=0, concat_axis=0, tiled=True)  24.9 us
    pallas_call x1, Pallas kernels, local(): pl.pallas_call(functools.partial(first_kernel, slabs), out_shape=(shape(1...  21 us
    pallas_call x1, Pallas kernels, local(): pl.pallas_call(second_kernel, out_shape=(shape(10, COLS, depth), shape(TI...  19.4 us
    ppermute x6, waiting for transfers between devices, neighbours(): return (lax.ppermute(block, axis, up), lax.ppermute(block, axis, down))  16.1 us
    ppermute x6, starting transfers between devices, neighbours(): return (lax.ppermute(block, axis, up), lax.ppermute(block, axis, down))  14.3 us
    all_to_all x1, starting transfers between devices, local(): lax.all_to_all(picked, 'shot', split_axis=0, concat_axis=0, tiled=True)  13 us
    all_to_all x1, waiting for transfers between devices, local(): lax.all_to_all(picked, 'shot', split_axis=0, concat_axis=0, tiled=True)  10.2 us
    ppermute x3, waiting for transfers between devices, added(): return rows + lax.ppermute(rows, 'slab', partner)  8.68 us
  transfers between devices with their start and end apart: 10, of which 6 were waited for; matrix products, arithmetic and copies ran while one was open for 1% of the time, Pallas kernels for 2%

profile of v4, /device:TPU:32, one launch (start us, length us, event | category | flops | bytes accessed | tf_op | source)
XLA Modules:
  0.0 137.8 jit_solution(17316231950862875040)
XLA Ops:
  0.6 0.0 copy-start
  0.6 2.2 %shard_map.86 = bf16[32,7,8,128]{3,2,1,0:T(8,128)(2,1)} custom-call(s32[32]{0:T(128)} %offsets_ref.3, s32[8]{0:T(128)} %directory_ref.1, bf16[7,8,8,128]{3,2,1,0:T(8,128)(2,1)} %store_ref.1), custom_call_target="tpu_custom_call" | custom-call | tf_op jit(solution)/shard_map/pallas_call | solution.py:309
  2.8 13.0 %all-to-all-start = ((bf16[32,7,8,128]{3,2,1,0:T(8,128)(2,1)}), bf16[32,7,8,128]{3,2,1,0:T(8,128)(2,1)S(1)}, u32[]{:S(2)}, u32[]{:S(2)}) async-start(bf16[32,7,8,128]{3,2,1,0:T(8,128)(2,1)} %shard_map.86), calls=%async_computation | async-start | bytes 917504 | tf_op jit(solution)/shard_map/all_to_all | solution.py:317
  15.8 0.0 copy-done
  15.9 1.3 shard_map.88.own_ref
  17.2 2.1 %collective-permute-start.4 = (f32[10,256,128]{2,1,0:T(8,128)S(1)}, f32[10,256,128]{2,1,0:T(8,128)S(1)}, u32[]{:S(2)}, u32[]{:S(2)}) collective-permute-start(f32[10,256,128]{2,1,0:T(8,128)S(1)} %shard_map.88.own_ref), channel_id=1, source_target_pairs={{1,0},{2,1},{3,2},{4,3},{5,4},{6,5},{7,6},{9,8},{10,9},{11,10},{12... | collective-permute-start | bytes 3932168 | tf_op jit(solution)/shard_map/ppermute | solution.py:286
  19.2 2.3 %collective-permute-start.3 = (f32[10,256,128]{2,1,0:T(8,128)S(1)}, f32[10,256,128]{2,1,0:T(8,128)}, u32[]{:S(2)}, u32[]{:S(2)}) collective-permute-start(f32[10,256,128]{2,1,0:T(8,128)S(1)} %shard_map.88.own_ref), channel_id=1, source_target_pairs={{0,1},{1,2},{2,3},{3,4},{4,5},{5,6},{6,7},{8,9},{9,10},{10,11},{11... | collective-permute-start | bytes 3932168 | tf_op jit(solution)/shard_map/ppermute | solution.py:286
  21.5 1.5 %shard_map.87 = f32[16,128]{1,0:T(8,128)} custom-call(f32[16,128]{1,0:T(8,128)} %bitcast.6, s32[1,128]{1,0:T(1,128)} %bitcast.7, s32[1,128]{1,0:T(1,128)} %col_ref.1), custom_call_target="tpu_custom_call" | custom-call | tf_op jit(solution)/shard_map/pallas_call | solution.py:326
  23.0 0.8 collective-permute-start
  23.8 1.0 collective-permute-done
  24.9 0.7 add.9
  25.6 10.2 %all-to-all-done.coef_own_ref = bf16[32,7,8,128]{3,2,1,0:T(8,128)(2,1)S(1)} async-done(((bf16[32,7,8,128]{3,2,1,0:T(8,128)(2,1)}), bf16[32,7,8,128]{3,2,1,0:T(8,128)(2,1)S(1)}, u32[]{:S(2)}, u32[]{:S(2)}) %all-to-all-start) | async-done | bytes 458784 | tf_op jit(solution)/shard_map/all_to_all | solution.py:317
  35.7 1.9 %collective-permute-start.6 = (bf16[32,7,8,128]{3,2,1,0:T(8,128)(2,1)S(1)}, bf16[32,7,8,128]{3,2,1,0:T(8,128)(2,1)S(1)}, u32[]{:S(2)}, u32[]{:S(2)}) collective-permute-start(bf16[32,7,8,128]{3,2,1,0:T(8,128)(2,1)S(1)} %all-to-all-done.coef_own_ref), channel_id=1, source_target_pairs={{1,0},{2,1},{3,2},{4,3},{5,4},{6,5},{7,6},{9,8},{10,9},{11,10},{12... | collective-permute-start | bytes 1376264 | tf_op jit(solution)/shard_map/ppermute | solution.py:286
  37.6 2.4 %collective-permute-start.5 = (bf16[32,7,8,128]{3,2,1,0:T(8,128)(2,1)S(1)}, bf16[32,7,8,128]{3,2,1,0:T(8,128)(2,1)}, u32[]{:S(2)}, u32[]{:S(2)}) collective-permute-start(bf16[32,7,8,128]{3,2,1,0:T(8,128)(2,1)S(1)} %all-to-all-done.coef_own_ref), channel_id=1, source_target_pairs={{0,1},{1,2},{2,3},{3,4},{4,5},{5,6},{6,7},{8,9},{9,10},{10,11},{11... | collective-permute-start | bytes 1376264 | tf_op jit(solution)/shard_map/ppermute | solution.py:286
  40.1 0.1 collective-permute-start.1
  40.2 4.6 %collective-permute-done.1 = f32[16,128]{1,0:T(8,128)S(1)} collective-permute-done((f32[16,128]{1,0:T(8,128)S(1)}, f32[16,128]{1,0:T(8,128)S(1)}, u32[]{:S(2)}, u32[]{:S(2)}) %collective-permute-start.1) | collective-permute-done | bytes 8224 | tf_op jit(solution)/shard_map/ppermute | solution.py:307
  44.7 1.5 %collective-permute-start.2 = (f32[16,128]{1,0:T(8,128)S(1)}, f32[16,128]{1,0:T(8,128)S(1)}, u32[]{:S(2)}, u32[]{:S(2)}) collective-permute-start(f32[16,128]{1,0:T(8,128)S(1)} %add.10), channel_id=1, source_target_pairs={{0,4},{1,5},{2,6},{3,7},{4,0},{5,1},{6,2},{7,3},{8,12},{9,13},{10,... | collective-permute-start | bytes 24584 | tf_op jit(solution)/shard_map/ppermute | solution.py:307
  46.2 3.1 %collective-permute-done.2 = f32[16,128]{1,0:T(8,128)S(1)} collective-permute-done((f32[16,128]{1,0:T(8,128)S(1)}, f32[16,128]{1,0:T(8,128)S(1)}, u32[]{:S(2)}, u32[]{:S(2)}) %collective-permute-start.2) | collective-permute-done | bytes 8224 | tf_op jit(solution)/shard_map/ppermute | solution.py:307
  49.3 0.0 collective-permute-done.4.right_ref
  49.3 0.0 collective-permute-done.3.left_ref
  49.3 0.0 collective-permute-done.6.coef_right_ref
  49.3 0.0 collective-permute-done.5.coef_left_ref
  49.3 21.0 %shard_map.89 = (f32[10,256,128]{2,1,0:T(8,128)S(1)}, f32[8,1152,128]{2,1,0:T(8,128)S(1)}, f32[256,128]{1,0:T(8,128)S(1)}) custom-call(s32[1]{0:T(128)} %bitcast.slab_ref, f32[16,128]{1,0:T(8,128)S(1)} %add.11.inject_ref, f32[10,256,128]{2,1,0:T(8,128)} %collective-permute-done.3.left_ref, f32[10,256,128]{2,1,0:T(8,128)S(1)} %shard_map.88.own_ref, ...), custom_call_target="tpu_custom_call" | custom-call | tf_op jit(solution)/shard_map/pallas_call | solution.py:337
  70.3 2.9 %collective-permute-start.8 = (f32[10,256,128]{2,1,0:T(8,128)S(1)}, f32[10,256,128]{2,1,0:T(8,128)S(1)}, u32[]{:S(2)}, u32[]{:S(2)}) collective-permute-start(f32[10,256,128]{2,1,0:T(8,128)S(1)} %get-tuple-element.17.own_ref), channel_id=1, source_target_pairs={{1,0},{2,1},{3,2},{4,3},{5,4},{6,5},{7,6},{9,8},{10,9},{11,10},{12... | collective-permute-start | bytes 3932168 | tf_op jit(solution)/shard_map/ppermute | solution.py:286
  73.2 2.8 %collective-permute-start.7 = (f32[10,256,128]{2,1,0:T(8,128)S(1)}, f32[10,256,128]{2,1,0:T(8,128)S(1)}, u32[]{:S(2)}, u32[]{:S(2)}) collective-permute-start(f32[10,256,128]{2,1,0:T(8,128)S(1)} %get-tuple-element.17.own_ref), channel_id=1, source_target_pairs={{0,1},{1,2},{2,3},{3,4},{4,5},{5,6},{6,7},{8,9},{9,10},{10,11},{11... | collective-permute-start | bytes 3932168 | tf_op jit(solution)/shard_map/ppermute | solution.py:286
  76.0 12.3 %collective-permute-done.8.right_ref = f32[10,256,128]{2,1,0:T(8,128)S(1)} collective-permute-done((f32[10,256,128]{2,1,0:T(8,128)S(1)}, f32[10,256,128]{2,1,0:T(8,128)S(1)}, u32[]{:S(2)}, u32[]{:S(2)}) %collective-permute-start.8) | collective-permute-done | bytes 1310752 | tf_op jit(solution)/shard_map/ppermute | solution.py:286
  88.3 3.8 %collective-permute-done.7.left_ref = f32[10,256,128]{2,1,0:T(8,128)S(1)} collective-permute-done((f32[10,256,128]{2,1,0:T(8,128)S(1)}, f32[10,256,128]{2,1,0:T(8,128)S(1)}, u32[]{:S(2)}, u32[]{:S(2)}) %collective-permute-start.7) | collective-permute-done | bytes 1310752 | tf_op jit(solution)/shard_map/ppermute | solution.py:286
  92.1 0.0 copy-start.1
  92.2 19.4 %shard_map.90 = (f32[10,8,4096]{2,1,0:T(8,128)}, f32[32,8,128]{2,1,0:T(8,128)S(1)}) custom-call(s32[1]{0:T(128)} %bitcast.slab_ref, f32[16,128]{1,0:T(8,128)S(1)} %add.11.inject_ref, f32[10,256,128]{2,1,0:T(8,128)S(1)} %collective-permute-done.7.left_ref, f32[10,256,128]{2,1,0:T(8,128)S(1)} %get-tuple-element.17.own_ref, ...), custom_call_target="tpu_custom_call" | custom-call | tf_op jit(solution)/shard_map/pallas_call | solution.py:346
  111.6 24.9 %all_to_all.10.pieces_ref = f32[32,8,128]{2,1,0:T(8,128)S(1)} all-to-all(f32[32,8,128]{2,1,0:T(8,128)S(1)} %get-tuple-element.21), channel_id=1, replica_groups=mesh['shot'=32,'slab'=8] {'shot'}, dimensions={0} | all-to-all | bytes 262144 | tf_op jit(solution)/shard_map/all_to_all | solution.py:354
  136.4 0.0 copy-done.1
  136.4 1.4 shard_map.91
  (2 shorter events, 0.0 us)
Async XLA Ops:
  0.6 15.2 %copy-start = (f32[1,2,5,8,4096]{4,3,2,1,0:T(8,128)S(1)}, f32[1,2,5,8,4096]{4,3,2,1,0:T(8,128)}, u32[]{:S(2)}) copy-start(f32[1,2,5,8,4096]{4,3,2,1,0:T(8,128)} %param.7) | copy-start | bytes 3932164
  2.8 32.9 %all-to-all-start = ((bf16[32,7,8,128]{3,2,1,0:T(8,128)(2,1)}), bf16[32,7,8,128]{3,2,1,0:T(8,128)(2,1)S(1)}, u32[]{:S(2)}, u32[]{:S(2)}) async-start(bf16[32,7,8,128]{3,2,1,0:T(8,128)(2,1)} %shard_map.86), calls=%async_computation | async-start | bytes 917504 | tf_op jit(solution)/shard_map/all_to_all | solution.py:317
  17.2 32.1 %collective-permute-start.4 = (f32[10,256,128]{2,1,0:T(8,128)S(1)}, f32[10,256,128]{2,1,0:T(8,128)S(1)}, u32[]{:S(2)}, u32[]{:S(2)}) collective-permute-start(f32[10,256,128]{2,1,0:T(8,128)S(1)} %shard_map.88.own_ref), channel_id=1, source_target_pairs={{1,0},{2,1},{3,2},{4,3},{5,4},{6,5},{7,6},{9,8},{10,9},{11,10},{12... | collective-permute-start | bytes 3932168 | tf_op jit(solution)/shard_map/ppermute | solution.py:286
  19.2 30.0 %collective-permute-start.3 = (f32[10,256,128]{2,1,0:T(8,128)S(1)}, f32[10,256,128]{2,1,0:T(8,128)}, u32[]{:S(2)}, u32[]{:S(2)}) collective-permute-start(f32[10,256,128]{2,1,0:T(8,128)S(1)} %shard_map.88.own_ref), channel_id=1, source_target_pairs={{0,1},{1,2},{2,3},{3,4},{4,5},{5,6},{6,7},{8,9},{9,10},{10,11},{11... | collective-permute-start | bytes 3932168 | tf_op jit(solution)/shard_map/ppermute | solution.py:286
  23.0 1.8 %collective-permute-start = (f32[16,128]{1,0:T(8,128)}, f32[16,128]{1,0:T(8,128)S(1)}, u32[]{:S(2)}, u32[]{:S(2)}) collective-permute-start(f32[16,128]{1,0:T(8,128)} %shard_map.87), channel_id=1, source_target_pairs={{0,1},{1,0},{2,3},{3,2},{4,5},{5,4},{6,7},{7,6},{8,9},{9,8},{10,11... | collective-permute-start | bytes 24584 | tf_op jit(solution)/shard_map/ppermute | solution.py:307
  35.7 13.6 %collective-permute-start.6 = (bf16[32,7,8,128]{3,2,1,0:T(8,128)(2,1)S(1)}, bf16[32,7,8,128]{3,2,1,0:T(8,128)(2,1)S(1)}, u32[]{:S(2)}, u32[]{:S(2)}) collective-permute-start(bf16[32,7,8,128]{3,2,1,0:T(8,128)(2,1)S(1)} %all-to-all-done.coef_own_ref), channel_id=1, source_target_pairs={{1,0},{2,1},{3,2},{4,3},{5,4},{6,5},{7,6},{9,8},{10,9},{11,10},{12... | collective-permute-start | bytes 1376264 | tf_op jit(solution)/shard_map/ppermute | solution.py:286
  37.6 11.7 %collective-permute-start.5 = (bf16[32,7,8,128]{3,2,1,0:T(8,128)(2,1)S(1)}, bf16[32,7,8,128]{3,2,1,0:T(8,128)(2,1)}, u32[]{:S(2)}, u32[]{:S(2)}) collective-permute-start(bf16[32,7,8,128]{3,2,1,0:T(8,128)(2,1)S(1)} %all-to-all-done.coef_own_ref), channel_id=1, source_target_pairs={{0,1},{1,2},{2,3},{3,4},{4,5},{5,6},{6,7},{8,9},{9,10},{10,11},{11... | collective-permute-start | bytes 1376264 | tf_op jit(solution)/shard_map/ppermute | solution.py:286
  40.1 4.7 %collective-permute-start.1 = (f32[16,128]{1,0:T(8,128)S(1)}, f32[16,128]{1,0:T(8,128)S(1)}, u32[]{:S(2)}, u32[]{:S(2)}) collective-permute-start(f32[16,128]{1,0:T(8,128)S(1)} %add.9), channel_id=1, source_target_pairs={{0,2},{1,3},{2,0},{3,1},{4,6},{5,7},{6,4},{7,5},{8,10},{9,11},{10,... | collective-permute-start | bytes 24584 | tf_op jit(solution)/shard_map/ppermute | solution.py:307
  44.7 4.5 %collective-permute-start.2 = (f32[16,128]{1,0:T(8,128)S(1)}, f32[16,128]{1,0:T(8,128)S(1)}, u32[]{:S(2)}, u32[]{:S(2)}) collective-permute-start(f32[16,128]{1,0:T(8,128)S(1)} %add.10), channel_id=1, source_target_pairs={{0,4},{1,5},{2,6},{3,7},{4,0},{5,1},{6,2},{7,3},{8,12},{9,13},{10,... | collective-permute-start | bytes 24584 | tf_op jit(solution)/shard_map/ppermute | solution.py:307
  70.3 18.0 %collective-permute-start.8 = (f32[10,256,128]{2,1,0:T(8,128)S(1)}, f32[10,256,128]{2,1,0:T(8,128)S(1)}, u32[]{:S(2)}, u32[]{:S(2)}) collective-permute-start(f32[10,256,128]{2,1,0:T(8,128)S(1)} %get-tuple-element.17.own_ref), channel_id=1, source_target_pairs={{1,0},{2,1},{3,2},{4,3},{5,4},{6,5},{7,6},{9,8},{10,9},{11,10},{12... | collective-permute-start | bytes 3932168 | tf_op jit(solution)/shard_map/ppermute | solution.py:286
  73.2 18.9 %collective-permute-start.7 = (f32[10,256,128]{2,1,0:T(8,128)S(1)}, f32[10,256,128]{2,1,0:T(8,128)S(1)}, u32[]{:S(2)}, u32[]{:S(2)}) collective-permute-start(f32[10,256,128]{2,1,0:T(8,128)S(1)} %get-tuple-element.17.own_ref), channel_id=1, source_target_pairs={{0,1},{1,2},{2,3},{3,4},{4,5},{5,6},{6,7},{8,9},{9,10},{10,11},{11... | collective-permute-start | bytes 3932168 | tf_op jit(solution)/shard_map/ppermute | solution.py:286
  92.1 44.3 %copy-start.1 = (s32[32]{0:T(128)S(1)}, s32[32]{0:T(128)}, u32[]{:S(2)}) copy-start(s32[32]{0:T(128)} %offsets_ref.3) | copy-start | bytes 388

commit v5 on v4

--- a/solution.py
+++ b/solution.py
@@ -129,19 +129,25 @@
                 pressure.append(new[0] + new[1])
             image[at(base, k), :] += pressure[0] * pressure[1]
 
+    def base_of(a):
+        return pl.multiple_of((a + PAD) * ROWS, ROWS)
+
     def one_step(step, _):
-        start = pl.multiple_of((step + PAD) * ROWS, ROWS)
+        start = base_of(step)
         gradients(start, (0, 1))
+        velocities(step, start, (0, 1), step)
+        gradients(start, (2, 3))
 
         def turn(j, _):
             a = step + 2 * j
-            base = pl.multiple_of((a + PAD) * ROWS, ROWS)
+            base = base_of(a)
             velocities(a, base, (0, 1), step)
             gradients(base, (2, 3))
             stresses(base, (-3, -2))
             return 0
 
-        lax.fori_loop(0, PHASE + 6 - step, turn, 0)
+        lax.fori_loop(1, PHASE + 5 - step, turn, 0)
+        stresses(base_of(WIDE + 2 - step), (-3,))
         return 0
 
     lax.fori_loop(1, PHASE + 1, one_step, 0)
@@ -239,7 +245,7 @@
     right_ref,
     coef,
     image_in,
-    waves_out,
+    state_out,
     image_out,
     state,
     image,
@@ -251,11 +257,18 @@
     for copy in copies:
         copy.wait()
     advance(state, coef, image, slab_ref[0], inject_ref, PHASE)
+    for q in range(10):
+        state_out[q] = state[q, window(1), :]
     for tile in range(TILES):
         rows = pl.ds((PAD + COLS) * ROWS + row_of(tile), COLS, stride=ROWS)
+        image_out[tile] = image[rows, :] * (1.0 / STEPS)
+
+
+def final_kernel(state_ref, waves_out):
+    for tile in range(TILES):
+        rows = pl.ds(row_of(tile), COLS, stride=ROWS)
         for q in range(10):
-            waves_out[q, :, pl.ds(tile * 128, 128)] = state[q, rows, :]
-        image_out[tile] = image[rows, :] * (1.0 / STEPS)
+            waves_out[q, :, pl.ds(tile * 128, 128)] = state_ref[q, rows, :]
 
 
 def stack_kernel(offsets_ref, pieces_ref, out_ref):
@@ -302,9 +315,8 @@
     own = waves.reshape(10, COLS, depth)
     own_rows = COLS * ROWS
 
-    def added(rows, bit):
-        partner = [(i, i ^ bit) for i in range(slabs)]
-        return rows + lax.ppermute(rows, "slab", partner)
+    def exchanged(rows, bits):
+        return lax.ppermute(rows, "slab", [(i, i ^ bits) for i in range(slabs)])
 
     picked = pl.pallas_call(
         pick_kernel,
@@ -330,8 +342,9 @@
         out_specs=VMEM,
         compiler_params=LARGE,
     )(traces[0], rec_tile.reshape(1, -1), rec_col)
-    coef_own, inject = lax.optimization_barrier((coef_own, added(inject, 1)))
-    inject = added(added(inject, 2), 4)
+    coef_own, inject = lax.optimization_barrier((coef_own, inject + exchanged(inject, 1)))
+    left, right, inject = lax.optimization_barrier((left, right, inject))
+    inject = inject + sum(exchanged(inject, bits) for bits in range(2, slabs, 2))
     slab = lax.axis_index("slab").astype(jnp.int32).reshape(1)
     coef_left, coef_right = neighbours(coef_own, "slab")
     state, coef, image = pl.pallas_call(
@@ -343,15 +356,22 @@
         compiler_params=PARAMS,
     )(slab, inject, left, own, right, coef_left, coef_own, coef_right)
     state_left, state_right = neighbours(state, "slab")
-    waves_out, pieces = pl.pallas_call(
+    state, pieces = pl.pallas_call(
         second_kernel,
-        out_shape=(shape(10, COLS, depth), shape(TILES, COLS, 128)),
+        out_shape=(shape(10, own_rows, 128), shape(TILES, COLS, 128)),
         in_specs=[SMEM, SMEM] + [ANY] * 3 + [VMEM] * 2,
         out_specs=(VMEM,) * 2,
         scratch_shapes=scratch(),
         compiler_params=PARAMS,
     )(slab, inject, state_left, state, state_right, coef, image)
     pieces = lax.all_to_all(pieces, "shot", split_axis=0, concat_axis=0, tiled=True)
+    waves_out = pl.pallas_call(
+        final_kernel,
+        out_shape=shape(10, COLS, depth),
+        in_specs=[VMEM],
+        out_specs=VMEM,
+        compiler_params=PARAMS,
+    )(state)
     stacked = pl.pallas_call(
         stack_kernel,
         out_shape=shape(model_store.shape[1], COLS, 128),

time: 138 us -> 133 us (0.964)
  blocking collectives: 24.9 us -> 0 us
  waiting for transfers between devices: 35 us -> 46.2 us
  starting transfers between devices: 29.8 us -> 39.3 us
  Pallas kernels: 46.7 us -> 43.1 us
    all_to_all x1 -> x0, blocking collectives: 24.9 us -> none  [local(): lax.all_to_all(pieces, 'shot', split_axis=0, concat_axis=0, tiled=True)]
    all_to_all x0 -> x1, waiting for transfers between devices: none -> 10.5 us  [local(): lax.all_to_all(pieces, 'shot', split_axis=0, concat_axis=0, tiled=True)]
    all_to_all x0 -> x1, starting transfers between devices: none -> 4.87 us  [local(): lax.all_to_all(pieces, 'shot', split_axis=0, concat_axis=0, tiled=True)]
    all_to_all x1, waiting for transfers between devices: 10.2 us -> 14.5 us  [local(): lax.all_to_all(picked, 'shot', split_axis=0, concat_axis=0, tiled=True)]
    ppermute x3 -> x4, waiting for transfers between devices: 8.68 us -> 4.77 us  [exchanged(): return lax.ppermute(rows, 'slab', [(i, i ^ bits) for i in range(slabs)])]
    ppermute x6, starting transfers between devices: 14.3 us -> 16.9 us  [neighbours(): return (lax.ppermute(block, axis, up), lax.ppermute(block, axis, down))]
    pallas_call x1, Pallas kernels: 21 us -> 18.8 us  [local(): pl.pallas_call(functools.partial(first_kernel, slabs), out_shape=(shape(1...]
    ppermute x3 -> x4, starting transfers between devices: 2.36 us -> 4.49 us  [exchanged(): return lax.ppermute(rows, 'slab', [(i, i ^ bits) for i in range(slabs)])]
  transfers between devices with their start and end apart: 10 -> 12, of which waited for: 6 -> 8; matrix products, arithmetic and copies ran while one was open for 1% -> 1% of each run, Pallas kernels for 2% -> 3%
where the time goes in v5:
time: 133 us; the launch traced here: 132 us
  waiting for transfers between devices  46.2 us (35%)
  Pallas kernels  43.1 us (32%)
  starting transfers between devices  39.3 us (30%)
  other arithmetic  1.42 us (1%)
    pallas_call x1, Pallas kernels, local(): pl.pallas_call(functools.partial(first_kernel, slabs), out_shape=(shape(1...  18.8 us
    ppermute x6, starting transfers between devices, neighbours(): return (lax.ppermute(block, axis, up), lax.ppermute(block, axis, down))  16.9 us
    ppermute x6, waiting for transfers between devices, neighbours(): return (lax.ppermute(block, axis, up), lax.ppermute(block, axis, down))  16.4 us
    pallas_call x1, Pallas kernels, local(): pl.pallas_call(second_kernel, out_shape=(shape(10, own_rows, 128), shape(...  16.1 us
    all_to_all x1, waiting for transfers between devices, local(): lax.all_to_all(picked, 'shot', split_axis=0, concat_axis=0, tiled=True)  14.5 us
    all_to_all x1, starting transfers between devices, local(): lax.all_to_all(picked, 'shot', split_axis=0, concat_axis=0, tiled=True)  13.1 us
    all_to_all x1, waiting for transfers between devices, local(): lax.all_to_all(pieces, 'shot', split_axis=0, concat_axis=0, tiled=True)  10.5 us
    all_to_all x1, starting transfers between devices, local(): lax.all_to_all(pieces, 'shot', split_axis=0, concat_axis=0, tiled=True)  4.87 us
  transfers between devices with their start and end apart: 12, of which 8 were waited for; matrix products, arithmetic and copies ran while one was open for 1% of the time, Pallas kernels for 3%

profile of v5, /device:TPU:32, one launch (start us, length us, event | category | flops | bytes accessed | tf_op | source)
XLA Modules:
  0.0 132.1 jit_solution(14444477168275813823)
XLA Ops:
  0.6 2.0 %shard_map.86 = bf16[32,7,8,128]{3,2,1,0:T(8,128)(2,1)} custom-call(s32[32]{0:T(128)} %offsets_ref.3, s32[8]{0:T(128)} %directory_ref.1, bf16[7,8,8,128]{3,2,1,0:T(8,128)(2,1)} %store_ref.1), custom_call_target="tpu_custom_call" | custom-call | tf_op jit(solution)/shard_map/pallas_call | solution.py:321
  2.7 1.3 copy-done
  4.0 1.3 shard_map.87.own_ref
  5.3 1.9 %collective-permute-start.1 = (f32[10,256,128]{2,1,0:T(8,128)S(1)}, f32[10,256,128]{2,1,0:T(8,128)S(1)}, u32[]{:S(2)}, u32[]{:S(2)}) collective-permute-start(f32[10,256,128]{2,1,0:T(8,128)S(1)} %shard_map.87.own_ref), channel_id=1, source_target_pairs={{1,0},{2,1},{3,2},{4,3},{5,4},{6,5},{7,6},{9,8},{10,9},{11,10},{12... | collective-permute-start | bytes 3932168 | tf_op jit(solution)/shard_map/ppermute | solution.py:299
  7.2 2.4 %collective-permute-start = (f32[10,256,128]{2,1,0:T(8,128)S(1)}, f32[10,256,128]{2,1,0:T(8,128)}, u32[]{:S(2)}, u32[]{:S(2)}) collective-permute-start(f32[10,256,128]{2,1,0:T(8,128)S(1)} %shard_map.87.own_ref), channel_id=1, source_target_pairs={{0,1},{1,2},{2,3},{3,4},{4,5},{5,6},{6,7},{8,9},{9,10},{10,11},{11... | collective-permute-start | bytes 3932168 | tf_op jit(solution)/shard_map/ppermute | solution.py:299
  9.6 13.1 %all-to-all-start = ((bf16[32,7,8,128]{3,2,1,0:T(8,128)(2,1)}), bf16[32,7,8,128]{3,2,1,0:T(8,128)(2,1)S(1)}, u32[]{:S(2)}, u32[]{:S(2)}) async-start(bf16[32,7,8,128]{3,2,1,0:T(8,128)(2,1)} %shard_map.86), calls=%async_computation | async-start | bytes 917504 | tf_op jit(solution)/shard_map/all_to_all | solution.py:329
  22.7 1.5 %shard_map.88 = f32[16,128]{1,0:T(8,128)} custom-call(f32[16,128]{1,0:T(8,128)} %bitcast.7, s32[1,128]{1,0:T(1,128)} %bitcast.8, s32[1,128]{1,0:T(1,128)} %col_ref.1), custom_call_target="tpu_custom_call" | custom-call | tf_op jit(solution)/shard_map/pallas_call | solution.py:338
  24.2 0.8 collective-permute-start.2
  25.0 1.0 collective-permute-done.2
  26.1 0.7 add.12
  26.8 14.5 %all-to-all-done.coef_own_ref = bf16[32,7,8,128]{3,2,1,0:T(8,128)(2,1)S(1)} async-done(((bf16[32,7,8,128]{3,2,1,0:T(8,128)(2,1)}), bf16[32,7,8,128]{3,2,1,0:T(8,128)(2,1)S(1)}, u32[]{:S(2)}, u32[]{:S(2)}) %all-to-all-start) | async-done | bytes 458784 | tf_op jit(solution)/shard_map/all_to_all | solution.py:329
  41.3 6.0 %collective-permute-start.7 = (bf16[32,7,8,128]{3,2,1,0:T(8,128)(2,1)S(1)}, bf16[32,7,8,128]{3,2,1,0:T(8,128)(2,1)S(1)}, u32[]{:S(2)}, u32[]{:S(2)}) collective-permute-start(bf16[32,7,8,128]{3,2,1,0:T(8,128)(2,1)S(1)} %all-to-all-done.coef_own_ref), channel_id=1, source_target_pairs={{1,0},{2,1},{3,2},{4,3},{5,4},{6,5},{7,6},{9,8},{10,9},{11,10},{12... | collective-permute-start | bytes 1376264 | tf_op jit(solution)/shard_map/ppermute | solution.py:299
  47.3 1.9 %collective-permute-start.6 = (bf16[32,7,8,128]{3,2,1,0:T(8,128)(2,1)S(1)}, bf16[32,7,8,128]{3,2,1,0:T(8,128)(2,1)}, u32[]{:S(2)}, u32[]{:S(2)}) collective-permute-start(bf16[32,7,8,128]{3,2,1,0:T(8,128)(2,1)S(1)} %all-to-all-done.coef_own_ref), channel_id=1, source_target_pairs={{0,1},{1,2},{2,3},{3,4},{4,5},{5,6},{6,7},{8,9},{9,10},{10,11},{11... | collective-permute-start | bytes 1376264 | tf_op jit(solution)/shard_map/ppermute | solution.py:299
  49.2 1.2 collective-permute-start.5
  50.4 2.4 %collective-permute-start.4 = (f32[16,128]{1,0:T(8,128)S(1)}, f32[16,128]{1,0:T(8,128)}, u32[]{:S(2)}, u32[]{:S(2)}) collective-permute-start(f32[16,128]{1,0:T(8,128)S(1)} %add.12), channel_id=1, source_target_pairs={{0,4},{1,5},{2,6},{3,7},{4,0},{5,1},{6,2},{7,3},{8,12},{9,13},{10,... | collective-permute-start | bytes 24584 | tf_op jit(solution)/shard_map/ppermute | solution.py:319
  52.7 0.2 collective-permute-start.3
  52.9 0.0 collective-permute-done.5
  53.0 3.4 %collective-permute-done.4 = f32[16,128]{1,0:T(8,128)} collective-permute-done((f32[16,128]{1,0:T(8,128)S(1)}, f32[16,128]{1,0:T(8,128)}, u32[]{:S(2)}, u32[]{:S(2)}) %collective-permute-start.4) | collective-permute-done | bytes 8224 | tf_op jit(solution)/shard_map/ppermute | solution.py:319
  56.4 0.3 collective-permute-done.3
  56.7 0.7 add_add_fusion.inject_ref
  57.4 0.1 collective-permute-done.6.coef_left_ref
  57.4 18.8 %shard_map.89 = (f32[10,256,128]{2,1,0:T(8,128)S(1)}, f32[8,1152,128]{2,1,0:T(8,128)S(1)}, f32[256,128]{1,0:T(8,128)S(1)}) custom-call(s32[1]{0:T(128)} %bitcast.slab_ref, f32[16,128]{1,0:T(8,128)S(1)} %add_add_fusion.inject_ref, f32[10,256,128]{2,1,0:T(8,128)} %collective-permute-done.left_ref, f32[10,256,128]{2,1,0:T(8,128)S(1)} %shard_map.87.own_ref, ...), custom_call_target="tpu_custom_call" | custom-call | tf_op jit(solution)/shard_map/pallas_call | solution.py:350
  76.3 2.1 %collective-permute-start.9 = (f32[10,256,128]{2,1,0:T(8,128)S(1)}, f32[10,256,128]{2,1,0:T(8,128)S(1)}, u32[]{:S(2)}, u32[]{:S(2)}) collective-permute-start(f32[10,256,128]{2,1,0:T(8,128)S(1)} %get-tuple-element.23.own_ref), channel_id=1, source_target_pairs={{1,0},{2,1},{3,2},{4,3},{5,4},{6,5},{7,6},{9,8},{10,9},{11,10},{12... | collective-permute-start | bytes 3932168 | tf_op jit(solution)/shard_map/ppermute | solution.py:299
  78.4 2.6 %collective-permute-start.8 = (f32[10,256,128]{2,1,0:T(8,128)S(1)}, f32[10,256,128]{2,1,0:T(8,128)S(1)}, u32[]{:S(2)}, u32[]{:S(2)}) collective-permute-start(f32[10,256,128]{2,1,0:T(8,128)S(1)} %get-tuple-element.23.own_ref), channel_id=1, source_target_pairs={{0,1},{1,2},{2,3},{3,4},{4,5},{5,6},{6,7},{8,9},{9,10},{10,11},{11... | collective-permute-start | bytes 3932168 | tf_op jit(solution)/shard_map/ppermute | solution.py:299
  81.0 12.5 %collective-permute-done.9.right_ref = f32[10,256,128]{2,1,0:T(8,128)S(1)} collective-permute-done((f32[10,256,128]{2,1,0:T(8,128)S(1)}, f32[10,256,128]{2,1,0:T(8,128)S(1)}, u32[]{:S(2)}, u32[]{:S(2)}) %collective-permute-start.9) | collective-permute-done | bytes 1310752 | tf_op jit(solution)/shard_map/ppermute | solution.py:299
  93.5 3.8 %collective-permute-done.8.left_ref = f32[10,256,128]{2,1,0:T(8,128)S(1)} collective-permute-done((f32[10,256,128]{2,1,0:T(8,128)S(1)}, f32[10,256,128]{2,1,0:T(8,128)S(1)}, u32[]{:S(2)}, u32[]{:S(2)}) %collective-permute-start.8) | collective-permute-done | bytes 1310752 | tf_op jit(solution)/shard_map/ppermute | solution.py:299
  97.3 16.1 %shard_map.90 = (f32[10,256,128]{2,1,0:T(8,128)S(1)}, f32[32,8,128]{2,1,0:T(8,128)}) custom-call(s32[1]{0:T(128)} %bitcast.slab_ref, f32[16,128]{1,0:T(8,128)S(1)} %add_add_fusion.inject_ref, f32[10,256,128]{2,1,0:T(8,128)S(1)} %collective-permute-done.8.left_ref, f32[10,256,128]{2,1,0:T(8,128)S(1)} %get-tuple-element.23.own_ref, ...), custom_call_target="tpu_custom_call" | custom-call | tf_op jit(solution)/shard_map/pallas_call | solution.py:359
  113.4 4.9 %all-to-all-start.1 = ((f32[32,8,128]{2,1,0:T(8,128)}), f32[32,8,128]{2,1,0:T(8,128)S(1)}, u32[]{:S(2)}, u32[]{:S(2)}) async-start(f32[32,8,128]{2,1,0:T(8,128)} %get-tuple-element.27), calls=%async_computation.1 | async-start | bytes 262144 | tf_op jit(solution)/shard_map/all_to_all | solution.py:367
  118.3 0.0 copy-start.1
  118.3 1.9 %shard_map.91 = f32[10,8,4096]{2,1,0:T(8,128)} custom-call(f32[10,256,128]{2,1,0:T(8,128)S(1)} %get-tuple-element.26.state_ref), custom_call_target="tpu_custom_call" | custom-call | tf_op jit(solution)/shard_map/pallas_call | solution.py:368
  120.2 10.5 %all-to-all-done.1.pieces_ref = f32[32,8,128]{2,1,0:T(8,128)S(1)} async-done(((f32[32,8,128]{2,1,0:T(8,128)}), f32[32,8,128]{2,1,0:T(8,128)S(1)}, u32[]{:S(2)}, u32[]{:S(2)}) %all-to-all-start.1) | async-done | bytes 131104 | tf_op jit(solution)/shard_map/all_to_all | solution.py:367
  130.7 1.4 %shard_map.92 = f32[8,8,128]{2,1,0:T(8,128)} custom-call(s32[32]{0:T(128)S(1)} %copy-done.1, f32[32,8,128]{2,1,0:T(8,128)S(1)} %all-to-all-done.1.pieces_ref), custom_call_target="tpu_custom_call" | custom-call | tf_op jit(solution)/shard_map/pallas_call | solution.py:375
  (5 shorter events, 0.0 us)
Async XLA Ops:
  2.7 1.3 copy-start
  5.3 43.9 %collective-permute-start.1 = (f32[10,256,128]{2,1,0:T(8,128)S(1)}, f32[10,256,128]{2,1,0:T(8,128)S(1)}, u32[]{:S(2)}, u32[]{:S(2)}) collective-permute-start(f32[10,256,128]{2,1,0:T(8,128)S(1)} %shard_map.87.own_ref), channel_id=1, source_target_pairs={{1,0},{2,1},{3,2},{4,3},{5,4},{6,5},{7,6},{9,8},{10,9},{11,10},{12... | collective-permute-start | bytes 3932168 | tf_op jit(solution)/shard_map/ppermute | solution.py:299
  7.2 42.0 %collective-permute-start = (f32[10,256,128]{2,1,0:T(8,128)S(1)}, f32[10,256,128]{2,1,0:T(8,128)}, u32[]{:S(2)}, u32[]{:S(2)}) collective-permute-start(f32[10,256,128]{2,1,0:T(8,128)S(1)} %shard_map.87.own_ref), channel_id=1, source_target_pairs={{0,1},{1,2},{2,3},{3,4},{4,5},{5,6},{6,7},{8,9},{9,10},{10,11},{11... | collective-permute-start | bytes 3932168 | tf_op jit(solution)/shard_map/ppermute | solution.py:299
  9.6 31.6 %all-to-all-start = ((bf16[32,7,8,128]{3,2,1,0:T(8,128)(2,1)}), bf16[32,7,8,128]{3,2,1,0:T(8,128)(2,1)S(1)}, u32[]{:S(2)}, u32[]{:S(2)}) async-start(bf16[32,7,8,128]{3,2,1,0:T(8,128)(2,1)} %shard_map.86), calls=%async_computation | async-start | bytes 917504 | tf_op jit(solution)/shard_map/all_to_all | solution.py:329
  24.2 1.8 %collective-permute-start.2 = (f32[16,128]{1,0:T(8,128)}, f32[16,128]{1,0:T(8,128)S(1)}, u32[]{:S(2)}, u32[]{:S(2)}) collective-permute-start(f32[16,128]{1,0:T(8,128)} %shard_map.88), channel_id=1, source_target_pairs={{0,1},{1,0},{2,3},{3,2},{4,5},{5,4},{6,7},{7,6},{8,9},{9,8},{10,11... | collective-permute-start | bytes 24584 | tf_op jit(solution)/shard_map/ppermute | solution.py:319
  41.3 16.1 %collective-permute-start.7 = (bf16[32,7,8,128]{3,2,1,0:T(8,128)(2,1)S(1)}, bf16[32,7,8,128]{3,2,1,0:T(8,128)(2,1)S(1)}, u32[]{:S(2)}, u32[]{:S(2)}) collective-permute-start(bf16[32,7,8,128]{3,2,1,0:T(8,128)(2,1)S(1)} %all-to-all-done.coef_own_ref), channel_id=1, source_target_pairs={{1,0},{2,1},{3,2},{4,3},{5,4},{6,5},{7,6},{9,8},{10,9},{11,10},{12... | collective-permute-start | bytes 1376264 | tf_op jit(solution)/shard_map/ppermute | solution.py:299
  47.3 10.2 %collective-permute-start.6 = (bf16[32,7,8,128]{3,2,1,0:T(8,128)(2,1)S(1)}, bf16[32,7,8,128]{3,2,1,0:T(8,128)(2,1)}, u32[]{:S(2)}, u32[]{:S(2)}) collective-permute-start(bf16[32,7,8,128]{3,2,1,0:T(8,128)(2,1)S(1)} %all-to-all-done.coef_own_ref), channel_id=1, source_target_pairs={{0,1},{1,2},{2,3},{3,4},{4,5},{5,6},{6,7},{8,9},{9,10},{10,11},{11... | collective-permute-start | bytes 1376264 | tf_op jit(solution)/shard_map/ppermute | solution.py:299
  49.2 3.7 %collective-permute-start.5 = (f32[16,128]{1,0:T(8,128)S(1)}, f32[16,128]{1,0:T(8,128)S(1)}, u32[]{:S(2)}, u32[]{:S(2)}) collective-permute-start(f32[16,128]{1,0:T(8,128)S(1)} %add.12), channel_id=1, source_target_pairs={{0,6},{1,7},{2,4},{3,5},{4,2},{5,3},{6,0},{7,1},{8,14},{9,15},{10,... | collective-permute-start | bytes 24584 | tf_op jit(solution)/shard_map/ppermute | solution.py:319
  50.4 6.0 %collective-permute-start.4 = (f32[16,128]{1,0:T(8,128)S(1)}, f32[16,128]{1,0:T(8,128)}, u32[]{:S(2)}, u32[]{:S(2)}) collective-permute-start(f32[16,128]{1,0:T(8,128)S(1)} %add.12), channel_id=1, source_target_pairs={{0,4},{1,5},{2,6},{3,7},{4,0},{5,1},{6,2},{7,3},{8,12},{9,13},{10,... | collective-permute-start | bytes 24584 | tf_op jit(solution)/shard_map/ppermute | solution.py:319
  52.7 3.9 %collective-permute-start.3 = (f32[16,128]{1,0:T(8,128)S(1)}, f32[16,128]{1,0:T(8,128)}, u32[]{:S(2)}, u32[]{:S(2)}) collective-permute-start(f32[16,128]{1,0:T(8,128)S(1)} %add.12), channel_id=1, source_target_pairs={{0,2},{1,3},{2,0},{3,1},{4,6},{5,7},{6,4},{7,5},{8,10},{9,11},{10,... | collective-permute-start | bytes 24584 | tf_op jit(solution)/shard_map/ppermute | solution.py:319
  76.3 17.2 %collective-permute-start.9 = (f32[10,256,128]{2,1,0:T(8,128)S(1)}, f32[10,256,128]{2,1,0:T(8,128)S(1)}, u32[]{:S(2)}, u32[]{:S(2)}) collective-permute-start(f32[10,256,128]{2,1,0:T(8,128)S(1)} %get-tuple-element.23.own_ref), channel_id=1, source_target_pairs={{1,0},{2,1},{3,2},{4,3},{5,4},{6,5},{7,6},{9,8},{10,9},{11,10},{12... | collective-permute-start | bytes 3932168 | tf_op jit(solution)/shard_map/ppermute | solution.py:299
  78.4 18.9 %collective-permute-start.8 = (f32[10,256,128]{2,1,0:T(8,128)S(1)}, f32[10,256,128]{2,1,0:T(8,128)S(1)}, u32[]{:S(2)}, u32[]{:S(2)}) collective-permute-start(f32[10,256,128]{2,1,0:T(8,128)S(1)} %get-tuple-element.23.own_ref), channel_id=1, source_target_pairs={{0,1},{1,2},{2,3},{3,4},{4,5},{5,6},{6,7},{8,9},{9,10},{10,11},{11... | collective-permute-start | bytes 3932168 | tf_op jit(solution)/shard_map/ppermute | solution.py:299
  113.4 17.3 %all-to-all-start.1 = ((f32[32,8,128]{2,1,0:T(8,128)}), f32[32,8,128]{2,1,0:T(8,128)S(1)}, u32[]{:S(2)}, u32[]{:S(2)}) async-start(f32[32,8,128]{2,1,0:T(8,128)} %get-tuple-element.27), calls=%async_computation.1 | async-start | bytes 262144 | tf_op jit(solution)/shard_map/all_to_all | solution.py:367
  118.3 12.4 %copy-start.1 = (s32[32]{0:T(128)S(1)}, s32[32]{0:T(128)}, u32[]{:S(2)}) copy-start(s32[32]{0:T(128)} %offsets_ref.3) | copy-start | bytes 388

commit v6 on v5

--- a/solution.py
+++ b/solution.py
@@ -343,8 +343,10 @@
         compiler_params=LARGE,
     )(traces[0], rec_tile.reshape(1, -1), rec_col)
     coef_own, inject = lax.optimization_barrier((coef_own, inject + exchanged(inject, 1)))
-    left, right, inject = lax.optimization_barrier((left, right, inject))
-    inject = inject + sum(exchanged(inject, bits) for bits in range(2, slabs, 2))
+    bit = 2
+    while bit < slabs:
+        inject = inject + exchanged(inject, bit)
+        bit *= 2
     slab = lax.axis_index("slab").astype(jnp.int32).reshape(1)
     coef_left, coef_right = neighbours(coef_own, "slab")
     state, coef, image = pl.pallas_call(

time: 133 us -> 133 us (level)
  starting transfers between devices: 39.3 us -> 41.7 us
    all_to_all x1, starting transfers between devices: 4.87 us -> 11.9 us  [local(): lax.all_to_all(pieces, 'shot', split_axis=0, concat_axis=0, tiled=True)]
    all_to_all x1, waiting for transfers between devices: 14.5 us -> 10.2 us  [local(): lax.all_to_all(picked, 'shot', split_axis=0, concat_axis=0, tiled=True)]
    ppermute x4 -> x3, waiting for transfers between devices: 4.77 us -> 8.68 us  [exchanged(): return lax.ppermute(rows, 'slab', [(i, i ^ bits) for i in range(slabs)])]
    ppermute x6, starting transfers between devices: 16.9 us -> 14.3 us  [neighbours(): return (lax.ppermute(block, axis, up), lax.ppermute(block, axis, down))]
    ppermute x4 -> x3, starting transfers between devices: 4.49 us -> 2.36 us  [exchanged(): return lax.ppermute(rows, 'slab', [(i, i ^ bits) for i in range(slabs)])]
  transfers between devices with their start and end apart: 12 -> 11, of which waited for: 8 -> 7; matrix products, arithmetic and copies ran while one was open for 1% -> 1% of each run, Pallas kernels for 3% -> 4%
where the time goes in v6:
time: 133 us
  waiting for transfers between devices  46.2 us (35%)
  Pallas kernels  43.2 us (32%)
  starting transfers between devices  41.7 us (31%)
    pallas_call x1, Pallas kernels, local(): pl.pallas_call(functools.partial(first_kernel, slabs), out_shape=(shape(1...  18.8 us
    ppermute x6, waiting for transfers between devices, neighbours(): return (lax.ppermute(block, axis, up), lax.ppermute(block, axis, down))  16.1 us
    pallas_call x1, Pallas kernels, local(): pl.pallas_call(second_kernel, out_shape=(shape(10, own_rows, 128), shape(...  16.1 us
    ppermute x6, starting transfers between devices, neighbours(): return (lax.ppermute(block, axis, up), lax.ppermute(block, axis, down))  14.3 us
    all_to_all x1, starting transfers between devices, local(): lax.all_to_all(picked, 'shot', split_axis=0, concat_axis=0, tiled=True)  13 us
    all_to_all x1, starting transfers between devices, local(): lax.all_to_all(pieces, 'shot', split_axis=0, concat_axis=0, tiled=True)  11.9 us
    all_to_all x1, waiting for transfers between devices, local(): lax.all_to_all(pieces, 'shot', split_axis=0, concat_axis=0, tiled=True)  11.2 us
    all_to_all x1, waiting for transfers between devices, local(): lax.all_to_all(picked, 'shot', split_axis=0, concat_axis=0, tiled=True)  10.2 us
  transfers between devices with their start and end apart: 11, of which 7 were waited for; matrix products, arithmetic and copies ran while one was open for 1% of the time, Pallas kernels for 4%

profile of v6, /device:TPU:32, one launch (start us, length us, event | category | flops | bytes accessed | tf_op | source)
XLA Modules:
  0.0 132.6 jit_solution(1349024223297901402)
XLA Ops:
  0.6 2.2 %shard_map.86 = bf16[32,7,8,128]{3,2,1,0:T(8,128)(2,1)} custom-call(s32[32]{0:T(128)} %offsets_ref.3, s32[8]{0:T(128)} %directory_ref.1, bf16[7,8,8,128]{3,2,1,0:T(8,128)(2,1)} %store_ref.1), custom_call_target="tpu_custom_call" | custom-call | tf_op jit(solution)/shard_map/pallas_call | solution.py:321
  2.8 13.0 %all-to-all-start = ((bf16[32,7,8,128]{3,2,1,0:T(8,128)(2,1)}), bf16[32,7,8,128]{3,2,1,0:T(8,128)(2,1)S(1)}, u32[]{:S(2)}, u32[]{:S(2)}) async-start(bf16[32,7,8,128]{3,2,1,0:T(8,128)(2,1)} %shard_map.86), calls=%async_computation | async-start | bytes 917504 | tf_op jit(solution)/shard_map/all_to_all | solution.py:329
  15.8 0.0 copy-done
  15.9 1.3 shard_map.88.own_ref
  17.2 2.1 %collective-permute-start.4 = (f32[10,256,128]{2,1,0:T(8,128)S(1)}, f32[10,256,128]{2,1,0:T(8,128)S(1)}, u32[]{:S(2)}, u32[]{:S(2)}) collective-permute-start(f32[10,256,128]{2,1,0:T(8,128)S(1)} %shard_map.88.own_ref), channel_id=1, source_target_pairs={{1,0},{2,1},{3,2},{4,3},{5,4},{6,5},{7,6},{9,8},{10,9},{11,10},{12... | collective-permute-start | bytes 3932168 | tf_op jit(solution)/shard_map/ppermute | solution.py:299
  19.2 2.3 %collective-permute-start.3 = (f32[10,256,128]{2,1,0:T(8,128)S(1)}, f32[10,256,128]{2,1,0:T(8,128)}, u32[]{:S(2)}, u32[]{:S(2)}) collective-permute-start(f32[10,256,128]{2,1,0:T(8,128)S(1)} %shard_map.88.own_ref), channel_id=1, source_target_pairs={{0,1},{1,2},{2,3},{3,4},{4,5},{5,6},{6,7},{8,9},{9,10},{10,11},{11... | collective-permute-start | bytes 3932168 | tf_op jit(solution)/shard_map/ppermute | solution.py:299
  21.5 1.5 %shard_map.87 = f32[16,128]{1,0:T(8,128)} custom-call(f32[16,128]{1,0:T(8,128)} %bitcast.7, s32[1,128]{1,0:T(1,128)} %bitcast.8, s32[1,128]{1,0:T(1,128)} %col_ref.1), custom_call_target="tpu_custom_call" | custom-call | tf_op jit(solution)/shard_map/pallas_call | solution.py:338
  23.0 0.8 collective-permute-start
  23.8 1.0 collective-permute-done
  24.9 0.7 add.9
  25.6 10.2 %all-to-all-done.coef_own_ref = bf16[32,7,8,128]{3,2,1,0:T(8,128)(2,1)S(1)} async-done(((bf16[32,7,8,128]{3,2,1,0:T(8,128)(2,1)}), bf16[32,7,8,128]{3,2,1,0:T(8,128)(2,1)S(1)}, u32[]{:S(2)}, u32[]{:S(2)}) %all-to-all-start) | async-done | bytes 458784 | tf_op jit(solution)/shard_map/all_to_all | solution.py:329
  35.7 1.9 %collective-permute-start.6 = (bf16[32,7,8,128]{3,2,1,0:T(8,128)(2,1)S(1)}, bf16[32,7,8,128]{3,2,1,0:T(8,128)(2,1)S(1)}, u32[]{:S(2)}, u32[]{:S(2)}) collective-permute-start(bf16[32,7,8,128]{3,2,1,0:T(8,128)(2,1)S(1)} %all-to-all-done.coef_own_ref), channel_id=1, source_target_pairs={{1,0},{2,1},{3,2},{4,3},{5,4},{6,5},{7,6},{9,8},{10,9},{11,10},{12... | collective-permute-start | bytes 1376264 | tf_op jit(solution)/shard_map/ppermute | solution.py:299
  37.6 2.4 %collective-permute-start.5 = (bf16[32,7,8,128]{3,2,1,0:T(8,128)(2,1)S(1)}, bf16[32,7,8,128]{3,2,1,0:T(8,128)(2,1)}, u32[]{:S(2)}, u32[]{:S(2)}) collective-permute-start(bf16[32,7,8,128]{3,2,1,0:T(8,128)(2,1)S(1)} %all-to-all-done.coef_own_ref), channel_id=1, source_target_pairs={{0,1},{1,2},{2,3},{3,4},{4,5},{5,6},{6,7},{8,9},{9,10},{10,11},{11... | collective-permute-start | bytes 1376264 | tf_op jit(solution)/shard_map/ppermute | solution.py:299
  40.1 0.1 collective-permute-start.1
  40.2 4.6 %collective-permute-done.1 = f32[16,128]{1,0:T(8,128)S(1)} collective-permute-done((f32[16,128]{1,0:T(8,128)S(1)}, f32[16,128]{1,0:T(8,128)S(1)}, u32[]{:S(2)}, u32[]{:S(2)}) %collective-permute-start.1) | collective-permute-done | bytes 8224 | tf_op jit(solution)/shard_map/ppermute | solution.py:319
  44.7 1.5 %collective-permute-start.2 = (f32[16,128]{1,0:T(8,128)S(1)}, f32[16,128]{1,0:T(8,128)S(1)}, u32[]{:S(2)}, u32[]{:S(2)}) collective-permute-start(f32[16,128]{1,0:T(8,128)S(1)} %add.10), channel_id=1, source_target_pairs={{0,4},{1,5},{2,6},{3,7},{4,0},{5,1},{6,2},{7,3},{8,12},{9,13},{10,... | collective-permute-start | bytes 24584 | tf_op jit(solution)/shard_map/ppermute | solution.py:319
  46.2 3.1 %collective-permute-done.2 = f32[16,128]{1,0:T(8,128)S(1)} collective-permute-done((f32[16,128]{1,0:T(8,128)S(1)}, f32[16,128]{1,0:T(8,128)S(1)}, u32[]{:S(2)}, u32[]{:S(2)}) %collective-permute-start.2) | collective-permute-done | bytes 8224 | tf_op jit(solution)/shard_map/ppermute | solution.py:319
  49.3 0.0 collective-permute-done.4.right_ref
  49.3 0.0 collective-permute-done.3.left_ref
  49.3 0.0 collective-permute-done.6.coef_right_ref
  49.3 0.0 collective-permute-done.5.coef_left_ref
  49.3 18.8 %shard_map.89 = (f32[10,256,128]{2,1,0:T(8,128)S(1)}, f32[8,1152,128]{2,1,0:T(8,128)S(1)}, f32[256,128]{1,0:T(8,128)S(1)}) custom-call(s32[1]{0:T(128)} %bitcast.slab_ref, f32[16,128]{1,0:T(8,128)S(1)} %add.11.inject_ref, f32[10,256,128]{2,1,0:T(8,128)} %collective-permute-done.3.left_ref, f32[10,256,128]{2,1,0:T(8,128)S(1)} %shard_map.88.own_ref, ...), custom_call_target="tpu_custom_call" | custom-call | tf_op jit(solution)/shard_map/pallas_call | solution.py:352
  68.2 2.9 %collective-permute-start.8 = (f32[10,256,128]{2,1,0:T(8,128)S(1)}, f32[10,256,128]{2,1,0:T(8,128)S(1)}, u32[]{:S(2)}, u32[]{:S(2)}) collective-permute-start(f32[10,256,128]{2,1,0:T(8,128)S(1)} %get-tuple-element.17.own_ref), channel_id=1, source_target_pairs={{1,0},{2,1},{3,2},{4,3},{5,4},{6,5},{7,6},{9,8},{10,9},{11,10},{12... | collective-permute-start | bytes 3932168 | tf_op jit(solution)/shard_map/ppermute | solution.py:299
  71.1 2.8 %collective-permute-start.7 = (f32[10,256,128]{2,1,0:T(8,128)S(1)}, f32[10,256,128]{2,1,0:T(8,128)S(1)}, u32[]{:S(2)}, u32[]{:S(2)}) collective-permute-start(f32[10,256,128]{2,1,0:T(8,128)S(1)} %get-tuple-element.17.own_ref), channel_id=1, source_target_pairs={{0,1},{1,2},{2,3},{3,4},{4,5},{5,6},{6,7},{8,9},{9,10},{10,11},{11... | collective-permute-start | bytes 3932168 | tf_op jit(solution)/shard_map/ppermute | solution.py:299
  73.9 12.3 %collective-permute-done.8.right_ref = f32[10,256,128]{2,1,0:T(8,128)S(1)} collective-permute-done((f32[10,256,128]{2,1,0:T(8,128)S(1)}, f32[10,256,128]{2,1,0:T(8,128)S(1)}, u32[]{:S(2)}, u32[]{:S(2)}) %collective-permute-start.8) | collective-permute-done | bytes 1310752 | tf_op jit(solution)/shard_map/ppermute | solution.py:299
  86.2 3.8 %collective-permute-done.7.left_ref = f32[10,256,128]{2,1,0:T(8,128)S(1)} collective-permute-done((f32[10,256,128]{2,1,0:T(8,128)S(1)}, f32[10,256,128]{2,1,0:T(8,128)S(1)}, u32[]{:S(2)}, u32[]{:S(2)}) %collective-permute-start.7) | collective-permute-done | bytes 1310752 | tf_op jit(solution)/shard_map/ppermute | solution.py:299
  90.0 16.1 %shard_map.90 = (f32[10,256,128]{2,1,0:T(8,128)S(1)}, f32[32,8,128]{2,1,0:T(8,128)}) custom-call(s32[1]{0:T(128)} %bitcast.slab_ref, f32[16,128]{1,0:T(8,128)S(1)} %add.11.inject_ref, f32[10,256,128]{2,1,0:T(8,128)S(1)} %collective-permute-done.7.left_ref, f32[10,256,128]{2,1,0:T(8,128)S(1)} %get-tuple-element.17.own_ref, ...), custom_call_target="tpu_custom_call" | custom-call | tf_op jit(solution)/shard_map/pallas_call | solution.py:361
  106.1 11.9 %all-to-all-start.1 = ((f32[32,8,128]{2,1,0:T(8,128)}), f32[32,8,128]{2,1,0:T(8,128)S(1)}, u32[]{:S(2)}, u32[]{:S(2)}) async-start(f32[32,8,128]{2,1,0:T(8,128)} %get-tuple-element.21), calls=%async_computation.1 | async-start | bytes 262144 | tf_op jit(solution)/shard_map/all_to_all | solution.py:369
  118.1 0.0 copy-start.1
  118.1 1.9 %shard_map.91 = f32[10,8,4096]{2,1,0:T(8,128)} custom-call(f32[10,256,128]{2,1,0:T(8,128)S(1)} %get-tuple-element.20.state_ref), custom_call_target="tpu_custom_call" | custom-call | tf_op jit(solution)/shard_map/pallas_call | solution.py:370
  120.0 11.2 %all-to-all-done.1.pieces_ref = f32[32,8,128]{2,1,0:T(8,128)S(1)} async-done(((f32[32,8,128]{2,1,0:T(8,128)}), f32[32,8,128]{2,1,0:T(8,128)S(1)}, u32[]{:S(2)}, u32[]{:S(2)}) %all-to-all-start.1) | async-done | bytes 131104 | tf_op jit(solution)/shard_map/all_to_all | solution.py:369
  131.2 1.4 %shard_map.92 = f32[8,8,128]{2,1,0:T(8,128)} custom-call(s32[32]{0:T(128)S(1)} %copy-done.1, f32[32,8,128]{2,1,0:T(8,128)S(1)} %all-to-all-done.1.pieces_ref), custom_call_target="tpu_custom_call" | custom-call | tf_op jit(solution)/shard_map/pallas_call | solution.py:377
  (4 shorter events, 0.0 us)
Async XLA Ops:
  0.6 15.2 %copy-start = (f32[1,2,5,8,4096]{4,3,2,1,0:T(8,128)S(1)}, f32[1,2,5,8,4096]{4,3,2,1,0:T(8,128)}, u32[]{:S(2)}) copy-start(f32[1,2,5,8,4096]{4,3,2,1,0:T(8,128)} %param.7) | copy-start | bytes 3932164
  2.8 32.9 %all-to-all-start = ((bf16[32,7,8,128]{3,2,1,0:T(8,128)(2,1)}), bf16[32,7,8,128]{3,2,1,0:T(8,128)(2,1)S(1)}, u32[]{:S(2)}, u32[]{:S(2)}) async-start(bf16[32,7,8,128]{3,2,1,0:T(8,128)(2,1)} %shard_map.86), calls=%async_computation | async-start | bytes 917504 | tf_op jit(solution)/shard_map/all_to_all | solution.py:329
  17.2 32.1 %collective-permute-start.4 = (f32[10,256,128]{2,1,0:T(8,128)S(1)}, f32[10,256,128]{2,1,0:T(8,128)S(1)}, u32[]{:S(2)}, u32[]{:S(2)}) collective-permute-start(f32[10,256,128]{2,1,0:T(8,128)S(1)} %shard_map.88.own_ref), channel_id=1, source_target_pairs={{1,0},{2,1},{3,2},{4,3},{5,4},{6,5},{7,6},{9,8},{10,9},{11,10},{12... | collective-permute-start | bytes 3932168 | tf_op jit(solution)/shard_map/ppermute | solution.py:299
  19.2 30.0 %collective-permute-start.3 = (f32[10,256,128]{2,1,0:T(8,128)S(1)}, f32[10,256,128]{2,1,0:T(8,128)}, u32[]{:S(2)}, u32[]{:S(2)}) collective-permute-start(f32[10,256,128]{2,1,0:T(8,128)S(1)} %shard_map.88.own_ref), channel_id=1, source_target_pairs={{0,1},{1,2},{2,3},{3,4},{4,5},{5,6},{6,7},{8,9},{9,10},{10,11},{11... | collective-permute-start | bytes 3932168 | tf_op jit(solution)/shard_map/ppermute | solution.py:299
  23.0 1.8 %collective-permute-start = (f32[16,128]{1,0:T(8,128)}, f32[16,128]{1,0:T(8,128)S(1)}, u32[]{:S(2)}, u32[]{:S(2)}) collective-permute-start(f32[16,128]{1,0:T(8,128)} %shard_map.87), channel_id=1, source_target_pairs={{0,1},{1,0},{2,3},{3,2},{4,5},{5,4},{6,7},{7,6},{8,9},{9,8},{10,11... | collective-permute-start | bytes 24584 | tf_op jit(solution)/shard_map/ppermute | solution.py:319
  35.7 13.6 %collective-permute-start.6 = (bf16[32,7,8,128]{3,2,1,0:T(8,128)(2,1)S(1)}, bf16[32,7,8,128]{3,2,1,0:T(8,128)(2,1)S(1)}, u32[]{:S(2)}, u32[]{:S(2)}) collective-permute-start(bf16[32,7,8,128]{3,2,1,0:T(8,128)(2,1)S(1)} %all-to-all-done.coef_own_ref), channel_id=1, source_target_pairs={{1,0},{2,1},{3,2},{4,3},{5,4},{6,5},{7,6},{9,8},{10,9},{11,10},{12... | collective-permute-start | bytes 1376264 | tf_op jit(solution)/shard_map/ppermute | solution.py:299
  37.6 11.7 %collective-permute-start.5 = (bf16[32,7,8,128]{3,2,1,0:T(8,128)(2,1)S(1)}, bf16[32,7,8,128]{3,2,1,0:T(8,128)(2,1)}, u32[]{:S(2)}, u32[]{:S(2)}) collective-permute-start(bf16[32,7,8,128]{3,2,1,0:T(8,128)(2,1)S(1)} %all-to-all-done.coef_own_ref), channel_id=1, source_target_pairs={{0,1},{1,2},{2,3},{3,4},{4,5},{5,6},{6,7},{8,9},{9,10},{10,11},{11... | collective-permute-start | bytes 1376264 | tf_op jit(solution)/shard_map/ppermute | solution.py:299
  40.1 4.7 %collective-permute-start.1 = (f32[16,128]{1,0:T(8,128)S(1)}, f32[16,128]{1,0:T(8,128)S(1)}, u32[]{:S(2)}, u32[]{:S(2)}) collective-permute-start(f32[16,128]{1,0:T(8,128)S(1)} %add.9), channel_id=1, source_target_pairs={{0,2},{1,3},{2,0},{3,1},{4,6},{5,7},{6,4},{7,5},{8,10},{9,11},{10,... | collective-permute-start | bytes 24584 | tf_op jit(solution)/shard_map/ppermute | solution.py:319
  44.7 4.5 %collective-permute-start.2 = (f32[16,128]{1,0:T(8,128)S(1)}, f32[16,128]{1,0:T(8,128)S(1)}, u32[]{:S(2)}, u32[]{:S(2)}) collective-permute-start(f32[16,128]{1,0:T(8,128)S(1)} %add.10), channel_id=1, source_target_pairs={{0,4},{1,5},{2,6},{3,7},{4,0},{5,1},{6,2},{7,3},{8,12},{9,13},{10,... | collective-permute-start | bytes 24584 | tf_op jit(solution)/shard_map/ppermute | solution.py:319
  68.2 18.0 %collective-permute-start.8 = (f32[10,256,128]{2,1,0:T(8,128)S(1)}, f32[10,256,128]{2,1,0:T(8,128)S(1)}, u32[]{:S(2)}, u32[]{:S(2)}) collective-permute-start(f32[10,256,128]{2,1,0:T(8,128)S(1)} %get-tuple-element.17.own_ref), channel_id=1, source_target_pairs={{1,0},{2,1},{3,2},{4,3},{5,4},{6,5},{7,6},{9,8},{10,9},{11,10},{12... | collective-permute-start | bytes 3932168 | tf_op jit(solution)/shard_map/ppermute | solution.py:299
  71.1 18.9 %collective-permute-start.7 = (f32[10,256,128]{2,1,0:T(8,128)S(1)}, f32[10,256,128]{2,1,0:T(8,128)S(1)}, u32[]{:S(2)}, u32[]{:S(2)}) collective-permute-start(f32[10,256,128]{2,1,0:T(8,128)S(1)} %get-tuple-element.17.own_ref), channel_id=1, source_target_pairs={{0,1},{1,2},{2,3},{3,4},{4,5},{5,6},{6,7},{8,9},{9,10},{10,11},{11... | collective-permute-start | bytes 3932168 | tf_op jit(solution)/shard_map/ppermute | solution.py:299
  106.1 25.1 %all-to-all-start.1 = ((f32[32,8,128]{2,1,0:T(8,128)}), f32[32,8,128]{2,1,0:T(8,128)S(1)}, u32[]{:S(2)}, u32[]{:S(2)}) async-start(f32[32,8,128]{2,1,0:T(8,128)} %get-tuple-element.21), calls=%async_computation.1 | async-start | bytes 262144 | tf_op jit(solution)/shard_map/all_to_all | solution.py:369
  118.1 13.1 %copy-start.1 = (s32[32]{0:T(128)S(1)}, s32[32]{0:T(128)}, u32[]{:S(2)}) copy-start(s32[32]{0:T(128)} %offsets_ref.3) | copy-start | bytes 388

commit v7 on v5

--- a/solution.py
+++ b/solution.py
@@ -186,24 +186,7 @@
     )
 
 
-def first_kernel(
-    slabs,
-    slab_ref,
-    inject_ref,
-    left_ref,
-    own_ref,
-    right_ref,
-    coef_left_ref,
-    coef_own_ref,
-    coef_right_ref,
-    state_out,
-    coef,
-    image_out,
-    state,
-    image,
-    sems,
-):
-    copies = fetch((left_ref, own_ref, right_ref), state, sems)
+def coef_kernel(slabs, slab_ref, coef_left_ref, coef_own_ref, coef_right_ref, coef):
     for part, store in enumerate((coef_left_ref, coef_own_ref, coef_right_ref)):
         base = (PAD + part * COLS) * ROWS
         for tile in range(TILES):
@@ -216,8 +199,7 @@
     depth = ROWS * 128
     wide_z = jnp.maximum(jnp.maximum(PML - z, z - (depth - 1 - PML)), 0).astype(jnp.float32) / PML
     square_z = wide_z * wide_z
-    slab = slab_ref[0]
-    first = (slab - 1) * COLS
+    first = (slab_ref[0] - 1) * COLS
 
     def profile(i, _):
         x = first + i
@@ -228,10 +210,26 @@
         return 0
 
     lax.fori_loop(0, WIDE, profile, 0)
+
+
+def first_kernel(
+    slab_ref,
+    inject_ref,
+    left_ref,
+    own_ref,
+    right_ref,
+    coef,
+    state_out,
+    image_out,
+    state,
+    image,
+    sems,
+):
+    copies = fetch((left_ref, own_ref, right_ref), state, sems)
     image[...] = jnp.zeros_like(image)
     for copy in copies:
         copy.wait()
-    advance(state, coef, image, slab, inject_ref, 0)
+    advance(state, coef, image, slab_ref[0], inject_ref, 0)
     for q in range(10):
         state_out[q] = state[q, window(1), :]
     image_out[...] = image[window(1), :]
@@ -343,18 +341,28 @@
         compiler_params=LARGE,
     )(traces[0], rec_tile.reshape(1, -1), rec_col)
     coef_own, inject = lax.optimization_barrier((coef_own, inject + exchanged(inject, 1)))
-    left, right, inject = lax.optimization_barrier((left, right, inject))
-    inject = inject + sum(exchanged(inject, bits) for bits in range(2, slabs, 2))
+    inject = inject + exchanged(inject, 2)
+    inject_far = exchanged(inject, 4)
     slab = lax.axis_index("slab").astype(jnp.int32).reshape(1)
     coef_left, coef_right = neighbours(coef_own, "slab")
-    state, coef, image = pl.pallas_call(
-        functools.partial(first_kernel, slabs),
-        out_shape=(shape(10, own_rows, 128), shape(8, HELD * ROWS, 128), shape(own_rows, 128)),
-        in_specs=[SMEM, SMEM] + [ANY] * 3 + [VMEM] * 3,
-        out_specs=(VMEM,) * 3,
+    coef = pl.pallas_call(
+        functools.partial(coef_kernel, slabs),
+        out_shape=shape(8, HELD * ROWS, 128),
+        in_specs=[SMEM] + [VMEM] * 3,
+        out_specs=VMEM,
+        compiler_params=PARAMS,
+        cost_estimate=pl.CostEstimate(flops=0, bytes_accessed=6 << 20, transcendentals=0),
+    )(slab, coef_left, coef_own, coef_right)
+    inject_far, coef = lax.optimization_barrier((inject_far, coef))
+    inject = inject + inject_far
+    state, image = pl.pallas_call(
+        first_kernel,
+        out_shape=(shape(10, own_rows, 128), shape(own_rows, 128)),
+        in_specs=[SMEM, SMEM] + [ANY] * 3 + [VMEM],
+        out_specs=(VMEM,) * 2,
         scratch_shapes=scratch(),
         compiler_params=PARAMS,
-    )(slab, inject, left, own, right, coef_left, coef_own, coef_right)
+    )(slab, inject, left, own, right, coef)
     state_left, state_right = neighbours(state, "slab")
     state, pieces = pl.pallas_call(
         second_kernel,

time: 133 us -> 130 us (0.977)
  waiting for transfers between devices: 46.2 us -> 43.9 us
    all_to_all x1, starting transfers between devices: 4.87 us -> 11 us  [local(): lax.all_to_all(pieces, 'shot', split_axis=0, concat_axis=0, tiled=True)]
    all_to_all x1, waiting for transfers between devices: 14.5 us -> 10.2 us  [local(): lax.all_to_all(picked, 'shot', split_axis=0, concat_axis=0, tiled=True)]
    ppermute x6, starting transfers between devices: 16.9 us -> 13.5 us  [neighbours(): return (lax.ppermute(block, axis, up), lax.ppermute(block, axis, down))]
    ppermute x4 -> x3, starting transfers between devices: 4.49 us -> 2.36 us  [exchanged(): return lax.ppermute(rows, 'slab', [(i, i ^ bits) for i in range(slabs)])]
    pallas_call x1 -> x2, Pallas kernels: 18.8 us -> 20.2 us  [the longest x1 16.1 us: local(): pl.pallas_call(first_kernel, out_shape=(shape(10, own_rows, 128), shape(o...]
    ppermute x4 -> x3, waiting for transfers between devices: 4.77 us -> 5.61 us  [exchanged(): return lax.ppermute(rows, 'slab', [(i, i ^ bits) for i in range(slabs)])]
  transfers between devices with their start and end apart: 12 -> 11, of which waited for: 8 -> 7; matrix products, arithmetic and copies ran while one was open for 1% -> 1% of each run, Pallas kernels for 3% -> 7%
where the time goes in v7:
time: 130 us; the launch traced here: 129 us
  Pallas kernels  44.1 us (34%)
  waiting for transfers between devices  43.9 us (34%)
  starting transfers between devices  39.9 us (31%)
    ppermute x6, waiting for transfers between devices, neighbours(): return (lax.ppermute(block, axis, up), lax.ppermute(block, axis, down))  17.6 us
    pallas_call x1, Pallas kernels, local(): pl.pallas_call(first_kernel, out_shape=(shape(10, own_rows, 128), shape(o...  16.1 us
    pallas_call x1, Pallas kernels, local(): pl.pallas_call(second_kernel, out_shape=(shape(10, own_rows, 128), shape(...  15.7 us
    ppermute x6, starting transfers between devices, neighbours(): return (lax.ppermute(block, axis, up), lax.ppermute(block, axis, down))  13.5 us
    all_to_all x1, starting transfers between devices, local(): lax.all_to_all(picked, 'shot', split_axis=0, concat_axis=0, tiled=True)  13 us
    all_to_all x1, starting transfers between devices, local(): lax.all_to_all(pieces, 'shot', split_axis=0, concat_axis=0, tiled=True)  11 us
    all_to_all x1, waiting for transfers between devices, local(): lax.all_to_all(pieces, 'shot', split_axis=0, concat_axis=0, tiled=True)  10.5 us
    all_to_all x1, waiting for transfers between devices, local(): lax.all_to_all(picked, 'shot', split_axis=0, concat_axis=0, tiled=True)  10.2 us
  transfers between devices with their start and end apart: 11, of which 7 were waited for; matrix products, arithmetic and copies ran while one was open for 1% of the time, Pallas kernels for 7%

profile of v7, /device:TPU:32, one launch (start us, length us, event | category | flops | bytes accessed | tf_op | source)
XLA Modules:
  0.0 129.3 jit_solution(277951099223237265)
XLA Ops:
  0.6 2.2 %shard_map.86 = bf16[32,7,8,128]{3,2,1,0:T(8,128)(2,1)} custom-call(s32[32]{0:T(128)} %offsets_ref.3, s32[8]{0:T(128)} %directory_ref.1, bf16[7,8,8,128]{3,2,1,0:T(8,128)(2,1)} %store_ref.1), custom_call_target="tpu_custom_call" | custom-call | tf_op jit(solution)/shard_map/pallas_call | solution.py:319
  2.8 13.0 %all-to-all-start = ((bf16[32,7,8,128]{3,2,1,0:T(8,128)(2,1)}), bf16[32,7,8,128]{3,2,1,0:T(8,128)(2,1)S(1)}, u32[]{:S(2)}, u32[]{:S(2)}) async-start(bf16[32,7,8,128]{3,2,1,0:T(8,128)(2,1)} %shard_map.86), calls=%async_computation | async-start | bytes 917504 | tf_op jit(solution)/shard_map/all_to_all | solution.py:327
  15.9 1.3 %shard_map.89.own_ref = f32[10,256,128]{2,1,0:T(8,128)S(1)} custom-call(f32[10,8,4096]{2,1,0:T(8,128)S(1)} %bitcast.5), custom_call_target="tpu_custom_call" | custom-call | tf_op jit(solution)/shard_map/pallas_call | solution.py:328
  17.2 2.1 %collective-permute-start.6 = (f32[10,256,128]{2,1,0:T(8,128)S(1)}, f32[10,256,128]{2,1,0:T(8,128)S(1)}, u32[]{:S(2)}, u32[]{:S(2)}) collective-permute-start(f32[10,256,128]{2,1,0:T(8,128)S(1)} %shard_map.89.own_ref), channel_id=1, source_target_pairs={{1,0},{2,1},{3,2},{4,3},{5,4},{6,5},{7,6},{9,8},{10,9},{11,10},{12... | collective-permute-start | bytes 3932168 | tf_op jit(solution)/shard_map/ppermute | solution.py:297
  19.2 2.3 %collective-permute-start.5 = (f32[10,256,128]{2,1,0:T(8,128)S(1)}, f32[10,256,128]{2,1,0:T(8,128)}, u32[]{:S(2)}, u32[]{:S(2)}) collective-permute-start(f32[10,256,128]{2,1,0:T(8,128)S(1)} %shard_map.89.own_ref), channel_id=1, source_target_pairs={{0,1},{1,2},{2,3},{3,4},{4,5},{5,6},{6,7},{8,9},{9,10},{10,11},{11... | collective-permute-start | bytes 3932168 | tf_op jit(solution)/shard_map/ppermute | solution.py:297
  21.5 1.5 %shard_map.87 = f32[16,128]{1,0:T(8,128)} custom-call(f32[16,128]{1,0:T(8,128)} %bitcast.7, s32[1,128]{1,0:T(1,128)} %bitcast.8, s32[1,128]{1,0:T(1,128)} %col_ref.1), custom_call_target="tpu_custom_call" | custom-call | tf_op jit(solution)/shard_map/pallas_call | solution.py:336
  23.0 0.8 collective-permute-start
  23.8 1.0 collective-permute-done
  24.9 0.7 add.9
  25.6 10.2 %all-to-all-done.coef_own_ref = bf16[32,7,8,128]{3,2,1,0:T(8,128)(2,1)S(1)} async-done(((bf16[32,7,8,128]{3,2,1,0:T(8,128)(2,1)}), bf16[32,7,8,128]{3,2,1,0:T(8,128)(2,1)S(1)}, u32[]{:S(2)}, u32[]{:S(2)}) %all-to-all-start) | async-done | bytes 458784 | tf_op jit(solution)/shard_map/all_to_all | solution.py:327
  35.7 1.9 %collective-permute-start.4 = (bf16[32,7,8,128]{3,2,1,0:T(8,128)(2,1)S(1)}, bf16[32,7,8,128]{3,2,1,0:T(8,128)(2,1)S(1)}, u32[]{:S(2)}, u32[]{:S(2)}) collective-permute-start(bf16[32,7,8,128]{3,2,1,0:T(8,128)(2,1)S(1)} %all-to-all-done.coef_own_ref), channel_id=1, source_target_pairs={{1,0},{2,1},{3,2},{4,3},{5,4},{6,5},{7,6},{9,8},{10,9},{11,10},{12... | collective-permute-start | bytes 1376264 | tf_op jit(solution)/shard_map/ppermute | solution.py:297
  37.6 2.4 %collective-permute-start.3 = (bf16[32,7,8,128]{3,2,1,0:T(8,128)(2,1)S(1)}, bf16[32,7,8,128]{3,2,1,0:T(8,128)(2,1)}, u32[]{:S(2)}, u32[]{:S(2)}) collective-permute-start(bf16[32,7,8,128]{3,2,1,0:T(8,128)(2,1)S(1)} %all-to-all-done.coef_own_ref), channel_id=1, source_target_pairs={{0,1},{1,2},{2,3},{3,4},{4,5},{5,6},{6,7},{8,9},{9,10},{10,11},{11... | collective-permute-start | bytes 1376264 | tf_op jit(solution)/shard_map/ppermute | solution.py:297
  40.1 0.1 collective-permute-start.1
  40.2 4.6 %collective-permute-done.1 = f32[16,128]{1,0:T(8,128)S(1)} collective-permute-done((f32[16,128]{1,0:T(8,128)S(1)}, f32[16,128]{1,0:T(8,128)S(1)}, u32[]{:S(2)}, u32[]{:S(2)}) %collective-permute-start.1) | collective-permute-done | bytes 8224 | tf_op jit(solution)/shard_map/ppermute | solution.py:317
  44.7 1.5 %collective-permute-start.2 = (f32[16,128]{1,0:T(8,128)S(1)}, f32[16,128]{1,0:T(8,128)S(1)}, u32[]{:S(2)}, u32[]{:S(2)}) collective-permute-start(f32[16,128]{1,0:T(8,128)S(1)} %add.10), channel_id=1, source_target_pairs={{0,4},{1,5},{2,6},{3,7},{4,0},{5,1},{6,2},{7,3},{8,12},{9,13},{10,... | collective-permute-start | bytes 24584 | tf_op jit(solution)/shard_map/ppermute | solution.py:317
  46.2 0.0 collective-permute-done.4.coef_right_ref
  46.2 1.4 %collective-permute-done.3.coef_left_ref = bf16[32,7,8,128]{3,2,1,0:T(8,128)(2,1)} collective-permute-done((bf16[32,7,8,128]{3,2,1,0:T(8,128)(2,1)S(1)}, bf16[32,7,8,128]{3,2,1,0:T(8,128)(2,1)}, u32[]{:S(2)}, u32[]{:S(2)}) %collective-permute-start.3) | collective-permute-done | bytes 458784 | tf_op jit(solution)/shard_map/ppermute | solution.py:297
  47.6 4.1 %shard_map.88.coef = f32[8,1152,128]{2,1,0:T(8,128)S(1)} custom-call(s32[1]{0:T(128)} %bitcast.slab_ref, bf16[32,7,8,128]{3,2,1,0:T(8,128)(2,1)} %collective-permute-done.3.coef_left_ref, bf16[32,7,8,128]{3,2,1,0:T(8,128)(2,1)S(1)} %all-to-all-done.coef_own_ref, bf16[32,7,8,128]{3,2,1,0:T(8,128)(2,1)S(1)} %collective-permute-done.4.coef_right_ref), custom_call_target="tpu_custom_call" | custom-call | bytes 6291456 | tf_op jit(solution)/shard_map/pallas_call | solution.py:348
  51.7 0.0 collective-permute-done.2
  51.8 0.0 collective-permute-done.6.right_ref
  51.8 0.0 collective-permute-done.5.left_ref
  51.8 16.1 %shard_map.90 = (f32[10,256,128]{2,1,0:T(8,128)S(1)}, f32[256,128]{1,0:T(8,128)S(1)}) custom-call(s32[1]{0:T(128)} %bitcast.slab_ref, f32[16,128]{1,0:T(8,128)S(1)} %add.11.inject_ref, f32[10,256,128]{2,1,0:T(8,128)} %collective-permute-done.5.left_ref, f32[10,256,128]{2,1,0:T(8,128)S(1)} %shard_map.89.own_ref, ...), custom_call_target="tpu_custom_call" | custom-call | tf_op jit(solution)/shard_map/pallas_call | solution.py:358
  67.9 2.0 %collective-permute-start.8 = (f32[10,256,128]{2,1,0:T(8,128)S(1)}, f32[10,256,128]{2,1,0:T(8,128)S(1)}, u32[]{:S(2)}, u32[]{:S(2)}) collective-permute-start(f32[10,256,128]{2,1,0:T(8,128)S(1)} %get-tuple-element.20.own_ref), channel_id=1, source_target_pairs={{1,0},{2,1},{3,2},{4,3},{5,4},{6,5},{7,6},{9,8},{10,9},{11,10},{12... | collective-permute-start | bytes 3932168 | tf_op jit(solution)/shard_map/ppermute | solution.py:297
  69.9 2.8 %collective-permute-start.7 = (f32[10,256,128]{2,1,0:T(8,128)S(1)}, f32[10,256,128]{2,1,0:T(8,128)S(1)}, u32[]{:S(2)}, u32[]{:S(2)}) collective-permute-start(f32[10,256,128]{2,1,0:T(8,128)S(1)} %get-tuple-element.20.own_ref), channel_id=1, source_target_pairs={{0,1},{1,2},{2,3},{3,4},{4,5},{5,6},{6,7},{8,9},{9,10},{10,11},{11... | collective-permute-start | bytes 3932168 | tf_op jit(solution)/shard_map/ppermute | solution.py:297
  72.7 12.3 %collective-permute-done.8.right_ref = f32[10,256,128]{2,1,0:T(8,128)S(1)} collective-permute-done((f32[10,256,128]{2,1,0:T(8,128)S(1)}, f32[10,256,128]{2,1,0:T(8,128)S(1)}, u32[]{:S(2)}, u32[]{:S(2)}) %collective-permute-start.8) | collective-permute-done | bytes 1310752 | tf_op jit(solution)/shard_map/ppermute | solution.py:297
  85.0 3.8 %collective-permute-done.7.left_ref = f32[10,256,128]{2,1,0:T(8,128)S(1)} collective-permute-done((f32[10,256,128]{2,1,0:T(8,128)S(1)}, f32[10,256,128]{2,1,0:T(8,128)S(1)}, u32[]{:S(2)}, u32[]{:S(2)}) %collective-permute-start.7) | collective-permute-done | bytes 1310752 | tf_op jit(solution)/shard_map/ppermute | solution.py:297
  88.8 15.7 %shard_map.91 = (f32[10,256,128]{2,1,0:T(8,128)S(1)}, f32[32,8,128]{2,1,0:T(8,128)}) custom-call(s32[1]{0:T(128)} %bitcast.slab_ref, f32[16,128]{1,0:T(8,128)S(1)} %add.11.inject_ref, f32[10,256,128]{2,1,0:T(8,128)S(1)} %collective-permute-done.7.left_ref, f32[10,256,128]{2,1,0:T(8,128)S(1)} %get-tuple-element.20.own_ref, ...), custom_call_target="tpu_custom_call" | custom-call | tf_op jit(solution)/shard_map/pallas_call | solution.py:367
  104.5 11.0 %all-to-all-start.1 = ((f32[32,8,128]{2,1,0:T(8,128)}), f32[32,8,128]{2,1,0:T(8,128)S(1)}, u32[]{:S(2)}, u32[]{:S(2)}) async-start(f32[32,8,128]{2,1,0:T(8,128)} %get-tuple-element.23), calls=%async_computation.1 | async-start | bytes 262144 | tf_op jit(solution)/shard_map/all_to_all | solution.py:375
  115.5 0.0 copy-start.1
  115.5 1.9 %shard_map.92 = f32[10,8,4096]{2,1,0:T(8,128)} custom-call(f32[10,256,128]{2,1,0:T(8,128)S(1)} %get-tuple-element.22.state_ref), custom_call_target="tpu_custom_call" | custom-call | tf_op jit(solution)/shard_map/pallas_call | solution.py:376
  117.4 10.5 %all-to-all-done.1.pieces_ref = f32[32,8,128]{2,1,0:T(8,128)S(1)} async-done(((f32[32,8,128]{2,1,0:T(8,128)}), f32[32,8,128]{2,1,0:T(8,128)S(1)}, u32[]{:S(2)}, u32[]{:S(2)}) %all-to-all-start.1) | async-done | bytes 131104 | tf_op jit(solution)/shard_map/all_to_all | solution.py:375
  128.0 1.4 %shard_map.93 = f32[8,8,128]{2,1,0:T(8,128)} custom-call(s32[32]{0:T(128)S(1)} %copy-done.1, f32[32,8,128]{2,1,0:T(8,128)S(1)} %all-to-all-done.1.pieces_ref), custom_call_target="tpu_custom_call" | custom-call | tf_op jit(solution)/shard_map/pallas_call | solution.py:383
  (5 shorter events, 0.0 us)
Async XLA Ops:
  0.6 15.2 %copy-start = (f32[1,2,5,8,4096]{4,3,2,1,0:T(8,128)S(1)}, f32[1,2,5,8,4096]{4,3,2,1,0:T(8,128)}, u32[]{:S(2)}) copy-start(f32[1,2,5,8,4096]{4,3,2,1,0:T(8,128)} %param.7) | copy-start | bytes 3932164
  2.8 32.9 %all-to-all-start = ((bf16[32,7,8,128]{3,2,1,0:T(8,128)(2,1)}), bf16[32,7,8,128]{3,2,1,0:T(8,128)(2,1)S(1)}, u32[]{:S(2)}, u32[]{:S(2)}) async-start(bf16[32,7,8,128]{3,2,1,0:T(8,128)(2,1)} %shard_map.86), calls=%async_computation | async-start | bytes 917504 | tf_op jit(solution)/shard_map/all_to_all | solution.py:327
  17.2 34.6 %collective-permute-start.6 = (f32[10,256,128]{2,1,0:T(8,128)S(1)}, f32[10,256,128]{2,1,0:T(8,128)S(1)}, u32[]{:S(2)}, u32[]{:S(2)}) collective-permute-start(f32[10,256,128]{2,1,0:T(8,128)S(1)} %shard_map.89.own_ref), channel_id=1, source_target_pairs={{1,0},{2,1},{3,2},{4,3},{5,4},{6,5},{7,6},{9,8},{10,9},{11,10},{12... | collective-permute-start | bytes 3932168 | tf_op jit(solution)/shard_map/ppermute | solution.py:297
  19.2 32.5 %collective-permute-start.5 = (f32[10,256,128]{2,1,0:T(8,128)S(1)}, f32[10,256,128]{2,1,0:T(8,128)}, u32[]{:S(2)}, u32[]{:S(2)}) collective-permute-start(f32[10,256,128]{2,1,0:T(8,128)S(1)} %shard_map.89.own_ref), channel_id=1, source_target_pairs={{0,1},{1,2},{2,3},{3,4},{4,5},{5,6},{6,7},{8,9},{9,10},{10,11},{11... | collective-permute-start | bytes 3932168 | tf_op jit(solution)/shard_map/ppermute | solution.py:297
  23.0 1.8 %collective-permute-start = (f32[16,128]{1,0:T(8,128)}, f32[16,128]{1,0:T(8,128)S(1)}, u32[]{:S(2)}, u32[]{:S(2)}) collective-permute-start(f32[16,128]{1,0:T(8,128)} %shard_map.87), channel_id=1, source_target_pairs={{0,1},{1,0},{2,3},{3,2},{4,5},{5,4},{6,7},{7,6},{8,9},{9,8},{10,11... | collective-permute-start | bytes 24584 | tf_op jit(solution)/shard_map/ppermute | solution.py:317
  35.7 10.5 %collective-permute-start.4 = (bf16[32,7,8,128]{3,2,1,0:T(8,128)(2,1)S(1)}, bf16[32,7,8,128]{3,2,1,0:T(8,128)(2,1)S(1)}, u32[]{:S(2)}, u32[]{:S(2)}) collective-permute-start(bf16[32,7,8,128]{3,2,1,0:T(8,128)(2,1)S(1)} %all-to-all-done.coef_own_ref), channel_id=1, source_target_pairs={{1,0},{2,1},{3,2},{4,3},{5,4},{6,5},{7,6},{9,8},{10,9},{11,10},{12... | collective-permute-start | bytes 1376264 | tf_op jit(solution)/shard_map/ppermute | solution.py:297
  37.6 10.0 %collective-permute-start.3 = (bf16[32,7,8,128]{3,2,1,0:T(8,128)(2,1)S(1)}, bf16[32,7,8,128]{3,2,1,0:T(8,128)(2,1)}, u32[]{:S(2)}, u32[]{:S(2)}) collective-permute-start(bf16[32,7,8,128]{3,2,1,0:T(8,128)(2,1)S(1)} %all-to-all-done.coef_own_ref), channel_id=1, source_target_pairs={{0,1},{1,2},{2,3},{3,4},{4,5},{5,6},{6,7},{8,9},{9,10},{10,11},{11... | collective-permute-start | bytes 1376264 | tf_op jit(solution)/shard_map/ppermute | solution.py:297
  40.1 4.7 %collective-permute-start.1 = (f32[16,128]{1,0:T(8,128)S(1)}, f32[16,128]{1,0:T(8,128)S(1)}, u32[]{:S(2)}, u32[]{:S(2)}) collective-permute-start(f32[16,128]{1,0:T(8,128)S(1)} %add.9), channel_id=1, source_target_pairs={{0,2},{1,3},{2,0},{3,1},{4,6},{5,7},{6,4},{7,5},{8,10},{9,11},{10,... | collective-permute-start | bytes 24584 | tf_op jit(solution)/shard_map/ppermute | solution.py:317
  44.7 7.0 %collective-permute-start.2 = (f32[16,128]{1,0:T(8,128)S(1)}, f32[16,128]{1,0:T(8,128)S(1)}, u32[]{:S(2)}, u32[]{:S(2)}) collective-permute-start(f32[16,128]{1,0:T(8,128)S(1)} %add.10), channel_id=1, source_target_pairs={{0,4},{1,5},{2,6},{3,7},{4,0},{5,1},{6,2},{7,3},{8,12},{9,13},{10,... | collective-permute-start | bytes 24584 | tf_op jit(solution)/shard_map/ppermute | solution.py:317
  67.9 17.2 %collective-permute-start.8 = (f32[10,256,128]{2,1,0:T(8,128)S(1)}, f32[10,256,128]{2,1,0:T(8,128)S(1)}, u32[]{:S(2)}, u32[]{:S(2)}) collective-permute-start(f32[10,256,128]{2,1,0:T(8,128)S(1)} %get-tuple-element.20.own_ref), channel_id=1, source_target_pairs={{1,0},{2,1},{3,2},{4,3},{5,4},{6,5},{7,6},{9,8},{10,9},{11,10},{12... | collective-permute-start | bytes 3932168 | tf_op jit(solution)/shard_map/ppermute | solution.py:297
  69.9 18.9 %collective-permute-start.7 = (f32[10,256,128]{2,1,0:T(8,128)S(1)}, f32[10,256,128]{2,1,0:T(8,128)S(1)}, u32[]{:S(2)}, u32[]{:S(2)}) collective-permute-start(f32[10,256,128]{2,1,0:T(8,128)S(1)} %get-tuple-element.20.own_ref), channel_id=1, source_target_pairs={{0,1},{1,2},{2,3},{3,4},{4,5},{5,6},{6,7},{8,9},{9,10},{10,11},{11... | collective-permute-start | bytes 3932168 | tf_op jit(solution)/shard_map/ppermute | solution.py:297
  104.5 23.4 %all-to-all-start.1 = ((f32[32,8,128]{2,1,0:T(8,128)}), f32[32,8,128]{2,1,0:T(8,128)S(1)}, u32[]{:S(2)}, u32[]{:S(2)}) async-start(f32[32,8,128]{2,1,0:T(8,128)} %get-tuple-element.23), calls=%async_computation.1 | async-start | bytes 262144 | tf_op jit(solution)/shard_map/all_to_all | solution.py:375
  115.5 12.4 %copy-start.1 = (s32[32]{0:T(128)S(1)}, s32[32]{0:T(128)}, u32[]{:S(2)}) copy-start(s32[32]{0:T(128)} %offsets_ref.3) | copy-start | bytes 388
